TPU v7x, 256 devices: a whole 4x4x8 slice. The times are simulated.
256 devices in a mesh: island: 32 (over y, x, core), shard: 8 (over z).
Axes of the slice: x: 4, y: 4, z: 8, core: 2. Of those that a mesh axis runs over, the one named last changes fastest.
Arguments:
- pseudo_grad: bfloat16 [32, 2, 2048, 2048], P('island', None, None, 'shard'), may hold values from -4 to 4
- path_table: int32 [32, 2], replicated, may hold values from 0 to 15
- owner_place: int32 [32], replicated, may hold values from 0 to 31, each once
- outer_param: float32 [32, 2048, 2048], P('island', 'shard'), may hold values from -4 to 4
- outer_momentum: float32 [32, 2048, 2048], P('island', 'shard'), may hold values from -3 to 3
Outputs:
- new_param: float32 [32, 2048, 2048], P('island', 'shard')
- new_momentum: float32 [32, 2048, 2048], P('island', 'shard')
- returned: bfloat16 [32, 2, 2048, 2048], P('island', None, None, 'shard')
Inputs may be any that keep to these rules, and one draw needn't show every extreme that they name: `path_table`: entry [i, l] picks module l * 16 + entry of level l for island i. Each value appears once; module m's outer state is row owner_place[m] of outer_param and outer_momentum.
All inputs are finite; a program needn't handle non-finite values.
Results may differ from a plain program's by a relative error of at most 0.001.
Values may be sent and summed in bfloat16 or wider, within the bound.
No kernel may reach another device: no remote copies, remote signals or barrier semaphores. Data moves between devices by JAX's collectives and lax.ppermute only.
A program may use at most 128 MiB of HBM per device.

v0:
```python
import jax
import jax.numpy as jnp
from jax import lax
from jax.sharding import PartitionSpec as P

LEARN_RATE = 0.7
MOMENTUM_COEF = 0.9


def nesterov(current, velocity, update):
    next_velocity = MOMENTUM_COEF * velocity + update
    next_current = current - LEARN_RATE * (update + MOMENTUM_COEF * next_velocity)
    return (next_current, next_velocity)


def body(pseudo_grad, path_table, owner_place, outer_param, outer_momentum):
    islands = lax.axis_size("island")
    shards = lax.axis_size("shard")
    levels = pseudo_grad.shape[1]
    full_rows = pseudo_grad.shape[2]
    narrow = pseudo_grad.shape[3]
    modules = owner_place.shape[0]
    per_level = modules // levels
    shard_rows = outer_param.shape[1]
    model_width = outer_param.shape[2]
    sub_rows = shard_rows // islands
    module_ids = jnp.arange(levels, dtype=jnp.int32)[None, :] * per_level + path_table
    targets = jnp.take(owner_place, module_ids.reshape(-1), axis=0)
    sectioned = pseudo_grad.reshape(1, levels, shards, islands, sub_rows, narrow)
    received = lax.all_to_all(
        lax.all_to_all(sectioned, "island", split_axis=3, concat_axis=0, tiled=True),
        "shard",
        split_axis=2,
        concat_axis=5,
        tiled=True,
    )
    received = received.reshape(islands * levels, sub_rows * model_width)
    member = targets[None, :] == jnp.arange(modules, dtype=jnp.int32)[:, None]
    totals = jnp.dot(member.astype(jnp.bfloat16), received, preferred_element_type=jnp.float32)
    counts = jnp.sum(member.astype(jnp.float32), axis=1, keepdims=True)
    mean_grad = (totals / jnp.maximum(counts, 1.0)).reshape(modules, sub_rows, model_width)
    owned_mean = lax.all_to_all(mean_grad, "island", split_axis=0, concat_axis=1, tiled=True)
    new_param, new_momentum = nesterov(outer_param, outer_momentum, owned_mean)
    row_param = lax.all_to_all(
        new_param.astype(jnp.bfloat16), "island", split_axis=1, concat_axis=0, tiled=True
    )
    picked = jnp.take(row_param, targets, axis=0).reshape(
        islands, levels, 1, 1, sub_rows, model_width
    )
    arrived = lax.all_to_all(
        lax.all_to_all(picked, "island", split_axis=0, concat_axis=3, tiled=True),
        "shard",
        split_axis=5,
        concat_axis=2,
        tiled=True,
    )
    returned = arrived.reshape(1, levels, full_rows, narrow)
    return (new_param, new_momentum, returned)


def solution(mesh):
    placed = (
        P("island", None, None, "shard"),
        P(),
        P(),
        P("island", "shard", None),
        P("island", "shard", None),
    )
    return jax.shard_map(
        body,
        mesh=mesh,
        in_specs=placed,
        out_specs=(
            P("island", "shard", None),
            P("island", "shard", None),
            P("island", None, None, "shard"),
        ),
        check_vma=False,
    )
```

profile of v0, /device:TPU:1, one launch (start us, length us, event | category | flops | bytes accessed | tf_op | source)
XLA Modules:
  0.0 307.3 jit_solution(9583582239870586912)
XLA Ops:
  0.6 3.8 %copy.57 = bf16[1,2,8,32,8,256]{5,2,4,1,0,3:T(8,128)(2,1)S(1)} copy(bf16[1,2,8,32,8,256]{5,4,3,2,1,0:T(8,128)(2,1)} %bitcast.64) | data formatting | bytes 4194304 | tf_op jit(solution)/shard_map/reshape | solution.py:29
  4.5 36.8 %all_to_all.90 = bf16[1,2,8,32,8,256]{5,2,4,1,0,3:T(8,128)(2,1)S(1)} all-to-all(bf16[1,2,8,32,8,256]{5,2,4,1,0,3:T(8,128)(2,1)S(1)} %copy.57), channel_id=1, replica_groups=mesh['island'=32,'shard'=8] {'island'}, dimensions={3} | all-to-all | bytes 4194304 | tf_op jit(solution)/shard_map/all_to_all | solution.py:31
  41.3 1.7 copy.58
  43.0 8.3 %all-to-all-start.1 = ((bf16[32,2,8,1,8,256]{5,4,1,0,3,2:T(8,128)(2,1)}), bf16[32,2,8,1,8,256]{5,4,1,0,3,2:T(8,128)(2,1)S(1)}, u32[]{:S(2)}, u32[]{:S(2)}) async-start(bf16[32,2,8,1,8,256]{5,4,1,0,3,2:T(8,128)(2,1)} %copy.58), calls=%async_computation.1 | async-start | bytes 4194304 | tf_op jit(solution)/shard_map/all_to_all | solution.py:30
  51.6 0.1 reshape.148
  51.8 0.8 gather_fusion
  52.6 0.1 convert_reduce_fusion
  52.7 47.0 %all-to-all-done.1 = bf16[32,2,8,1,8,256]{5,4,1,0,3,2:T(8,128)(2,1)S(1)} async-done(((bf16[32,2,8,1,8,256]{5,4,1,0,3,2:T(8,128)(2,1)}), bf16[32,2,8,1,8,256]{5,4,1,0,3,2:T(8,128)(2,1)S(1)}, u32[]{:S(2)}, u32[]{:S(2)}) %all-to-all-start.1) | async-done | bytes 2097184 | tf_op jit(solution)/shard_map/all_to_all | solution.py:30
  99.7 3.6 %copy.59 = bf16[32,2,1,1,8,8,256]{6,5,4,1,0,3,2:T(8,128)(2,1)} copy(bf16[32,2,1,1,8,8,256]{6,4,1,0,5,3,2:T(8,128)(2,1)S(1)} %bitcast.60) | data formatting | bytes 4194304 | tf_op jit(solution)/shard_map/all_to_all | solution.py:30
  103.3 2.9 reshape.151
  106.2 0.4 convolution_divide_fusion
  106.6 1.2 copy.69
  107.8 36.0 %all_to_all.91 = f32[32,8,2048]{2,1,0:T(8,128)S(1)} all-to-all(f32[32,8,2048]{2,1,0:T(8,128)S(1)} %bitcast.63), channel_id=1, replica_groups=mesh['island'=32,'shard'=8] {'island'}, dimensions={0} | all-to-all | bytes 4194304 | tf_op jit(solution)/shard_map/all_to_all | solution.py:42
  143.9 2.8 fusion.5
  146.6 1.6 copy.73
  148.3 0.5 broadcast.161
  148.8 6.8 %reduce = bf16[256,2048]{1,0:T(8,128)(2,1)S(1)} reduce(bf16[256,1,2048]{2,1,0:T(2,128)(2,1)S(1)} %bitcast.61, bf16[]{:T(256)} %broadcast.161), dimensions={1}, to_apply=%bitcast.52.reduce_sub_computation | reduce | bytes 2097154
  155.6 1.9 reshape.170
  157.5 4.0 %all-to-all-start.3 = ((bf16[32,2,8192]{2,1,0:T(2,128)(2,1)}), bf16[32,2,8192]{2,1,0:T(2,128)(2,1)S(1)}, u32[]{:S(2)}, u32[]{:S(2)}) async-start(bf16[32,2,8192]{2,1,0:T(2,128)(2,1)} %reshape.170), calls=%async_computation.3 | async-start | bytes 2097152 | tf_op jit(solution)/shard_map/all_to_all | solution.py:44
  161.8 0.1 copy.61
  161.9 16.9 %all-to-all-done.3 = bf16[32,2,8192]{2,1,0:T(2,128)(2,1)S(1)} async-done(((bf16[32,2,8192]{2,1,0:T(2,128)(2,1)}), bf16[32,2,8192]{2,1,0:T(2,128)(2,1)S(1)}, u32[]{:S(2)}, u32[]{:S(2)}) %all-to-all-start.3) | async-done | bytes 1048608 | tf_op jit(solution)/shard_map/all_to_all | solution.py:44
  178.8 1.0 reshape.171
  179.8 0.6 copy.72
  180.4 0.7 gather_fusion.1
  181.1 0.3 select_bitcast_fusion
  181.4 31.9 %all_to_all.92 = bf16[32,2,1,1,8,2048]{5,4,1,3,2,0:T(8,128)(2,1)S(1)} all-to-all(bf16[32,2,1,1,8,2048]{5,4,1,3,2,0:T(8,128)(2,1)S(1)} %select_bitcast_fusion), channel_id=1, replica_groups=mesh['island'=32,'shard'=8] {'island'}, dimensions={0} | all-to-all | bytes 4194304 | tf_op jit(solution)/shard_map/all_to_all | solution.py:51
  213.3 9.2 %copy.64 = bf16[1,2,1,32,8,2048]{3,4,2,1,0,5:T(8,128)(2,1)} copy(bf16[1,2,1,32,8,2048]{5,4,1,3,2,0:T(8,128)(2,1)S(1)} %bitcast.56) | data formatting | bytes 4194304 | tf_op jit(solution)/shard_map/all_to_all | solution.py:51
  222.5 10.1 %reshape.172 = bf16[8,2,65536]{2,1,0:T(2,128)(2,1)S(1)} reshape(bf16[2048,1,2,1,8,32]{5,4,3,2,1,0:T(8,128)(2,1)} %bitcast.53) | data formatting | bytes 4194304
  232.7 54.8 %all_to_all.93 = bf16[8,2,65536]{2,1,0:T(2,128)(2,1)} all-to-all(bf16[8,2,65536]{2,1,0:T(2,128)(2,1)S(1)} %reshape.172), channel_id=1, replica_groups=mesh['island'=32,'shard'=8] {'shard'}, dimensions={0} | all-to-all | bytes 4194304 | tf_op jit(solution)/shard_map/all_to_all | solution.py:50
  287.5 8.7 %reshape.173 = bf16[2048,1,2,1,8,32]{5,4,3,2,1,0:T(8,128)(2,1)} reshape(bf16[8,2,65536]{2,1,0:T(2,128)(2,1)} %all_to_all.93) | data formatting | bytes 4194304
  296.2 9.3 %copy.67 = bf16[1,2,1,32,8,8,256]{6,5,4,3,1,2,0:T(8,128)(2,1)S(1)} copy(bf16[1,2,1,32,8,8,256]{3,4,1,6,5,2,0:T(8,128)(2,1)} %bitcast.54) | data formatting | bytes 4194304 | tf_op jit(solution)/shard_map/all_to_all | solution.py:50
  305.5 1.8 copy.66
  (23 shorter events, 0.6 us)
Async XLA Ops:
  0.6 51.1 %copy-start = (s32[32]{0:T(128)S(1)}, s32[32]{0:T(128)}, u32[]{:S(2)}) copy-start(s32[32]{0:T(128)} %param.7) | copy-start | bytes 388
  43.0 8.3 %copy-start.4 = (s32[32,2]{0,1:T(2,128)S(1)}, s32[32,2]{0,1:T(2,128)}, u32[]{:S(2)}) copy-start(s32[32,2]{0,1:T(2,128)} %param.6) | copy-start | bytes 772
  43.0 56.7 %all-to-all-start.1 = ((bf16[32,2,8,1,8,256]{5,4,1,0,3,2:T(8,128)(2,1)}), bf16[32,2,8,1,8,256]{5,4,1,0,3,2:T(8,128)(2,1)S(1)}, u32[]{:S(2)}, u32[]{:S(2)}) async-start(bf16[32,2,8,1,8,256]{5,4,1,0,3,2:T(8,128)(2,1)} %copy.58), calls=%async_computation.1 | async-start | bytes 4194304 | tf_op jit(solution)/shard_map/all_to_all | solution.py:30
  107.8 36.1 %copy-start.2 = (f32[1,256,2048]{2,1,0:T(8,128)S(1)}, f32[1,256,2048]{2,1,0:T(8,128)}, u32[]{:S(2)}) copy-start(f32[1,256,2048]{2,1,0:T(8,128)} %param.8) | copy-start | bytes 6291460
  107.8 36.1 %copy-start.3 = (f32[1,256,2048]{2,1,0:T(8,128)S(1)}, f32[1,256,2048]{2,1,0:T(8,128)}, u32[]{:S(2)}) copy-start(f32[1,256,2048]{2,1,0:T(8,128)} %param.9) | copy-start | bytes 6291460
  157.5 21.3 %all-to-all-start.3 = ((bf16[32,2,8192]{2,1,0:T(2,128)(2,1)}), bf16[32,2,8192]{2,1,0:T(2,128)(2,1)S(1)}, u32[]{:S(2)}, u32[]{:S(2)}) async-start(bf16[32,2,8192]{2,1,0:T(2,128)(2,1)} %reshape.170), calls=%async_computation.3 | async-start | bytes 2097152 | tf_op jit(solution)/shard_map/all_to_all | solution.py:44
  305.5 1.8 copy-start.1
where the time goes:
time: 308 us; the launch traced here: 307 us
  blocking collectives  160 us (52%)
  waiting for transfers between devices  63.9 us (21%)
  local copies, waits for them, and re-layouts  60.1 us (20%)
  starting transfers between devices  12.3 us (4%)
  other arithmetic  10.1 us (3%)
    all_to_all x1, blocking collectives, body(): lax.all_to_all(lax.all_to_all(picked, 'island', split_axis=0, concat_axis...  54.8 us
    all_to_all x1, waiting for transfers between devices, body(): lax.all_to_all(lax.all_to_all(sectioned, 'island', split_axis=3, concat_a...  47 us
    all_to_all x1, blocking collectives, body(): lax.all_to_all(sectioned, 'island', split_axis=3, concat_axis=0, tiled=True)  36.8 us
    all_to_all x1, blocking collectives, body(): lax.all_to_all(mean_grad, 'island', split_axis=0, concat_axis=1, tiled=True)  36 us
    all_to_all x1, blocking collectives, body(): lax.all_to_all(picked, 'island', split_axis=0, concat_axis=3, tiled=True)  31.9 us
    unnamed x17, local copies, waits for them, and re-layouts  24.1 us
    all_to_all x1, waiting for transfers between devices, body(): lax.all_to_all(new_param.astype(jnp.bfloat16), 'island', split_axis=1, co...  16.9 us
    all_to_all x2, local copies, waits for them, and re-layouts, body(): lax.all_to_all(lax.all_to_all(picked, 'island', split_axis=0, concat_axis...  11.1 us
  transfers between devices with their start and end apart: 2, of which 2 were waited for; matrix products, arithmetic and copies ran while one was open for 1% of the time, Pallas kernels for 0%

commit v1 on v0

v1 whole, which is shorter than its diff:
```python
import functools

import jax
import jax.numpy as jnp
from jax import lax
from jax.experimental import pallas as pl
from jax.experimental.pallas import tpu as pltpu
from jax.sharding import PartitionSpec as P

LEARN_RATE = 0.7
MOMENTUM_COEF = 0.9
Q_COEF = LEARN_RATE * MOMENTUM_COEF * MOMENTUM_COEF
G_COEF = LEARN_RATE * (1.0 + MOMENTUM_COEF)
TR, TC = 16, 128
VMEM_LIMIT = 32 * 1024 * 1024

SMEM = pl.BlockSpec(memory_space=pltpu.SMEM)
VMEM = pl.BlockSpec(memory_space=pltpu.VMEM)


def call(kernel, out_shape, in_specs, out_specs, scratch=(), grid=None, moved=0):
    extra = {} if grid is None else {"grid": grid}
    return pl.pallas_call(
        kernel,
        out_shape=out_shape,
        in_specs=in_specs,
        out_specs=out_specs,
        scratch_shapes=scratch,
        compiler_params=pltpu.CompilerParams(vmem_limit_bytes=VMEM_LIMIT),
        cost_estimate=pl.CostEstimate(flops=moved, bytes_accessed=moved, transcendentals=0),
        **extra,
    )


def tiles(*lead, dtype=jnp.bfloat16):
    return jax.ShapeDtypeStruct((*lead, TR, TC), dtype)


def pack_by_shard(n, zr, jrs, jcs, me_ref, x_ref, *outs):
    me = me_ref[0]
    for k in range(n):
        z = lax.rem(me + k, n)
        for jr in range(jrs):
            rows = pl.ds(pl.multiple_of(z * zr + jr * TR, TR), TR)
            for jc in range(jcs):
                outs[k][jr * jcs + jc] = x_ref[0, 0, rows, jc * TC : (jc + 1) * TC]


def pack_by_island(n, zr, jrs, jcs, x_ref, out_ref):
    for z in range(n):
        for jr in range(jrs):
            r0 = z * zr + jr * TR
            for jc in range(jcs):
                out_ref[jr * jcs + jc, z] = x_ref[0, 0, r0 : r0 + TR, jc * TC : (jc + 1) * TC]


def split_by_shard(n, count, me_ref, y_ref, *outs):
    me = me_ref[0]
    for k in range(n):
        z = lax.rem(me + k, n)
        for i in range(count):
            outs[k][i] = y_ref[i, z]


def join_by_shard(n, count, me_ref, *refs):
    me = me_ref[0]
    out_ref = refs[n]
    for k in range(n):
        s = lax.rem(me + n - k, n)
        for i in range(count):
            out_ref[i, s] = refs[k][i]


def q_kernel(n, jrs, jcs, p_ref, m_ref, out_ref):
    for jr in range(jrs):
        for s in range(n):
            for jc in range(jcs):
                rows = slice(jr * TR, (jr + 1) * TR)
                c0 = s * jcs * TC + jc * TC
                cols = slice(c0, c0 + TC)
                out_ref[jr * jcs + jc, s] = p_ref[0, rows, cols] - Q_COEF * m_ref[0, rows, cols]


def update_kernel(n, jrs, jcs, g_ref, p_ref, m_ref, np_ref, nm_ref):
    for jr in range(jrs):
        for s in range(n):
            for jc in range(jcs):
                rows = slice(jr * TR, (jr + 1) * TR)
                c0 = s * jcs * TC + jc * TC
                cols = slice(c0, c0 + TC)
                g = g_ref[jr * jcs + jc, s]
                nm = MOMENTUM_COEF * m_ref[0, rows, cols] + g
                nm_ref[0, rows, cols] = nm
                np_ref[0, rows, cols] = p_ref[0, rows, cols] - LEARN_RATE * (g + MOMENTUM_COEF * nm)


def reduce_kernel(n, islands, per_level, level, split, me_ref, path_ref, owner_ref, q_ref, *refs):
    me = me_ref[0]
    if split:
        grads, refs = refs[:n], refs[n:]
    else:
        grads, refs = refs[0], refs[1:]
    other = None
    if level == 0:
        other, refs = refs[0], refs[1:]
    mean_ref, outs, acc, cnt = refs[0], refs[1 : n + 1], refs[n + 1], refs[n + 2]
    acc[...] = jnp.zeros_like(acc)
    for m in range(per_level):
        cnt[m] = 0

    def add(i, carry):
        m = path_ref[i, level]
        cnt[m] = cnt[m] + 1
        for k in range(n):
            if split:
                s = lax.rem(me + n - k, n)
                acc[m, s] += grads[k][i].astype(jnp.float32)
            else:
                acc[m, k] += grads[i, k].astype(jnp.float32)
        return carry

    lax.fori_loop(0, islands, add, 0)

    def finish(m, carry):
        t = owner_ref[level * per_level + m]
        share = jnp.full((TR, TC), 1.0, jnp.float32) / jnp.maximum(cnt[m], 1).astype(jnp.float32)
        row = m if level else t
        for k in range(n):
            s = lax.rem(me + k, n)
            g = acc[m, s] * share
            mean_ref[row, s] = g
            outs[k][m] = (q_ref[t, s] - G_COEF * g).astype(jnp.bfloat16)
        if other is not None:
            row = owner_ref[per_level + m]
            for s in range(n):
                mean_ref[row, s] = other[m, s]
        return carry

    lax.fori_loop(0, per_level, finish, 0)


def pick_kernel(n, islands, levels, me_ref, path_ref, *refs):
    me = me_ref[0]
    out_ref = refs[levels * n]

    def one(i, carry):
        for l in range(levels):
            m = path_ref[i, l]
            for k in range(n):
                out_ref[i, l, lax.rem(me + n - k, n)] = refs[l * n + k][m]
        return carry

    lax.fori_loop(0, islands, one, 0)


def unpack_kernel(n, zr, jrs, jcs, levels, y_ref, out_ref):
    for l in range(levels):
        for z in range(n):
            for jr in range(jrs):
                r0 = z * zr + jr * TR
                for jc in range(jcs):
                    out_ref[0, l, r0 : r0 + TR, jc * TC : (jc + 1) * TC] = y_ref[jr * jcs + jc, l, z]


def body(pseudo_grad, path_table, owner_place, outer_param, outer_momentum):
    islands = lax.axis_size("island")
    n = lax.axis_size("shard")
    levels, full_rows, narrow = pseudo_grad.shape[1:]
    modules = owner_place.shape[0]
    per_level = modules // levels
    zr, width = outer_param.shape[1:]
    jrs, jcs = zr // TR, narrow // TC
    me = lax.axis_index("shard").astype(jnp.int32).reshape(1)

    def swap(x):
        return lax.all_to_all(x, "island", 0, 0, tiled=True)

    def shift(arrays):
        return [arrays[0]] + [
            lax.ppermute(arrays[k], "shard", [(i, (i + k) % n) for i in range(n)]) for k in range(1, n)
        ]

    def level_spec(l):
        return pl.BlockSpec((1, 1, full_rows, narrow), lambda g: (0, l, 0, 0))

    def whole(shape):
        return pl.BlockSpec(shape, lambda g: (0,) * len(shape))

    part = (islands, TR, TC)
    packed1 = call(
        functools.partial(pack_by_island, n, zr, jrs, jcs),
        tiles(islands, n),
        [level_spec(1)],
        whole((islands, n, TR, TC)),
        grid=(1,),
        moved=1 << 21,
    )(pseudo_grad)
    there1 = swap(packed1)
    parts0 = call(
        functools.partial(pack_by_shard, n, zr, jrs, jcs),
        [tiles(islands)] * n,
        [SMEM, level_spec(0)],
        [whole(part)] * n,
        grid=(1,),
        moved=1 << 21,
    )(me, pseudo_grad)
    parts0 = shift(parts0)

    steps = 4
    band = pl.BlockSpec((1, zr // steps, width), lambda g: (0, g, 0))
    tile_band = pl.BlockSpec((islands // steps, n, TR, TC), lambda g: (g, 0, 0, 0))
    q = call(
        functools.partial(q_kernel, n, jrs // steps, jcs),
        tiles(islands, n, dtype=jnp.float32),
        [band, band],
        tile_band,
        grid=(steps,),
        moved=6 << 20,
    )(outer_param, outer_momentum)
    q = swap(q)

    parts1 = call(
        functools.partial(split_by_shard, n, islands),
        [tiles(islands)] * n,
        [SMEM, VMEM],
        [VMEM] * n,
        moved=1 << 21,
    )(me, there1)
    parts1 = shift(parts1)

    joined0 = call(
        functools.partial(join_by_shard, n, islands),
        tiles(islands, n),
        [SMEM] + [VMEM] * n,
        VMEM,
        moved=1 << 21,
    )(me, *parts0)
    grads0 = swap(joined0)

    scratch = (pltpu.VMEM((per_level, n, TR, TC), jnp.float32), pltpu.SMEM((per_level,), jnp.int32))
    mean1, *new1 = call(
        functools.partial(reduce_kernel, n, islands, per_level, 1, True),
        [tiles(per_level, n, dtype=jnp.float32)] + [tiles(per_level)] * n,
        [SMEM] * 3 + [VMEM] * (n + 1),
        [VMEM] * (n + 1),
        scratch,
        moved=1 << 22,
    )(me, path_table, owner_place, q, *parts1)
    new1 = shift(new1)
    mean, *new0 = call(
        functools.partial(reduce_kernel, n, islands, per_level, 0, False),
        [tiles(modules, n, dtype=jnp.float32)] + [tiles(per_level)] * n,
        [SMEM] * 3 + [VMEM] * 3,
        [VMEM] * (n + 1),
        scratch,
        moved=1 << 22,
    )(me, path_table, owner_place, q, grads0, mean1)
    mean = swap(mean)
    new0 = shift(new0)

    picked = call(
        functools.partial(pick_kernel, n, islands, levels),
        tiles(islands, levels, n),
        [SMEM] * 2 + [VMEM] * (levels * n),
        VMEM,
        moved=1 << 22,
    )(me, path_table, *new0, *new1)
    arrived = swap(picked)

    new_param, new_momentum = call(
        functools.partial(update_kernel, n, jrs // steps, jcs),
        [jax.ShapeDtypeStruct(outer_param.shape, jnp.float32)] * 2,
        [tile_band, band, band],
        [band, band],
        grid=(steps,),
        moved=10 << 20,
    )(mean, outer_param, outer_momentum)
    returned = call(
        functools.partial(unpack_kernel, n, zr, jrs, jcs, levels),
        jax.ShapeDtypeStruct(pseudo_grad.shape, jnp.bfloat16),
        [VMEM],
        VMEM,
        moved=1 << 22,
    )(arrived)
    return new_param, new_momentum, returned


def solution(mesh):
    placed = (
        P("island", None, None, "shard"),
        P(),
        P(),
        P("island", "shard", None),
        P("island", "shard", None),
    )
    return jax.shard_map(
        body,
        mesh=mesh,
        in_specs=placed,
        out_specs=(
            P("island", "shard", None),
            P("island", "shard", None),
            P("island", None, None, "shard"),
        ),
        check_vma=False,
    )
```

time: 308 us -> 219 us (0.71)
  blocking collectives: 160 us -> 0 us
  starting transfers between devices: 12.3 us -> 94.4 us
  local copies, waits for them, and re-layouts: 60.1 us -> 24.2 us
  Pallas kernels: 0 us -> 17.1 us
  waiting for transfers between devices: 63.9 us -> 80.9 us
  other arithmetic: 10.1 us -> 0 us
    all_to_all x4 -> x0, blocking collectives: 160 us -> none  [the longest x1 54.8 us: body(): lax.all_to_all(lax.all_to_all(picked, 'island', split_axis=0, concat_axis...]
    ppermute x0 -> x28, starting transfers between devices: none -> 57.4 us  [shift(): lax.ppermute(arrays[k], 'shard', [(i, (i + k) % n) for i in range(n)])]
    ppermute x0 -> x28, waiting for transfers between devices: none -> 45 us  [shift(): lax.ppermute(arrays[k], 'shard', [(i, (i + k) % n) for i in range(n)])]
    all_to_all x2 -> x5, waiting for transfers between devices: 63.9 us -> 35.9 us  [swap(): return lax.all_to_all(x, 'island', 0, 0, tiled=True)]
    all_to_all x5 -> x0, local copies, waits for them, and re-layouts: 25.6 us -> none  [the longest x2 11.1 us: body(): lax.all_to_all(lax.all_to_all(picked, 'island', split_axis=0, concat_axis...]
    all_to_all x2 -> x5, starting transfers between devices: 12.3 us -> 37.1 us  [swap(): return lax.all_to_all(x, 'island', 0, 0, tiled=True)]
    pallas_call x0 -> x10, Pallas kernels: none -> 17.1 us  [the longest x1 4.31 us: body(): call(functools.partial(update_kernel, n, jrs // steps, jcs), [jax.ShapeDt...]
    reshape x4 -> x0, local copies, waits for them, and re-layouts: 6.93 us -> none  [the longest x1 3.85 us: body(): pseudo_grad.reshape(1, levels, shards, islands, sub_rows, narrow)]
  transfers between devices with their start and end apart: 2 -> 33, of which waited for: 2 -> 16; matrix products, arithmetic and copies ran while one was open for 1% -> 0% of each run, Pallas kernels for 0% -> 5%
where the time goes in v1:
time: 219 us; the launch traced here: 218 us
  starting transfers between devices  94.4 us (43%)
  waiting for transfers between devices  80.9 us (37%)
  local copies, waits for them, and re-layouts  24.2 us (11%)
  Pallas kernels  17.1 us (8%)
    ppermute x28, starting transfers between devices, shift(): lax.ppermute(arrays[k], 'shard', [(i, (i + k) % n) for i in range(n)])  57.4 us
    ppermute x28, waiting for transfers between devices, shift(): lax.ppermute(arrays[k], 'shard', [(i, (i + k) % n) for i in range(n)])  45 us
    all_to_all x5, starting transfers between devices, swap(): return lax.all_to_all(x, 'island', 0, 0, tiled=True)  37.1 us
    all_to_all x5, waiting for transfers between devices, swap(): return lax.all_to_all(x, 'island', 0, 0, tiled=True)  35.9 us
    unnamed x73, local copies, waits for them, and re-layouts  24.2 us
  transfers between devices with their start and end apart: 33, of which 16 were waited for; matrix products, arithmetic and copies ran while one was open for 0% of the time, Pallas kernels for 5%

profile of v1, /device:TPU:1, one launch (start us, length us, event | category | flops | bytes accessed | tf_op | source)
XLA Modules:
  0.0 217.6 jit_solution(12108662196866862834)
XLA Ops:
  3.5 8.6 %all-to-all-start.2 = ((bf16[32,8,16,128]{3,2,1,0:T(8,128)(2,1)}), bf16[32,8,16,128]{3,2,1,0:T(8,128)(2,1)S(1)}, u32[]{:S(2)}, u32[]{:S(2)}) async-start(bf16[32,8,16,128]{3,2,1,0:T(8,128)(2,1)} %shard_map.79), calls=%async_computation.2 | async-start | bytes 2097152 | tf_op jit(solution)/shard_map/all_to_all | solution.py:176
  15.4 13.9 %all-to-all-done.2.y_ref = bf16[32,8,16,128]{3,2,1,0:T(8,128)(2,1)S(1)} async-done(((bf16[32,8,16,128]{3,2,1,0:T(8,128)(2,1)}), bf16[32,8,16,128]{3,2,1,0:T(8,128)(2,1)S(1)}, u32[]{:S(2)}, u32[]{:S(2)}) %all-to-all-start.2) | async-done | bytes 1048608 | tf_op jit(solution)/shard_map/all_to_all | solution.py:176
  30.3 4.1 %all-to-all-start = ((f32[32,8,16,128]{3,2,1,0:T(8,128)}), f32[32,8,16,128]{3,2,1,0:T(8,128)S(1)}, u32[]{:S(2)}, u32[]{:S(2)}) async-start(f32[32,8,16,128]{3,2,1,0:T(8,128)} %copy-done.4), calls=%async_computation | async-start | bytes 4194304 | tf_op jit(solution)/shard_map/all_to_all | solution.py:176
  37.9 3.0 %collective-permute-start.1 = (bf16[32,16,128]{2,1,0:T(8,128)(2,1)S(1)}, bf16[32,16,128]{2,1,0:T(8,128)(2,1)S(1)}, u32[]{:S(2)}, u32[]{:S(2)}) collective-permute-start(bf16[32,16,128]{2,1,0:T(8,128)(2,1)S(1)} %get-tuple-element.41), channel_id=1, source_target_pairs={{0,2},{1,3},{2,4},{3,5},{4,6},{5,7},{6,0},{7,1},{8,10},{9,11},{10,... | collective-permute-start | bytes 393224 | tf_op jit(solution)/shard_map/ppermute | solution.py:180
  40.9 3.8 %collective-permute-start.2 = (bf16[32,16,128]{2,1,0:T(8,128)(2,1)S(1)}, bf16[32,16,128]{2,1,0:T(8,128)(2,1)S(1)}, u32[]{:S(2)}, u32[]{:S(2)}) collective-permute-start(bf16[32,16,128]{2,1,0:T(8,128)(2,1)S(1)} %get-tuple-element.42), channel_id=1, source_target_pairs={{0,3},{1,4},{2,5},{3,6},{4,7},{5,0},{6,1},{7,2},{8,11},{9,12},{10,... | collective-permute-start | bytes 393224 | tf_op jit(solution)/shard_map/ppermute | solution.py:180
  45.1 4.5 %collective-permute-start.4 = (bf16[32,16,128]{2,1,0:T(8,128)(2,1)S(1)}, bf16[32,16,128]{2,1,0:T(8,128)(2,1)S(1)}, u32[]{:S(2)}, u32[]{:S(2)}) collective-permute-start(bf16[32,16,128]{2,1,0:T(8,128)(2,1)S(1)} %get-tuple-element.44), channel_id=1, source_target_pairs={{0,5},{1,6},{2,7},{3,0},{4,1},{5,2},{6,3},{7,4},{8,13},{9,14},{10,... | collective-permute-start | bytes 393224 | tf_op jit(solution)/shard_map/ppermute | solution.py:180
  49.6 2.4 %collective-permute-start.5 = (bf16[32,16,128]{2,1,0:T(8,128)(2,1)S(1)}, bf16[32,16,128]{2,1,0:T(8,128)(2,1)S(1)}, u32[]{:S(2)}, u32[]{:S(2)}) collective-permute-start(bf16[32,16,128]{2,1,0:T(8,128)(2,1)S(1)} %get-tuple-element.45), channel_id=1, source_target_pairs={{0,6},{1,7},{2,0},{3,1},{4,2},{5,3},{6,4},{7,5},{8,14},{9,15},{10,... | collective-permute-start | bytes 393224 | tf_op jit(solution)/shard_map/ppermute | solution.py:180
  53.4 7.8 %collective-permute-done.2.refs_3_ = bf16[32,16,128]{2,1,0:T(8,128)(2,1)S(1)} collective-permute-done((bf16[32,16,128]{2,1,0:T(8,128)(2,1)S(1)}, bf16[32,16,128]{2,1,0:T(8,128)(2,1)S(1)}, u32[]{:S(2)}, u32[]{:S(2)}) %collective-permute-start.2) | collective-permute-done | bytes 131104 | tf_op jit(solution)/shard_map/ppermute | solution.py:180
  62.0 7.7 %collective-permute-done.5.refs_6_ = bf16[32,16,128]{2,1,0:T(8,128)(2,1)S(1)} collective-permute-done((bf16[32,16,128]{2,1,0:T(8,128)(2,1)S(1)}, bf16[32,16,128]{2,1,0:T(8,128)(2,1)S(1)}, u32[]{:S(2)}, u32[]{:S(2)}) %collective-permute-start.5) | collective-permute-done | bytes 131104 | tf_op jit(solution)/shard_map/ppermute | solution.py:180
  71.6 7.6 %all-to-all-start.1 = ((bf16[32,8,16,128]{3,2,1,0:T(8,128)(2,1)}), bf16[32,8,16,128]{3,2,1,0:T(8,128)(2,1)S(1)}, u32[]{:S(2)}, u32[]{:S(2)}) async-start(bf16[32,8,16,128]{3,2,1,0:T(8,128)(2,1)} %copy-done.8), calls=%async_computation.1 | async-start | bytes 2097152 | tf_op jit(solution)/shard_map/all_to_all | solution.py:176
  81.3 3.0 %collective-permute-start.7 = (bf16[32,16,128]{2,1,0:T(8,128)(2,1)S(1)}, bf16[32,16,128]{2,1,0:T(8,128)(2,1)S(1)}, u32[]{:S(2)}, u32[]{:S(2)}) collective-permute-start(bf16[32,16,128]{2,1,0:T(8,128)(2,1)S(1)} %get-tuple-element.48), channel_id=1, source_target_pairs={{0,1},{1,2},{2,3},{3,4},{4,5},{5,6},{6,7},{7,0},{8,9},{9,10},{10,1... | collective-permute-start | bytes 393224 | tf_op jit(solution)/shard_map/ppermute | solution.py:180
  85.6 4.5 %collective-permute-start.10 = (bf16[32,16,128]{2,1,0:T(8,128)(2,1)}, bf16[32,16,128]{2,1,0:T(8,128)(2,1)}, u32[]{:S(2)}, u32[]{:S(2)}) collective-permute-start(bf16[32,16,128]{2,1,0:T(8,128)(2,1)} %get-tuple-element.51), channel_id=1, source_target_pairs={{0,4},{1,5},{2,6},{3,7},{4,0},{5,1},{6,2},{7,3},{8,12},{9,13},{10,... | collective-permute-start | bytes 393224 | tf_op jit(solution)/shard_map/ppermute | solution.py:180
  93.3 2.2 %collective-permute-done.8.refs_2_ = bf16[32,16,128]{2,1,0:T(8,128)(2,1)S(1)} collective-permute-done((bf16[32,16,128]{2,1,0:T(8,128)(2,1)S(1)}, bf16[32,16,128]{2,1,0:T(8,128)(2,1)S(1)}, u32[]{:S(2)}, u32[]{:S(2)}) %collective-permute-start.8) | collective-permute-done | bytes 131104 | tf_op jit(solution)/shard_map/ppermute | solution.py:180
  96.3 4.4 %collective-permute-done.9.refs_3_ = bf16[32,16,128]{2,1,0:T(8,128)(2,1)} collective-permute-done((bf16[32,16,128]{2,1,0:T(8,128)(2,1)}, bf16[32,16,128]{2,1,0:T(8,128)(2,1)}, u32[]{:S(2)}, u32[]{:S(2)}) %collective-permute-start.9) | collective-permute-done | bytes 131104 | tf_op jit(solution)/shard_map/ppermute | solution.py:180
  100.7 5.3 %collective-permute-done.10.refs_4_ = bf16[32,16,128]{2,1,0:T(8,128)(2,1)} collective-permute-done((bf16[32,16,128]{2,1,0:T(8,128)(2,1)}, bf16[32,16,128]{2,1,0:T(8,128)(2,1)}, u32[]{:S(2)}, u32[]{:S(2)}) %collective-permute-start.10) | collective-permute-done | bytes 131104 | tf_op jit(solution)/shard_map/ppermute | solution.py:180
  106.0 6.1 %collective-permute-done.12.refs_6_ = bf16[32,16,128]{2,1,0:T(8,128)(2,1)} collective-permute-done((bf16[32,16,128]{2,1,0:T(8,128)(2,1)}, bf16[32,16,128]{2,1,0:T(8,128)(2,1)}, u32[]{:S(2)}, u32[]{:S(2)}) %collective-permute-start.12) | collective-permute-done | bytes 131104 | tf_op jit(solution)/shard_map/ppermute | solution.py:180
  112.1 2.8 %collective-permute-done.13.refs_7_ = bf16[32,16,128]{2,1,0:T(8,128)(2,1)} collective-permute-done((bf16[32,16,128]{2,1,0:T(8,128)(2,1)}, bf16[32,16,128]{2,1,0:T(8,128)(2,1)}, u32[]{:S(2)}, u32[]{:S(2)}) %collective-permute-start.13) | collective-permute-done | bytes 131104 | tf_op jit(solution)/shard_map/ppermute | solution.py:180
  115.5 2.8 %shard_map.81 = (f32[16,8,16,128]{3,2,1,0:T(8,128)S(1)}, bf16[16,16,128]{2,1,0:T(8,128)(2,1)S(1)}, bf16[16,16,128]{2,1,0:T(8,128)(2,1)S(1)}, bf16[16,16,128]{2,1...) custom-call(s32[1]{0:T(128)} %bitcast.me_ref, ...), custom_call_target="tpu_custom_call" | custom-call | flops 4194304 | bytes 4194304 | tf_op jit(solution)/shard_map/pallas_call | solution.py:241
  130.8 7.7 %all-to-all-start.3 = ((f32[32,8,16,128]{3,2,1,0:T(8,128)}), f32[32,8,16,128]{3,2,1,0:T(8,128)}, u32[]{:S(2)}, u32[]{:S(2)}) async-start(f32[32,8,16,128]{3,2,1,0:T(8,128)} %copy-done.11), calls=%async_computation.3 | async-start | bytes 4194304 | tf_op jit(solution)/shard_map/all_to_all | solution.py:176
  140.8 2.9 %collective-permute-start.16 = (bf16[16,16,128]{2,1,0:T(8,128)(2,1)S(1)}, bf16[16,16,128]{2,1,0:T(8,128)(2,1)S(1)}, u32[]{:S(2)}, u32[]{:S(2)}) collective-permute-start(bf16[16,16,128]{2,1,0:T(8,128)(2,1)S(1)} %get-tuple-element.62), channel_id=1, source_target_pairs={{0,3},{1,4},{2,5},{3,6},{4,7},{5,0},{6,1},{7,2},{8,11},{9,12},{10,... | collective-permute-start | bytes 196616 | tf_op jit(solution)/shard_map/ppermute | solution.py:180
  144.6 4.2 %collective-permute-start.18 = (bf16[16,16,128]{2,1,0:T(8,128)(2,1)S(1)}, bf16[16,16,128]{2,1,0:T(8,128)(2,1)S(1)}, u32[]{:S(2)}, u32[]{:S(2)}) collective-permute-start(bf16[16,16,128]{2,1,0:T(8,128)(2,1)S(1)} %get-tuple-element.64), channel_id=1, source_target_pairs={{0,5},{1,6},{2,7},{3,0},{4,1},{5,2},{6,3},{7,4},{8,13},{9,14},{10,... | collective-permute-start | bytes 196616 | tf_op jit(solution)/shard_map/ppermute | solution.py:180
  148.7 2.7 %collective-permute-start.19 = (bf16[16,16,128]{2,1,0:T(8,128)(2,1)S(1)}, bf16[16,16,128]{2,1,0:T(8,128)(2,1)S(1)}, u32[]{:S(2)}, u32[]{:S(2)}) collective-permute-start(bf16[16,16,128]{2,1,0:T(8,128)(2,1)S(1)} %get-tuple-element.65), channel_id=1, source_target_pairs={{0,6},{1,7},{2,0},{3,1},{4,2},{5,3},{6,4},{7,5},{8,14},{9,15},{10,... | collective-permute-start | bytes 196616 | tf_op jit(solution)/shard_map/ppermute | solution.py:180
  152.9 2.9 %collective-permute-start.22 = (bf16[16,16,128]{2,1,0:T(8,128)(2,1)S(1)}, bf16[16,16,128]{2,1,0:T(8,128)(2,1)S(1)}, u32[]{:S(2)}, u32[]{:S(2)}) collective-permute-start(bf16[16,16,128]{2,1,0:T(8,128)(2,1)S(1)} %copy-done.29), channel_id=1, source_target_pairs={{0,2},{1,3},{2,4},{3,5},{4,6},{5,7},{6,0},{7,1},{8,10},{9,11},{10,... | collective-permute-start | bytes 196616 | tf_op jit(solution)/shard_map/ppermute | solution.py:180
  155.8 3.4 %collective-permute-start.23 = (bf16[16,16,128]{2,1,0:T(8,128)(2,1)S(1)}, bf16[16,16,128]{2,1,0:T(8,128)(2,1)S(1)}, u32[]{:S(2)}, u32[]{:S(2)}) collective-permute-start(bf16[16,16,128]{2,1,0:T(8,128)(2,1)S(1)} %copy-done.27), channel_id=1, source_target_pairs={{0,3},{1,4},{2,5},{3,6},{4,7},{5,0},{6,1},{7,2},{8,11},{9,12},{10,... | collective-permute-start | bytes 196616 | tf_op jit(solution)/shard_map/ppermute | solution.py:180
  159.4 3.0 %collective-permute-start.24 = (bf16[16,16,128]{2,1,0:T(8,128)(2,1)S(1)}, bf16[16,16,128]{2,1,0:T(8,128)(2,1)S(1)}, u32[]{:S(2)}, u32[]{:S(2)}) collective-permute-start(bf16[16,16,128]{2,1,0:T(8,128)(2,1)S(1)} %copy-done.25), channel_id=1, source_target_pairs={{0,4},{1,5},{2,6},{3,7},{4,0},{5,1},{6,2},{7,3},{8,12},{9,13},{10,... | collective-permute-start | bytes 196616 | tf_op jit(solution)/shard_map/ppermute | solution.py:180
  165.0 2.1 collective-permute-start.27
  169.3 2.9 %collective-permute-done.26.refs_14_ = bf16[16,16,128]{2,1,0:T(8,128)(2,1)S(1)} collective-permute-done((bf16[16,16,128]{2,1,0:T(8,128)(2,1)S(1)}, bf16[16,16,128]{2,1,0:T(8,128)(2,1)S(1)}, u32[]{:S(2)}, u32[]{:S(2)}) %collective-permute-start.26) | collective-permute-done | bytes 65568 | tf_op jit(solution)/shard_map/ppermute | solution.py:180
  173.9 2.0 shard_map.84
  177.4 9.0 %all-to-all-start.4 = ((bf16[32,2,8,16,128]{4,3,2,1,0:T(8,128)(2,1)}), bf16[32,2,8,16,128]{4,3,2,1,0:T(8,128)(2,1)}, u32[]{:S(2)}, u32[]{:S(2)}) async-start(bf16[32,2,8,16,128]{4,3,2,1,0:T(8,128)(2,1)} %copy-done.7), calls=%async_computation.4 | async-start | bytes 4194304 | tf_op jit(solution)/shard_map/all_to_all | solution.py:176
  188.0 4.3 %shard_map.83 = (f32[1,256,2048]{2,1,0:T(8,128)}, f32[1,256,2048]{2,1,0:T(8,128)}) custom-call(f32[32,8,16,128]{3,2,1,0:T(8,128)} %all-to-all-done.3.g_ref, f32[1,256,2048]{2,1,0:T(8,128)S(1)} %copy-done.1, f32[1,256,2048]{2,1,0:T(8,128)S(1)} %copy-done.3), custom_call_target="tpu_custom_call" | custom-call | flops 10485760 | bytes 10485760 | tf_op jit(solution)/shard_map/pallas_call | solution.py:270
  192.3 22.0 %all-to-all-done.4.y_ref = bf16[32,2,8,16,128]{4,3,2,1,0:T(8,128)(2,1)} async-done(((bf16[32,2,8,16,128]{4,3,2,1,0:T(8,128)(2,1)}), bf16[32,2,8,16,128]{4,3,2,1,0:T(8,128)(2,1)}, u32[]{:S(2)}, u32[]{:S(2)}) %all-to-all-start.4) | async-done | bytes 2097184 | tf_op jit(solution)/shard_map/all_to_all | solution.py:176
  214.3 3.3 %shard_map.85 = bf16[1,2,2048,256]{3,2,1,0:T(8,128)(2,1)} custom-call(bf16[32,2,8,16,128]{4,3,2,1,0:T(8,128)(2,1)} %all-to-all-done.4.y_ref), custom_call_target="tpu_custom_call" | custom-call | flops 4194304 | bytes 4194304 | tf_op jit(solution)/shard_map/pallas_call | solution.py:278
  (117 shorter events, 49.9 us)
Async XLA Ops:
  3.5 25.8 %all-to-all-start.2 = ((bf16[32,8,16,128]{3,2,1,0:T(8,128)(2,1)}), bf16[32,8,16,128]{3,2,1,0:T(8,128)(2,1)S(1)}, u32[]{:S(2)}, u32[]{:S(2)}) async-start(bf16[32,8,16,128]{3,2,1,0:T(8,128)(2,1)} %shard_map.79), calls=%async_computation.2 | async-start | bytes 2097152 | tf_op jit(solution)/shard_map/all_to_all | solution.py:176
  30.3 41.3 %all-to-all-start = ((f32[32,8,16,128]{3,2,1,0:T(8,128)}), f32[32,8,16,128]{3,2,1,0:T(8,128)S(1)}, u32[]{:S(2)}, u32[]{:S(2)}) async-start(f32[32,8,16,128]{3,2,1,0:T(8,128)} %copy-done.4), calls=%async_computation | async-start | bytes 4194304 | tf_op jit(solution)/shard_map/all_to_all | solution.py:176
  36.2 13.4 %collective-permute-start = (bf16[32,16,128]{2,1,0:T(8,128)(2,1)S(1)}, bf16[32,16,128]{2,1,0:T(8,128)(2,1)S(1)}, u32[]{:S(2)}, u32[]{:S(2)}) collective-permute-start(bf16[32,16,128]{2,1,0:T(8,128)(2,1)S(1)} %get-tuple-element.40), channel_id=1, source_target_pairs={{0,1},{1,2},{2,3},{3,4},{4,5},{5,6},{6,7},{7,0},{8,9},{9,10},{10,1... | collective-permute-start | bytes 393224 | tf_op jit(solution)/shard_map/ppermute | solution.py:180
  37.9 14.1 %collective-permute-start.1 = (bf16[32,16,128]{2,1,0:T(8,128)(2,1)S(1)}, bf16[32,16,128]{2,1,0:T(8,128)(2,1)S(1)}, u32[]{:S(2)}, u32[]{:S(2)}) collective-permute-start(bf16[32,16,128]{2,1,0:T(8,128)(2,1)S(1)} %get-tuple-element.41), channel_id=1, source_target_pairs={{0,2},{1,3},{2,4},{3,5},{4,6},{5,7},{6,0},{7,1},{8,10},{9,11},{10,... | collective-permute-start | bytes 393224 | tf_op jit(solution)/shard_map/ppermute | solution.py:180
  40.9 20.3 %collective-permute-start.2 = (bf16[32,16,128]{2,1,0:T(8,128)(2,1)S(1)}, bf16[32,16,128]{2,1,0:T(8,128)(2,1)S(1)}, u32[]{:S(2)}, u32[]{:S(2)}) collective-permute-start(bf16[32,16,128]{2,1,0:T(8,128)(2,1)S(1)} %get-tuple-element.42), channel_id=1, source_target_pairs={{0,3},{1,4},{2,5},{3,6},{4,7},{5,0},{6,1},{7,2},{8,11},{9,12},{10,... | collective-permute-start | bytes 393224 | tf_op jit(solution)/shard_map/ppermute | solution.py:180
  44.7 17.3 %collective-permute-start.3 = (bf16[32,16,128]{2,1,0:T(8,128)(2,1)S(1)}, bf16[32,16,128]{2,1,0:T(8,128)(2,1)S(1)}, u32[]{:S(2)}, u32[]{:S(2)}) collective-permute-start(bf16[32,16,128]{2,1,0:T(8,128)(2,1)S(1)} %get-tuple-element.43), channel_id=1, source_target_pairs={{0,4},{1,5},{2,6},{3,7},{4,0},{5,1},{6,2},{7,3},{8,12},{9,13},{10,... | collective-permute-start | bytes 393224 | tf_op jit(solution)/shard_map/ppermute | solution.py:180
  45.1 16.9 %collective-permute-start.4 = (bf16[32,16,128]{2,1,0:T(8,128)(2,1)S(1)}, bf16[32,16,128]{2,1,0:T(8,128)(2,1)S(1)}, u32[]{:S(2)}, u32[]{:S(2)}) collective-permute-start(bf16[32,16,128]{2,1,0:T(8,128)(2,1)S(1)} %get-tuple-element.44), channel_id=1, source_target_pairs={{0,5},{1,6},{2,7},{3,0},{4,1},{5,2},{6,3},{7,4},{8,13},{9,14},{10,... | collective-permute-start | bytes 393224 | tf_op jit(solution)/shard_map/ppermute | solution.py:180
  49.6 20.1 %collective-permute-start.5 = (bf16[32,16,128]{2,1,0:T(8,128)(2,1)S(1)}, bf16[32,16,128]{2,1,0:T(8,128)(2,1)S(1)}, u32[]{:S(2)}, u32[]{:S(2)}) collective-permute-start(bf16[32,16,128]{2,1,0:T(8,128)(2,1)S(1)} %get-tuple-element.45), channel_id=1, source_target_pairs={{0,6},{1,7},{2,0},{3,1},{4,2},{5,3},{6,4},{7,5},{8,14},{9,15},{10,... | collective-permute-start | bytes 393224 | tf_op jit(solution)/shard_map/ppermute | solution.py:180
  52.0 18.5 %collective-permute-start.6 = (bf16[32,16,128]{2,1,0:T(8,128)(2,1)S(1)}, bf16[32,16,128]{2,1,0:T(8,128)(2,1)S(1)}, u32[]{:S(2)}, u32[]{:S(2)}) collective-permute-start(bf16[32,16,128]{2,1,0:T(8,128)(2,1)S(1)} %get-tuple-element.46), channel_id=1, source_target_pairs={{0,7},{1,0},{2,1},{3,2},{4,3},{5,4},{6,5},{7,6},{8,15},{9,8},{10,9... | collective-permute-start | bytes 393224 | tf_op jit(solution)/shard_map/ppermute | solution.py:180
  71.6 52.7 %all-to-all-start.1 = ((bf16[32,8,16,128]{3,2,1,0:T(8,128)(2,1)}), bf16[32,8,16,128]{3,2,1,0:T(8,128)(2,1)S(1)}, u32[]{:S(2)}, u32[]{:S(2)}) async-start(bf16[32,8,16,128]{3,2,1,0:T(8,128)(2,1)} %copy-done.8), calls=%async_computation.1 | async-start | bytes 2097152 | tf_op jit(solution)/shard_map/all_to_all | solution.py:176
  81.3 10.1 %collective-permute-start.7 = (bf16[32,16,128]{2,1,0:T(8,128)(2,1)S(1)}, bf16[32,16,128]{2,1,0:T(8,128)(2,1)S(1)}, u32[]{:S(2)}, u32[]{:S(2)}) collective-permute-start(bf16[32,16,128]{2,1,0:T(8,128)(2,1)S(1)} %get-tuple-element.48), channel_id=1, source_target_pairs={{0,1},{1,2},{2,3},{3,4},{4,5},{5,6},{6,7},{7,0},{8,9},{9,10},{10,1... | collective-permute-start | bytes 393224 | tf_op jit(solution)/shard_map/ppermute | solution.py:180
  84.4 11.2 %collective-permute-start.8 = (bf16[32,16,128]{2,1,0:T(8,128)(2,1)S(1)}, bf16[32,16,128]{2,1,0:T(8,128)(2,1)S(1)}, u32[]{:S(2)}, u32[]{:S(2)}) collective-permute-start(bf16[32,16,128]{2,1,0:T(8,128)(2,1)S(1)} %get-tuple-element.49), channel_id=1, source_target_pairs={{0,2},{1,3},{2,4},{3,5},{4,6},{5,7},{6,0},{7,1},{8,10},{9,11},{10,... | collective-permute-start | bytes 393224 | tf_op jit(solution)/shard_map/ppermute | solution.py:180
  85.3 15.4 %collective-permute-start.9 = (bf16[32,16,128]{2,1,0:T(8,128)(2,1)}, bf16[32,16,128]{2,1,0:T(8,128)(2,1)}, u32[]{:S(2)}, u32[]{:S(2)}) collective-permute-start(bf16[32,16,128]{2,1,0:T(8,128)(2,1)} %get-tuple-element.50), channel_id=1, source_target_pairs={{0,3},{1,4},{2,5},{3,6},{4,7},{5,0},{6,1},{7,2},{8,11},{9,12},{10,... | collective-permute-start | bytes 393224 | tf_op jit(solution)/shard_map/ppermute | solution.py:180
  85.6 20.4 %collective-permute-start.10 = (bf16[32,16,128]{2,1,0:T(8,128)(2,1)}, bf16[32,16,128]{2,1,0:T(8,128)(2,1)}, u32[]{:S(2)}, u32[]{:S(2)}) collective-permute-start(bf16[32,16,128]{2,1,0:T(8,128)(2,1)} %get-tuple-element.51), channel_id=1, source_target_pairs={{0,4},{1,5},{2,6},{3,7},{4,0},{5,1},{6,2},{7,3},{8,12},{9,13},{10,... | collective-permute-start | bytes 393224 | tf_op jit(solution)/shard_map/ppermute | solution.py:180
  90.0 15.9 %collective-permute-start.11 = (bf16[32,16,128]{2,1,0:T(8,128)(2,1)}, bf16[32,16,128]{2,1,0:T(8,128)(2,1)}, u32[]{:S(2)}, u32[]{:S(2)}) collective-permute-start(bf16[32,16,128]{2,1,0:T(8,128)(2,1)} %get-tuple-element.52), channel_id=1, source_target_pairs={{0,5},{1,6},{2,7},{3,0},{4,1},{5,2},{6,3},{7,4},{8,13},{9,14},{10,... | collective-permute-start | bytes 393224 | tf_op jit(solution)/shard_map/ppermute | solution.py:180
  91.5 20.6 %collective-permute-start.12 = (bf16[32,16,128]{2,1,0:T(8,128)(2,1)}, bf16[32,16,128]{2,1,0:T(8,128)(2,1)}, u32[]{:S(2)}, u32[]{:S(2)}) collective-permute-start(bf16[32,16,128]{2,1,0:T(8,128)(2,1)} %get-tuple-element.53), channel_id=1, source_target_pairs={{0,6},{1,7},{2,0},{3,1},{4,2},{5,3},{6,4},{7,5},{8,14},{9,15},{10,... | collective-permute-start | bytes 393224 | tf_op jit(solution)/shard_map/ppermute | solution.py:180
  95.5 19.3 %collective-permute-start.13 = (bf16[32,16,128]{2,1,0:T(8,128)(2,1)}, bf16[32,16,128]{2,1,0:T(8,128)(2,1)}, u32[]{:S(2)}, u32[]{:S(2)}) collective-permute-start(bf16[32,16,128]{2,1,0:T(8,128)(2,1)} %get-tuple-element.54), channel_id=1, source_target_pairs={{0,7},{1,0},{2,1},{3,2},{4,3},{5,4},{6,5},{7,6},{8,15},{9,8},{10,9... | collective-permute-start | bytes 393224 | tf_op jit(solution)/shard_map/ppermute | solution.py:180
  130.8 46.6 %all-to-all-start.3 = ((f32[32,8,16,128]{3,2,1,0:T(8,128)}), f32[32,8,16,128]{3,2,1,0:T(8,128)}, u32[]{:S(2)}, u32[]{:S(2)}) async-start(f32[32,8,16,128]{3,2,1,0:T(8,128)} %copy-done.11), calls=%async_computation.3 | async-start | bytes 4194304 | tf_op jit(solution)/shard_map/all_to_all | solution.py:176
  138.5 10.2 %collective-permute-start.14 = (bf16[16,16,128]{2,1,0:T(8,128)(2,1)S(1)}, bf16[16,16,128]{2,1,0:T(8,128)(2,1)S(1)}, u32[]{:S(2)}, u32[]{:S(2)}) collective-permute-start(bf16[16,16,128]{2,1,0:T(8,128)(2,1)S(1)} %copy-done.35), channel_id=1, source_target_pairs={{0,1},{1,2},{2,3},{3,4},{4,5},{5,6},{6,7},{7,0},{8,9},{9,10},{10,1... | collective-permute-start | bytes 196616 | tf_op jit(solution)/shard_map/ppermute | solution.py:180
  138.9 12.5 %collective-permute-start.15 = (bf16[16,16,128]{2,1,0:T(8,128)(2,1)S(1)}, bf16[16,16,128]{2,1,0:T(8,128)(2,1)S(1)}, u32[]{:S(2)}, u32[]{:S(2)}) collective-permute-start(bf16[16,16,128]{2,1,0:T(8,128)(2,1)S(1)} %copy-done.33), channel_id=1, source_target_pairs={{0,2},{1,3},{2,4},{3,5},{4,6},{5,7},{6,0},{7,1},{8,10},{9,11},{10,... | collective-permute-start | bytes 196616 | tf_op jit(solution)/shard_map/ppermute | solution.py:180
  140.8 10.6 %collective-permute-start.16 = (bf16[16,16,128]{2,1,0:T(8,128)(2,1)S(1)}, bf16[16,16,128]{2,1,0:T(8,128)(2,1)S(1)}, u32[]{:S(2)}, u32[]{:S(2)}) collective-permute-start(bf16[16,16,128]{2,1,0:T(8,128)(2,1)S(1)} %get-tuple-element.62), channel_id=1, source_target_pairs={{0,3},{1,4},{2,5},{3,6},{4,7},{5,0},{6,1},{7,2},{8,11},{9,12},{10,... | collective-permute-start | bytes 196616 | tf_op jit(solution)/shard_map/ppermute | solution.py:180
  143.7 9.2 %collective-permute-start.17 = (bf16[16,16,128]{2,1,0:T(8,128)(2,1)S(1)}, bf16[16,16,128]{2,1,0:T(8,128)(2,1)S(1)}, u32[]{:S(2)}, u32[]{:S(2)}) collective-permute-start(bf16[16,16,128]{2,1,0:T(8,128)(2,1)S(1)} %get-tuple-element.63), channel_id=1, source_target_pairs={{0,4},{1,5},{2,6},{3,7},{4,0},{5,1},{6,2},{7,3},{8,12},{9,13},{10,... | collective-permute-start | bytes 196616 | tf_op jit(solution)/shard_map/ppermute | solution.py:180
  144.6 11.2 %collective-permute-start.18 = (bf16[16,16,128]{2,1,0:T(8,128)(2,1)S(1)}, bf16[16,16,128]{2,1,0:T(8,128)(2,1)S(1)}, u32[]{:S(2)}, u32[]{:S(2)}) collective-permute-start(bf16[16,16,128]{2,1,0:T(8,128)(2,1)S(1)} %get-tuple-element.64), channel_id=1, source_target_pairs={{0,5},{1,6},{2,7},{3,0},{4,1},{5,2},{6,3},{7,4},{8,13},{9,14},{10,... | collective-permute-start | bytes 196616 | tf_op jit(solution)/shard_map/ppermute | solution.py:180
  148.7 10.7 %collective-permute-start.19 = (bf16[16,16,128]{2,1,0:T(8,128)(2,1)S(1)}, bf16[16,16,128]{2,1,0:T(8,128)(2,1)S(1)}, u32[]{:S(2)}, u32[]{:S(2)}) collective-permute-start(bf16[16,16,128]{2,1,0:T(8,128)(2,1)S(1)} %get-tuple-element.65), channel_id=1, source_target_pairs={{0,6},{1,7},{2,0},{3,1},{4,2},{5,3},{6,4},{7,5},{8,14},{9,15},{10,... | collective-permute-start | bytes 196616 | tf_op jit(solution)/shard_map/ppermute | solution.py:180
  151.4 11.1 %collective-permute-start.20 = (bf16[16,16,128]{2,1,0:T(8,128)(2,1)S(1)}, bf16[16,16,128]{2,1,0:T(8,128)(2,1)S(1)}, u32[]{:S(2)}, u32[]{:S(2)}) collective-permute-start(bf16[16,16,128]{2,1,0:T(8,128)(2,1)S(1)} %get-tuple-element.66), channel_id=1, source_target_pairs={{0,7},{1,0},{2,1},{3,2},{4,3},{5,4},{6,5},{7,6},{8,15},{9,8},{10,9... | collective-permute-start | bytes 196616 | tf_op jit(solution)/shard_map/ppermute | solution.py:180
  151.4 12.1 %collective-permute-start.21 = (bf16[16,16,128]{2,1,0:T(8,128)(2,1)S(1)}, bf16[16,16,128]{2,1,0:T(8,128)(2,1)S(1)}, u32[]{:S(2)}, u32[]{:S(2)}) collective-permute-start(bf16[16,16,128]{2,1,0:T(8,128)(2,1)S(1)} %copy-done.31), channel_id=1, source_target_pairs={{0,1},{1,2},{2,3},{3,4},{4,5},{5,6},{6,7},{7,0},{8,9},{9,10},{10,1... | collective-permute-start | bytes 196616 | tf_op jit(solution)/shard_map/ppermute | solution.py:180
  152.9 12.1 %collective-permute-start.22 = (bf16[16,16,128]{2,1,0:T(8,128)(2,1)S(1)}, bf16[16,16,128]{2,1,0:T(8,128)(2,1)S(1)}, u32[]{:S(2)}, u32[]{:S(2)}) collective-permute-start(bf16[16,16,128]{2,1,0:T(8,128)(2,1)S(1)} %copy-done.29), channel_id=1, source_target_pairs={{0,2},{1,3},{2,4},{3,5},{4,6},{5,7},{6,0},{7,1},{8,10},{9,11},{10,... | collective-permute-start | bytes 196616 | tf_op jit(solution)/shard_map/ppermute | solution.py:180
  155.8 11.3 %collective-permute-start.23 = (bf16[16,16,128]{2,1,0:T(8,128)(2,1)S(1)}, bf16[16,16,128]{2,1,0:T(8,128)(2,1)S(1)}, u32[]{:S(2)}, u32[]{:S(2)}) collective-permute-start(bf16[16,16,128]{2,1,0:T(8,128)(2,1)S(1)} %copy-done.27), channel_id=1, source_target_pairs={{0,3},{1,4},{2,5},{3,6},{4,7},{5,0},{6,1},{7,2},{8,11},{9,12},{10,... | collective-permute-start | bytes 196616 | tf_op jit(solution)/shard_map/ppermute | solution.py:180
  159.4 7.9 %collective-permute-start.24 = (bf16[16,16,128]{2,1,0:T(8,128)(2,1)S(1)}, bf16[16,16,128]{2,1,0:T(8,128)(2,1)S(1)}, u32[]{:S(2)}, u32[]{:S(2)}) collective-permute-start(bf16[16,16,128]{2,1,0:T(8,128)(2,1)S(1)} %copy-done.25), channel_id=1, source_target_pairs={{0,4},{1,5},{2,6},{3,7},{4,0},{5,1},{6,2},{7,3},{8,12},{9,13},{10,... | collective-permute-start | bytes 196616 | tf_op jit(solution)/shard_map/ppermute | solution.py:180
  163.5 8.7 %collective-permute-start.26 = (bf16[16,16,128]{2,1,0:T(8,128)(2,1)S(1)}, bf16[16,16,128]{2,1,0:T(8,128)(2,1)S(1)}, u32[]{:S(2)}, u32[]{:S(2)}) collective-permute-start(bf16[16,16,128]{2,1,0:T(8,128)(2,1)S(1)} %copy-done.21), channel_id=1, source_target_pairs={{0,6},{1,7},{2,0},{3,1},{4,2},{5,3},{6,4},{7,5},{8,14},{9,15},{10,... | collective-permute-start | bytes 196616 | tf_op jit(solution)/shard_map/ppermute | solution.py:180
  165.0 8.9 %collective-permute-start.27 = (bf16[16,16,128]{2,1,0:T(8,128)(2,1)S(1)}, bf16[16,16,128]{2,1,0:T(8,128)(2,1)S(1)}, u32[]{:S(2)}, u32[]{:S(2)}) collective-permute-start(bf16[16,16,128]{2,1,0:T(8,128)(2,1)S(1)} %copy-done.19), channel_id=1, source_target_pairs={{0,7},{1,0},{2,1},{3,2},{4,3},{5,4},{6,5},{7,6},{8,15},{9,8},{10,9... | collective-permute-start | bytes 196616 | tf_op jit(solution)/shard_map/ppermute | solution.py:180
  177.4 36.9 %all-to-all-start.4 = ((bf16[32,2,8,16,128]{4,3,2,1,0:T(8,128)(2,1)}), bf16[32,2,8,16,128]{4,3,2,1,0:T(8,128)(2,1)}, u32[]{:S(2)}, u32[]{:S(2)}) async-start(bf16[32,2,8,16,128]{4,3,2,1,0:T(8,128)(2,1)} %copy-done.7), calls=%async_computation.4 | async-start | bytes 4194304 | tf_op jit(solution)/shard_map/all_to_all | solution.py:176
  (37 other events, 305.5 us)

commit v2 on v0

v2 whole, which is shorter than its diff:
```python
import functools

import jax
import jax.numpy as jnp
from jax import lax
from jax.experimental import pallas as pl
from jax.experimental.pallas import tpu as pltpu
from jax.sharding import PartitionSpec as P

LEARN_RATE = 0.7
MOMENTUM_COEF = 0.9
Q_COEF = LEARN_RATE * MOMENTUM_COEF * MOMENTUM_COEF
G_COEF = LEARN_RATE * (1.0 + MOMENTUM_COEF)
LEAST = 1e-30
LIMIT = 32000.0
STEPS = 8.0
TR, TC = 16, 128
VMEM_LIMIT = 60 * 1024 * 1024

SMEM = pl.BlockSpec(memory_space=pltpu.SMEM)
VMEM = pl.BlockSpec(memory_space=pltpu.VMEM)
AFTER = pl.BlockSpec(memory_space=pl.ANY)


def call(kernel, out_shape, in_specs, out_specs, scratch=(), grid=None, moved=0):
    extra = {} if grid is None else {"grid": grid}
    return pl.pallas_call(
        kernel,
        out_shape=out_shape,
        in_specs=in_specs,
        out_specs=out_specs,
        scratch_shapes=scratch,
        compiler_params=pltpu.CompilerParams(vmem_limit_bytes=VMEM_LIMIT),
        cost_estimate=pl.CostEstimate(flops=moved, bytes_accessed=moved, transcendentals=0),
        **extra,
    )


def tiles(*lead, dtype=jnp.bfloat16):
    return jax.ShapeDtypeStruct((*lead, TR, TC), dtype)


def pack_kernel(jrs, jcs, levels, x_ref, out_ref):
    for l in range(levels):
        for jr in range(jrs):
            rows = slice(jr * TR, (jr + 1) * TR)
            for jc in range(jcs):
                out_ref[jr * jcs + jc, 0, l] = x_ref[0, l, rows, jc * TC : (jc + 1) * TC]


def unpack_kernel(jrs, jcs, levels, y_ref, out_ref):
    for l in range(levels):
        for jr in range(jrs):
            rows = slice(jr * TR, (jr + 1) * TR)
            for jc in range(jcs):
                out_ref[0, l, rows, jc * TC : (jc + 1) * TC] = y_ref[jr * jcs + jc, 0, l]


def store_coded(out, n, values):
    top = functools.reduce(jnp.maximum, [jnp.abs(v) for v in values])
    octave = jnp.ceil(jnp.log2(jnp.maximum(top, LEAST)) * STEPS)
    gain = LIMIT * jnp.exp2(octave * (-1.0 / STEPS))
    for s, v in enumerate(values):
        out[s] = jnp.round(v * gain).astype(jnp.int32).astype(jnp.int16)
    out[n] = octave.astype(jnp.int32).astype(jnp.int16)


def scale_of(code):
    return jnp.exp2(code.astype(jnp.int32).astype(jnp.float32) * (1.0 / STEPS)) * (1.0 / LIMIT)


def decoded(code, scale):
    return code.astype(jnp.int32).astype(jnp.float32) * scale


CORES, SIDE = 2, 4


def place(at_ref):
    at = at_ref[0]
    return at % CORES, at // CORES % SIDE, at // (CORES * SIDE)


def towards(at_ref, emit):
    core, x, _ = place(at_ref)
    for y in range(SIDE):
        for d in range(SIDE):
            emit(d, y, y, lax.rem(x + d, SIDE), core)
            emit(SIDE, y * SIDE + d, y, d, 1 - core)


def q_kernel(n, jcs, at_ref, p_ref, m_ref, *outs):
    def emit(d, slot, y, x, core):
        rows = pl.ds(pl.multiple_of((y * SIDE + x) * TR, TR), TR)
        cols = [pl.ds(pl.multiple_of((s * jcs + core) * TC, TC), TC) for s in range(n)]
        store_coded(outs[d].at[slot], n, [p_ref[0, rows, c] - Q_COEF * m_ref[0, rows, c] for c in cols])

    towards(at_ref, emit)


def update_kernel(n, jrs, jcs, g_ref, p_ref, m_ref, np_ref, nm_ref):
    for jr in range(jrs):
        rows = slice(jr * TR, (jr + 1) * TR)
        for jc in range(jcs):
            j = jr * jcs + jc
            scale = scale_of(g_ref[j, n])
            for s in range(n):
                cols = slice((s * jcs + jc) * TC, (s * jcs + jc + 1) * TC)
                g = decoded(g_ref[j, s], scale)
                nm = MOMENTUM_COEF * m_ref[0, rows, cols] + g
                nm_ref[0, rows, cols] = nm
                np_ref[0, rows, cols] = p_ref[0, rows, cols] - LEARN_RATE * (g + MOMENTUM_COEF * nm)


def reduce_kernel(n, islands, levels, per_level, path_ref, owner_ref, q_ref, x_ref, sum_ref, pick_ref, new, cnt):
    sum_ref[...] = jnp.zeros_like(sum_ref)
    for m in range(levels * per_level):
        cnt[m] = 0

    def add(i, carry):
        for l in range(levels):
            m = l * per_level + path_ref[i, l]
            cnt[m] = cnt[m] + 1
            for s in range(n):
                sum_ref[m, s] += x_ref[i, s, l].astype(jnp.float32)
        return carry

    lax.fori_loop(0, islands, add, 0)

    def finish(m, carry):
        t = owner_ref[m]
        share = jnp.full((TR, TC), 1.0, jnp.float32) / jnp.maximum(cnt[m], 1).astype(jnp.float32)
        scale = scale_of(q_ref[t, n])
        for s in range(n):
            g = sum_ref[m, s] * share
            sum_ref[m, s] = g
            new[m, s] = (decoded(q_ref[t, s], scale) - G_COEF * g).astype(jnp.bfloat16)
        return carry

    lax.fori_loop(0, levels * per_level, finish, 0)

    def pick(i, carry):
        for l in range(levels):
            m = l * per_level + path_ref[i, l]
            for s in range(n):
                pick_ref[i, s, l] = new[m, s]
        return carry

    lax.fori_loop(0, islands, pick, 0)


def mean_kernel(n, modules, at_ref, owner_ref, sum_ref, *refs):
    outs, module = refs[: SIDE + 1], refs[SIDE + 1]
    for m in range(modules):
        module[owner_ref[m]] = m

    def emit(d, slot, y, x, core):
        m = module[(y * SIDE + x) * CORES + core]
        store_coded(outs[d].at[slot], n, [sum_ref[m, s] for s in range(n)])

    towards(at_ref, emit)


def split_other(at_ref, other_ref, *outs):
    _, _, y = place(at_ref)
    for d in range(SIDE):
        for x in range(SIDE):
            outs[d][x] = other_ref[lax.rem(y + d, SIDE) * SIDE + x]


def turn(across, at_ref, *refs):
    ins, outs = refs[:SIDE], refs[SIDE:]
    mine = place(at_ref)[across]
    for d in range(SIDE):
        for e in range(SIDE):
            outs[d][e] = ins[e][lax.rem(mine + d, SIDE)]


def join_all(at_ref, *refs):
    same, other, out_ref = refs[:SIDE], refs[SIDE : 2 * SIDE], refs[2 * SIDE]
    core, x, y = place(at_ref)
    for d in range(SIDE):
        for e in range(SIDE):
            y_d, x_e = lax.rem(y + SIDE - d, SIDE), lax.rem(x + SIDE - e, SIDE)
            out_ref[(y_d * SIDE + x_e) * CORES + core] = same[d][e]
            y_e, x_d = lax.rem(y + SIDE - e, SIDE), lax.rem(x + SIDE - d, SIDE)
            out_ref[(y_e * SIDE + x_d) * CORES + 1 - core] = other[d][e]


def exchange(at, towards_x, other):
    block, dtype = other.shape[1:], other.dtype
    islands = other.shape[0] * CORES
    line = jax.ShapeDtypeStruct((SIDE, *block), dtype)
    moved = 2 * other.size * 2

    def shift(v, dy, dx, dc):
        pairs = []
        for i in range(islands):
            y, rest = divmod(i, SIDE * CORES)
            x, c = divmod(rest, CORES)
            to = ((y + dy) % SIDE * SIDE + (x + dx) % SIDE) * CORES + (c + dc) % CORES
            pairs.append((i, to))
        return lax.ppermute(v, "island", pairs)

    def along(parts, dy, dx):
        out = list(parts)
        for d in (2, 1, 3):
            out[d] = shift(parts[d], dy * d, dx * d, 0)
        return out

    def relay(kernel, parts):
        return call(kernel, [line] * SIDE, [SMEM] + [VMEM] * len(parts), [VMEM] * SIDE, moved=moved)(at, *parts)

    other = shift(other, 0, 0, 1)
    same = along(towards_x, 0, 1)
    other = along(relay(split_other, [other]), 1, 0)
    same = along(relay(functools.partial(turn, 2), same), 1, 0)
    other = along(relay(functools.partial(turn, 1), other), 0, 1)
    return call(
        join_all,
        jax.ShapeDtypeStruct((islands, *block), dtype),
        [SMEM] + [VMEM] * (2 * SIDE),
        VMEM,
        moved=2 * moved,
    )(at, *same, *other)


def body(pseudo_grad, path_table, owner_place, outer_param, outer_momentum):
    islands = lax.axis_size("island")
    n = lax.axis_size("shard")
    levels = pseudo_grad.shape[1]
    narrow = pseudo_grad.shape[3]
    modules = owner_place.shape[0]
    per_level = modules // levels
    zr, width = outer_param.shape[1:]
    jrs, jcs = zr // TR, narrow // TC

    def swap(x):
        x = x.reshape(islands * n, levels, TR, TC)
        x = lax.all_to_all(x, ("island", "shard"), 0, 0, tiled=True)
        return x.reshape(islands, n, levels, TR, TC)

    at = lax.axis_index("island").astype(jnp.int32).reshape(1)
    row_block = pl.BlockSpec((1, levels, zr, narrow), lambda z: (0, 0, z, 0))
    z_tiles = pl.BlockSpec((islands, 1, levels, TR, TC), lambda z: (0, z, 0, 0, 0))
    packed = call(
        functools.partial(pack_kernel, jrs, jcs, levels),
        tiles(islands, n, levels),
        [row_block],
        z_tiles,
        grid=(n,),
        moved=4 << 20,
    )(pseudo_grad)
    grads = swap(packed)

    steps = 4
    band = pl.BlockSpec((1, zr // steps, width), lambda g: (0, g, 0))
    tile_band = pl.BlockSpec((islands // steps, n + 1, TR, TC), lambda g: (g, 0, 0, 0))
    leaving = [tiles(SIDE, n + 1, dtype=jnp.int16)] * SIDE + [tiles(islands // CORES, n + 1, dtype=jnp.int16)]
    *q, other = call(
        functools.partial(q_kernel, n, jcs),
        leaving,
        [SMEM, VMEM, VMEM],
        [VMEM] * (SIDE + 1),
        moved=6 << 20,
    )(at, outer_param, outer_momentum)
    q = exchange(at, q, other)

    sums, picked = call(
        functools.partial(reduce_kernel, n, islands, levels, per_level),
        [tiles(modules, n, dtype=jnp.float32), tiles(islands, n, levels)],
        [SMEM] * 2 + [VMEM] * 2,
        [VMEM] * 2,
        (pltpu.VMEM((modules, n, TR, TC), jnp.bfloat16), pltpu.SMEM((modules,), jnp.int32)),
        moved=8 << 20,
    )(path_table, owner_place, q, grads)
    arrived = swap(picked)

    *mean, other = call(
        functools.partial(mean_kernel, n, modules),
        leaving,
        [SMEM] * 2 + [VMEM],
        [VMEM] * (SIDE + 1),
        (pltpu.SMEM((modules,), jnp.int32),),
        moved=3 << 20,
    )(at, owner_place, sums)
    mean = exchange(at, mean, other)

    new_param, new_momentum = call(
        functools.partial(update_kernel, n, jrs // steps, jcs),
        [jax.ShapeDtypeStruct(outer_param.shape, jnp.float32)] * 2,
        [tile_band, band, band],
        [band, band],
        grid=(steps,),
        moved=10 << 20,
    )(mean, outer_param, outer_momentum)
    returned = call(
        functools.partial(unpack_kernel, jrs, jcs, levels),
        jax.ShapeDtypeStruct(pseudo_grad.shape, jnp.bfloat16),
        [z_tiles],
        row_block,
        grid=(n,),
        moved=4 << 20,
    )(arrived)
    return new_param, new_momentum, returned


def solution(mesh):
    placed = (
        P("island", None, None, "shard"),
        P(),
        P(),
        P("island", "shard", None),
        P("island", "shard", None),
    )
    return jax.shard_map(
        body,
        mesh=mesh,
        in_specs=placed,
        out_specs=(
            P("island", "shard", None),
            P("island", "shard", None),
            P("island", None, None, "shard"),
        ),
        check_vma=False,
    )
```

time: 308 us -> 155 us (0.50)
  blocking collectives: 160 us -> 0 us
  local copies, waits for them, and re-layouts: 60.1 us -> 9.05 us
  starting transfers between devices: 12.3 us -> 62.7 us
  Pallas kernels: 0 us -> 45.9 us
  waiting for transfers between devices: 63.9 us -> 34.1 us
  other arithmetic: 10.1 us -> 0 us
    all_to_all x4 -> x0, blocking collectives: 160 us -> none  [the longest x1 54.8 us: body(): lax.all_to_all(lax.all_to_all(picked, 'island', split_axis=0, concat_axis...]
    all_to_all x2, waiting for transfers between devices: 63.9 us -> 6.63 us  [swap(): x = lax.all_to_all(x, ('island', 'shard'), 0, 0, tiled=True)]
    pallas_call x0 -> x14, Pallas kernels: none -> 45.9 us  [the longest x6 11.8 us: relay(): call(kernel, [line] * SIDE, [SMEM] + [VMEM] * len(parts), [VMEM] * SIDE,...]
    ppermute x0 -> x26, starting transfers between devices: none -> 38.2 us  [shift(): return lax.ppermute(v, 'island', pairs)]
    ppermute x0 -> x26, waiting for transfers between devices: none -> 27.5 us  [shift(): return lax.ppermute(v, 'island', pairs)]
    all_to_all x5 -> x0, local copies, waits for them, and re-layouts: 25.6 us -> none  [the longest x2 11.1 us: body(): lax.all_to_all(lax.all_to_all(picked, 'island', split_axis=0, concat_axis...]
    unnamed x17 -> x59, local copies, waits for them, and re-layouts: 24.1 us -> 9.05 us
    all_to_all x2, starting transfers between devices: 12.3 us -> 24.4 us  [swap(): x = lax.all_to_all(x, ('island', 'shard'), 0, 0, tiled=True)]
  transfers between devices with their start and end apart: 2 -> 28, of which waited for: 2 -> 13; matrix products, arithmetic and copies ran while one was open for 1% -> 0% of each run, Pallas kernels for 0% -> 19%
where the time goes in v2:
time: 155 us; the launch traced here: 153 us
  starting transfers between devices  62.7 us (40%)
  Pallas kernels  45.9 us (30%)
  waiting for transfers between devices  34.1 us (22%)
  local copies, waits for them, and re-layouts  9.05 us (6%)
    ppermute x26, starting transfers between devices, shift(): return lax.ppermute(v, 'island', pairs)  38.2 us
    ppermute x26, waiting for transfers between devices, shift(): return lax.ppermute(v, 'island', pairs)  27.5 us
    all_to_all x2, starting transfers between devices, swap(): x = lax.all_to_all(x, ('island', 'shard'), 0, 0, tiled=True)  24.4 us
    pallas_call x6, Pallas kernels, relay(): call(kernel, [line] * SIDE, [SMEM] + [VMEM] * len(parts), [VMEM] * SIDE,...  11.8 us
    unnamed x59, local copies, waits for them, and re-layouts  9.05 us
    all_to_all x2, waiting for transfers between devices, swap(): x = lax.all_to_all(x, ('island', 'shard'), 0, 0, tiled=True)  6.63 us
    pallas_call x1, Pallas kernels, body(): call(functools.partial(reduce_kernel, n, islands, levels, per_level), [ti...  5.85 us
    pallas_call x1, Pallas kernels, body(): call(functools.partial(unpack_kernel, jrs, jcs, levels), jax.ShapeDtypeSt...  5.76 us
  transfers between devices with their start and end apart: 28, of which 13 were waited for; matrix products, arithmetic and copies ran while one was open for 0% of the time, Pallas kernels for 19%

profile of v2, /device:TPU:1, one launch (start us, length us, event | category | flops | bytes accessed | tf_op | source)
XLA Modules:
  0.0 152.6 jit_solution(9551760012437996911)
XLA Ops:
  0.6 5.8 %shard_map.81 = bf16[32,8,2,16,128]{4,3,2,1,0:T(8,128)(2,1)} custom-call(bf16[1,2,2048,256]{3,2,1,0:T(8,128)(2,1)} %x_ref.1), custom_call_target="tpu_custom_call" | custom-call | flops 4194304 | bytes 4194304 | tf_op jit(solution)/shard_map/pallas_call | solution.py:246
  6.4 15.7 %all-to-all-start = ((bf16[256,2,16,128]{3,2,1,0:T(8,128)(2,1)}), bf16[256,2,16,128]{3,2,1,0:T(8,128)(2,1)S(1)}, u32[]{:S(2)}, u32[]{:S(2)}) async-start(bf16[256,2,16,128]{3,2,1,0:T(8,128)(2,1)} %bitcast.7), calls=%async_computation | async-start | bytes 4194304 | tf_op jit(solution)/shard_map/all_to_all | solution.py:240
  22.1 3.8 %shard_map.76 = (s16[4,9,16,128]{3,2,1,0:T(8,128)(2,1)}, s16[4,9,16,128]{3,2,1,0:T(8,128)(2,1)}, s16[4,9,16,128]{3,2,1,0:T(8,128)(2,1)}, s16[4,9,16,128]{3,2,1,0:T(8,128)(2,1)}, s16[16,9,16,128]{3,2,1,0:T(8,128)(2,1)}) custom-call(s32[1]{0:T(128)} %bitcast.at_ref, f32[1,256,2048]{2,1,0:T(8,128)} %p_ref.3, f32[1,256,2048]{2,1,0:T(8,128)} %m_ref.3), custom_call_target="tpu_custom_call" | custom-call | flops 6291456 | bytes 6291456 | tf_op jit(solution)/shard_map/pallas_call | solution.py:260
  25.9 2.1 %collective-permute-start.6 = (s16[16,9,16,128]{3,2,1,0:T(8,128)(2,1)}, s16[16,9,16,128]{3,2,1,0:T(8,128)(2,1)S(1)}, u32[]{:S(2)}, u32[]{:S(2)}) collective-permute-start(s16[16,9,16,128]{3,2,1,0:T(8,128)(2,1)} %get-tuple-element.49), channel_id=1, source_target_pairs={{0,8},{8,0},{16,24},{24,16},{32,40},{40,32},{48,56},{56,48},{64,72... | collective-permute-start | bytes 1769480 | tf_op jit(solution)/shard_map/ppermute | solution.py:203
  28.0 2.0 %collective-permute-start.1 = (s16[4,9,16,128]{3,2,1,0:T(8,128)(2,1)}, s16[4,9,16,128]{3,2,1,0:T(8,128)(2,1)S(1)}, u32[]{:S(2)}, u32[]{:S(2)}) collective-permute-start(s16[4,9,16,128]{3,2,1,0:T(8,128)(2,1)} %get-tuple-element.43), channel_id=1, source_target_pairs={{0,32},{8,40},{16,48},{24,56},{32,0},{40,8},{48,16},{56,24},{64,96... | collective-permute-start | bytes 442376 | tf_op jit(solution)/shard_map/ppermute | solution.py:203
  35.2 2.5 %collective-permute-start.8 = (s16[4,9,16,128]{3,2,1,0:T(8,128)(2,1)}, s16[4,9,16,128]{3,2,1,0:T(8,128)(2,1)S(1)}, u32[]{:S(2)}, u32[]{:S(2)}) collective-permute-start(s16[4,9,16,128]{3,2,1,0:T(8,128)(2,1)} %get-tuple-element.52), channel_id=1, source_target_pairs={{0,128},{8,136},{16,144},{24,152},{32,160},{40,168},{48,176},{56,1... | collective-permute-start | bytes 442376 | tf_op jit(solution)/shard_map/ppermute | solution.py:203
  38.8 3.1 %collective-permute-done.1.refs_2_ = s16[4,9,16,128]{3,2,1,0:T(8,128)(2,1)S(1)} collective-permute-done((s16[4,9,16,128]{3,2,1,0:T(8,128)(2,1)}, s16[4,9,16,128]{3,2,1,0:T(8,128)(2,1)S(1)}, u32[]{:S(2)}, u32[]{:S(2)}) %collective-permute-start.1) | collective-permute-done | bytes 147488 | tf_op jit(solution)/shard_map/ppermute | solution.py:203
  43.2 2.0 %shard_map.77 = (s16[4,9,16,128]{3,2,1,0:T(8,128)(2,1)}, s16[4,9,16,128]{3,2,1,0:T(8,128)(2,1)}, s16[4,9,16,128]{3,2,1,0:T(8,128)(2,1)}, s16[4,9,16,128]{3,2,1,0:T(8,128)(2,1)}) custom-call(s32[1]{0:T(128)} %bitcast.at_ref, s16[4,9,16,128]{3,2,1,0:T(8,128)(2,1)} %get-tuple-element.41.refs_0_, s16[4,9,16,128]{3,2,1,0:T(8,128)(2,1)} %copy-done.22, ...), custom_call_target="tpu_custom_call" | custom-call | flops 1179648 | bytes 1179648 | tf_op jit(solution)/shard_map/pallas_call | solution.py:212
  45.9 2.5 %collective-permute-start.4 = (s16[4,9,16,128]{3,2,1,0:T(8,128)(2,1)}, s16[4,9,16,128]{3,2,1,0:T(8,128)(2,1)S(1)}, u32[]{:S(2)}, u32[]{:S(2)}) collective-permute-start(s16[4,9,16,128]{3,2,1,0:T(8,128)(2,1)} %get-tuple-element.47), channel_id=1, source_target_pairs={{0,128},{8,136},{16,144},{24,152},{32,160},{40,168},{48,176},{56,1... | collective-permute-start | bytes 442376 | tf_op jit(solution)/shard_map/ppermute | solution.py:203
  50.2 2.0 %shard_map.79 = (s16[4,9,16,128]{3,2,1,0:T(8,128)(2,1)}, s16[4,9,16,128]{3,2,1,0:T(8,128)(2,1)}, s16[4,9,16,128]{3,2,1,0:T(8,128)(2,1)}, s16[4,9,16,128]{3,2,1,0:T(8,128)(2,1)}) custom-call(s32[1]{0:T(128)} %bitcast.at_ref, s16[4,9,16,128]{3,2,1,0:T(8,128)(2,1)} %get-tuple-element.50.refs_0_, s16[4,9,16,128]{3,2,1,0:T(8,128)(2,1)} %copy-done.16, ...), custom_call_target="tpu_custom_call" | custom-call | flops 1179648 | bytes 1179648 | tf_op jit(solution)/shard_map/pallas_call | solution.py:212
  52.9 3.5 %collective-permute-start.11 = (s16[4,9,16,128]{3,2,1,0:T(8,128)(2,1)}, s16[4,9,16,128]{3,2,1,0:T(8,128)(2,1)S(1)}, u32[]{:S(2)}, u32[]{:S(2)}) collective-permute-start(s16[4,9,16,128]{3,2,1,0:T(8,128)(2,1)} %get-tuple-element.56), channel_id=1, source_target_pairs={{0,32},{8,40},{16,48},{24,56},{32,0},{40,8},{48,16},{56,24},{64,96... | collective-permute-start | bytes 442376 | tf_op jit(solution)/shard_map/ppermute | solution.py:203
  57.5 2.9 %collective-permute-done.4.refs_2_ = s16[4,9,16,128]{3,2,1,0:T(8,128)(2,1)S(1)} collective-permute-done((s16[4,9,16,128]{3,2,1,0:T(8,128)(2,1)}, s16[4,9,16,128]{3,2,1,0:T(8,128)(2,1)S(1)}, u32[]{:S(2)}, u32[]{:S(2)}) %collective-permute-start.4) | collective-permute-done | bytes 147488 | tf_op jit(solution)/shard_map/ppermute | solution.py:203
  60.5 7.7 %collective-permute-done.11.refs_6_ = s16[4,9,16,128]{3,2,1,0:T(8,128)(2,1)S(1)} collective-permute-done((s16[4,9,16,128]{3,2,1,0:T(8,128)(2,1)}, s16[4,9,16,128]{3,2,1,0:T(8,128)(2,1)S(1)}, u32[]{:S(2)}, u32[]{:S(2)}) %collective-permute-start.11) | collective-permute-done | bytes 147488 | tf_op jit(solution)/shard_map/ppermute | solution.py:203
  68.9 2.4 %shard_map.80.q_ref = s16[32,9,16,128]{3,2,1,0:T(8,128)(2,1)} custom-call(s32[1]{0:T(128)} %bitcast.at_ref, s16[4,9,16,128]{3,2,1,0:T(8,128)(2,1)} %get-tuple-element.45.refs_0_, s16[4,9,16,128]{3,2,1,0:T(8,128)(2,1)} %copy-done.4, s16[4,9,16,128]{3,2,1,0:T(8,128)(2,1)} %copy-done.6, s16[4,9,16,128]{3,2,1,0:T(8,128)(2,1)} %copy-done.8, ...), custom_call_target="tpu_custom_call" | custom-call | flops 2359296 | bytes 2359296 | tf_op jit(solution)/shard_map/pallas_call | solution.py:219
  71.4 4.4 %all-to-all-done = bf16[256,2,16,128]{3,2,1,0:T(8,128)(2,1)S(1)} async-done(((bf16[256,2,16,128]{3,2,1,0:T(8,128)(2,1)}), bf16[256,2,16,128]{3,2,1,0:T(8,128)(2,1)S(1)}, u32[]{:S(2)}, u32[]{:S(2)}) %all-to-all-start) | async-done | bytes 2097184 | tf_op jit(solution)/shard_map/all_to_all | solution.py:240
  77.1 5.8 %shard_map.82 = (f32[32,8,16,128]{3,2,1,0:T(8,128)}, bf16[32,8,2,16,128]{4,3,2,1,0:T(8,128)(2,1)}) custom-call(s32[32,2]{1,0:T(8,128)} %copy.8.path_ref, s32[32]{0:T(128)} %owner_ref.3, s16[32,9,16,128]{3,2,1,0:T(8,128)(2,1)} %shard_map.80.q_ref, bf16[32,8,2,16,128]{4,3,2,1,0:T(8,128)(2,1)} %bitcast.5), custom_call_target="tpu_custom_call" | custom-call | flops 8388608 | bytes 8388608 | tf_op jit(solution)/shard_map/pallas_call | solution.py:269
  83.0 8.8 %all-to-all-start.1 = ((bf16[256,2,16,128]{3,2,1,0:T(8,128)(2,1)}), bf16[256,2,16,128]{3,2,1,0:T(8,128)(2,1)S(1)}, u32[]{:S(2)}, u32[]{:S(2)}) async-start(bf16[256,2,16,128]{3,2,1,0:T(8,128)(2,1)} %bitcast.8), calls=%async_computation.1 | async-start | bytes 4194304 | tf_op jit(solution)/shard_map/all_to_all | solution.py:240
  91.8 2.9 %shard_map.83 = (s16[4,9,16,128]{3,2,1,0:T(8,128)(2,1)}, s16[4,9,16,128]{3,2,1,0:T(8,128)(2,1)}, s16[4,9,16,128]{3,2,1,0:T(8,128)(2,1)}, s16[4,9,16,128]{3,2,1,0:T(8,128)(2,1)}, s16[16,9,16,128]{3,2,1,0:T(8,128)(2,1)}) custom-call(s32[1]{0:T(128)} %bitcast.at_ref, s32[32]{0:T(128)} %owner_ref.3, f32[32,8,16,128]{3,2,1,0:T(8,128)} %get-tuple-element.58.sum_ref), custom_call_target="tpu_custom_call" | custom-call | flops 3145728 | bytes 3145728 | tf_op jit(solution)/shard_map/pallas_call | solution.py:279
  94.7 2.1 %collective-permute-start.19 = (s16[16,9,16,128]{3,2,1,0:T(8,128)(2,1)}, s16[16,9,16,128]{3,2,1,0:T(8,128)(2,1)S(1)}, u32[]{:S(2)}, u32[]{:S(2)}) collective-permute-start(s16[16,9,16,128]{3,2,1,0:T(8,128)(2,1)} %get-tuple-element.67), channel_id=1, source_target_pairs={{0,8},{8,0},{16,24},{24,16},{32,40},{40,32},{48,56},{56,48},{64,72... | collective-permute-start | bytes 1769480 | tf_op jit(solution)/shard_map/ppermute | solution.py:203
  96.8 2.0 %collective-permute-start.14 = (s16[4,9,16,128]{3,2,1,0:T(8,128)(2,1)}, s16[4,9,16,128]{3,2,1,0:T(8,128)(2,1)S(1)}, u32[]{:S(2)}, u32[]{:S(2)}) collective-permute-start(s16[4,9,16,128]{3,2,1,0:T(8,128)(2,1)} %get-tuple-element.61), channel_id=1, source_target_pairs={{0,32},{8,40},{16,48},{24,56},{32,0},{40,8},{48,16},{56,24},{64,96... | collective-permute-start | bytes 442376 | tf_op jit(solution)/shard_map/ppermute | solution.py:203
  103.9 2.5 %collective-permute-start.21 = (s16[4,9,16,128]{3,2,1,0:T(8,128)(2,1)}, s16[4,9,16,128]{3,2,1,0:T(8,128)(2,1)S(1)}, u32[]{:S(2)}, u32[]{:S(2)}) collective-permute-start(s16[4,9,16,128]{3,2,1,0:T(8,128)(2,1)} %get-tuple-element.70), channel_id=1, source_target_pairs={{0,128},{8,136},{16,144},{24,152},{32,160},{40,168},{48,176},{56,1... | collective-permute-start | bytes 442376 | tf_op jit(solution)/shard_map/ppermute | solution.py:203
  107.5 4.0 %collective-permute-done.14.refs_2_ = s16[4,9,16,128]{3,2,1,0:T(8,128)(2,1)S(1)} collective-permute-done((s16[4,9,16,128]{3,2,1,0:T(8,128)(2,1)}, s16[4,9,16,128]{3,2,1,0:T(8,128)(2,1)S(1)}, u32[]{:S(2)}, u32[]{:S(2)}) %collective-permute-start.14) | collective-permute-done | bytes 147488 | tf_op jit(solution)/shard_map/ppermute | solution.py:203
  112.4 2.0 %shard_map.84 = (s16[4,9,16,128]{3,2,1,0:T(8,128)(2,1)}, s16[4,9,16,128]{3,2,1,0:T(8,128)(2,1)}, s16[4,9,16,128]{3,2,1,0:T(8,128)(2,1)}, s16[4,9,16,128]{3,2,1,0:T(8,128)(2,1)}) custom-call(s32[1]{0:T(128)} %bitcast.at_ref, s16[4,9,16,128]{3,2,1,0:T(8,128)(2,1)} %get-tuple-element.59.refs_0_, s16[4,9,16,128]{3,2,1,0:T(8,128)(2,1)} %copy-done.23, ...), custom_call_target="tpu_custom_call" | custom-call | flops 1179648 | bytes 1179648 | tf_op jit(solution)/shard_map/pallas_call | solution.py:212
  115.3 2.2 %collective-permute-start.17 = (s16[4,9,16,128]{3,2,1,0:T(8,128)(2,1)}, s16[4,9,16,128]{3,2,1,0:T(8,128)(2,1)S(1)}, u32[]{:S(2)}, u32[]{:S(2)}) collective-permute-start(s16[4,9,16,128]{3,2,1,0:T(8,128)(2,1)} %get-tuple-element.65), channel_id=1, source_target_pairs={{0,128},{8,136},{16,144},{24,152},{32,160},{40,168},{48,176},{56,1... | collective-permute-start | bytes 442376 | tf_op jit(solution)/shard_map/ppermute | solution.py:203
  119.3 2.0 %shard_map.86 = (s16[4,9,16,128]{3,2,1,0:T(8,128)(2,1)}, s16[4,9,16,128]{3,2,1,0:T(8,128)(2,1)}, s16[4,9,16,128]{3,2,1,0:T(8,128)(2,1)}, s16[4,9,16,128]{3,2,1,0:T(8,128)(2,1)}) custom-call(s32[1]{0:T(128)} %bitcast.at_ref, s16[4,9,16,128]{3,2,1,0:T(8,128)(2,1)} %get-tuple-element.68.refs_0_, s16[4,9,16,128]{3,2,1,0:T(8,128)(2,1)} %copy-done.17, ...), custom_call_target="tpu_custom_call" | custom-call | flops 1179648 | bytes 1179648 | tf_op jit(solution)/shard_map/pallas_call | solution.py:212
  122.5 2.4 %collective-permute-start.24 = (s16[4,9,16,128]{3,2,1,0:T(8,128)(2,1)}, s16[4,9,16,128]{3,2,1,0:T(8,128)(2,1)S(1)}, u32[]{:S(2)}, u32[]{:S(2)}) collective-permute-start(s16[4,9,16,128]{3,2,1,0:T(8,128)(2,1)} %get-tuple-element.74), channel_id=1, source_target_pairs={{0,32},{8,40},{16,48},{24,56},{32,0},{40,8},{48,16},{56,24},{64,96... | collective-permute-start | bytes 442376 | tf_op jit(solution)/shard_map/ppermute | solution.py:203
  127.3 2.2 %collective-permute-done.17.refs_2_ = s16[4,9,16,128]{3,2,1,0:T(8,128)(2,1)S(1)} collective-permute-done((s16[4,9,16,128]{3,2,1,0:T(8,128)(2,1)}, s16[4,9,16,128]{3,2,1,0:T(8,128)(2,1)S(1)}, u32[]{:S(2)}, u32[]{:S(2)}) %collective-permute-start.17) | collective-permute-done | bytes 147488 | tf_op jit(solution)/shard_map/ppermute | solution.py:203
  129.6 5.4 %collective-permute-done.24.refs_6_ = s16[4,9,16,128]{3,2,1,0:T(8,128)(2,1)S(1)} collective-permute-done((s16[4,9,16,128]{3,2,1,0:T(8,128)(2,1)}, s16[4,9,16,128]{3,2,1,0:T(8,128)(2,1)S(1)}, u32[]{:S(2)}, u32[]{:S(2)}) %collective-permute-start.24) | collective-permute-done | bytes 147488 | tf_op jit(solution)/shard_map/ppermute | solution.py:203
  135.8 2.4 %shard_map.87.g_ref = s16[32,9,16,128]{3,2,1,0:T(8,128)(2,1)} custom-call(s32[1]{0:T(128)} %bitcast.at_ref, s16[4,9,16,128]{3,2,1,0:T(8,128)(2,1)} %get-tuple-element.63.refs_0_, s16[4,9,16,128]{3,2,1,0:T(8,128)(2,1)} %copy-done.5, s16[4,9,16,128]{3,2,1,0:T(8,128)(2,1)} %copy-done.7, s16[4,9,16,128]{3,2,1,0:T(8,128)(2,1)} %copy-done.9, ...), custom_call_target="tpu_custom_call" | custom-call | flops 2359296 | bytes 2359296 | tf_op jit(solution)/shard_map/pallas_call | solution.py:219
  138.2 5.1 %shard_map.88 = (f32[1,256,2048]{2,1,0:T(8,128)}, f32[1,256,2048]{2,1,0:T(8,128)}) custom-call(s16[32,9,16,128]{3,2,1,0:T(8,128)(2,1)} %shard_map.87.g_ref, f32[1,256,2048]{2,1,0:T(8,128)} %p_ref.3, f32[1,256,2048]{2,1,0:T(8,128)} %m_ref.3), custom_call_target="tpu_custom_call" | custom-call | flops 10485760 | bytes 10485760 | tf_op jit(solution)/shard_map/pallas_call | solution.py:289
  143.3 2.2 %all-to-all-done.1 = bf16[256,2,16,128]{3,2,1,0:T(8,128)(2,1)S(1)} async-done(((bf16[256,2,16,128]{3,2,1,0:T(8,128)(2,1)}), bf16[256,2,16,128]{3,2,1,0:T(8,128)(2,1)S(1)}, u32[]{:S(2)}, u32[]{:S(2)}) %all-to-all-start.1) | async-done | bytes 2097184 | tf_op jit(solution)/shard_map/all_to_all | solution.py:240
  146.8 5.8 %shard_map.89 = bf16[1,2,2048,256]{3,2,1,0:T(8,128)(2,1)} custom-call(bf16[32,8,2,16,128]{4,3,2,1,0:T(8,128)(2,1)} %bitcast.6), custom_call_target="tpu_custom_call" | custom-call | flops 4194304 | bytes 4194304 | tf_op jit(solution)/shard_map/pallas_call | solution.py:297
  (97 shorter events, 29.3 us)
Async XLA Ops:
  6.4 69.4 %all-to-all-start = ((bf16[256,2,16,128]{3,2,1,0:T(8,128)(2,1)}), bf16[256,2,16,128]{3,2,1,0:T(8,128)(2,1)S(1)}, u32[]{:S(2)}, u32[]{:S(2)}) async-start(bf16[256,2,16,128]{3,2,1,0:T(8,128)(2,1)} %bitcast.7), calls=%async_computation | async-start | bytes 4194304 | tf_op jit(solution)/shard_map/all_to_all | solution.py:240
  22.1 34.8 %copy-start.28 = (s32[32,2]{0,1:T(2,128)S(1)}, s32[32,2]{0,1:T(2,128)}, u32[]{:S(2)}) copy-start(s32[32,2]{0,1:T(2,128)} %param.6) | copy-start | bytes 772
  25.9 5.3 %collective-permute-start.6 = (s16[16,9,16,128]{3,2,1,0:T(8,128)(2,1)}, s16[16,9,16,128]{3,2,1,0:T(8,128)(2,1)S(1)}, u32[]{:S(2)}, u32[]{:S(2)}) collective-permute-start(s16[16,9,16,128]{3,2,1,0:T(8,128)(2,1)} %get-tuple-element.49), channel_id=1, source_target_pairs={{0,8},{8,0},{16,24},{24,16},{32,40},{40,32},{48,56},{56,48},{64,72... | collective-permute-start | bytes 1769480 | tf_op jit(solution)/shard_map/ppermute | solution.py:203
  28.0 9.6 %collective-permute-start = (s16[4,9,16,128]{3,2,1,0:T(8,128)(2,1)}, s16[4,9,16,128]{3,2,1,0:T(8,128)(2,1)S(1)}, u32[]{:S(2)}, u32[]{:S(2)}) collective-permute-start(s16[4,9,16,128]{3,2,1,0:T(8,128)(2,1)} %get-tuple-element.42), channel_id=1, source_target_pairs={{0,16},{8,24},{16,32},{24,40},{32,48},{40,56},{48,0},{56,8},{64,80... | collective-permute-start | bytes 442376 | tf_op jit(solution)/shard_map/ppermute | solution.py:203
  28.0 13.9 %collective-permute-start.1 = (s16[4,9,16,128]{3,2,1,0:T(8,128)(2,1)}, s16[4,9,16,128]{3,2,1,0:T(8,128)(2,1)S(1)}, u32[]{:S(2)}, u32[]{:S(2)}) collective-permute-start(s16[4,9,16,128]{3,2,1,0:T(8,128)(2,1)} %get-tuple-element.43), channel_id=1, source_target_pairs={{0,32},{8,40},{16,48},{24,56},{32,0},{40,8},{48,16},{56,24},{64,96... | collective-permute-start | bytes 442376 | tf_op jit(solution)/shard_map/ppermute | solution.py:203
  30.0 12.5 %collective-permute-start.2 = (s16[4,9,16,128]{3,2,1,0:T(8,128)(2,1)}, s16[4,9,16,128]{3,2,1,0:T(8,128)(2,1)S(1)}, u32[]{:S(2)}, u32[]{:S(2)}) collective-permute-start(s16[4,9,16,128]{3,2,1,0:T(8,128)(2,1)} %get-tuple-element.44), channel_id=1, source_target_pairs={{0,48},{8,56},{16,0},{24,8},{32,16},{40,24},{48,32},{56,40},{64,11... | collective-permute-start | bytes 442376 | tf_op jit(solution)/shard_map/ppermute | solution.py:203
  34.0 14.4 %collective-permute-start.7 = (s16[4,9,16,128]{3,2,1,0:T(8,128)(2,1)}, s16[4,9,16,128]{3,2,1,0:T(8,128)(2,1)S(1)}, u32[]{:S(2)}, u32[]{:S(2)}) collective-permute-start(s16[4,9,16,128]{3,2,1,0:T(8,128)(2,1)} %get-tuple-element.51), channel_id=1, source_target_pairs={{0,64},{8,72},{16,80},{24,88},{32,96},{40,104},{48,112},{56,120},{... | collective-permute-start | bytes 442376 | tf_op jit(solution)/shard_map/ppermute | solution.py:203
  35.2 14.3 %collective-permute-start.8 = (s16[4,9,16,128]{3,2,1,0:T(8,128)(2,1)}, s16[4,9,16,128]{3,2,1,0:T(8,128)(2,1)S(1)}, u32[]{:S(2)}, u32[]{:S(2)}) collective-permute-start(s16[4,9,16,128]{3,2,1,0:T(8,128)(2,1)} %get-tuple-element.52), channel_id=1, source_target_pairs={{0,128},{8,136},{16,144},{24,152},{32,160},{40,168},{48,176},{56,1... | collective-permute-start | bytes 442376 | tf_op jit(solution)/shard_map/ppermute | solution.py:203
  37.7 11.8 %collective-permute-start.9 = (s16[4,9,16,128]{3,2,1,0:T(8,128)(2,1)}, s16[4,9,16,128]{3,2,1,0:T(8,128)(2,1)S(1)}, u32[]{:S(2)}, u32[]{:S(2)}) collective-permute-start(s16[4,9,16,128]{3,2,1,0:T(8,128)(2,1)} %get-tuple-element.53), channel_id=1, source_target_pairs={{0,192},{8,200},{16,208},{24,216},{32,224},{40,232},{48,240},{56,2... | collective-permute-start | bytes 442376 | tf_op jit(solution)/shard_map/ppermute | solution.py:203
  45.2 11.1 %collective-permute-start.3 = (s16[4,9,16,128]{3,2,1,0:T(8,128)(2,1)}, s16[4,9,16,128]{3,2,1,0:T(8,128)(2,1)S(1)}, u32[]{:S(2)}, u32[]{:S(2)}) collective-permute-start(s16[4,9,16,128]{3,2,1,0:T(8,128)(2,1)} %get-tuple-element.46), channel_id=1, source_target_pairs={{0,64},{8,72},{16,80},{24,88},{32,96},{40,104},{48,112},{56,120},{... | collective-permute-start | bytes 442376 | tf_op jit(solution)/shard_map/ppermute | solution.py:203
  45.9 14.5 %collective-permute-start.4 = (s16[4,9,16,128]{3,2,1,0:T(8,128)(2,1)}, s16[4,9,16,128]{3,2,1,0:T(8,128)(2,1)S(1)}, u32[]{:S(2)}, u32[]{:S(2)}) collective-permute-start(s16[4,9,16,128]{3,2,1,0:T(8,128)(2,1)} %get-tuple-element.47), channel_id=1, source_target_pairs={{0,128},{8,136},{16,144},{24,152},{32,160},{40,168},{48,176},{56,1... | collective-permute-start | bytes 442376 | tf_op jit(solution)/shard_map/ppermute | solution.py:203
  48.4 12.1 %collective-permute-start.5 = (s16[4,9,16,128]{3,2,1,0:T(8,128)(2,1)}, s16[4,9,16,128]{3,2,1,0:T(8,128)(2,1)S(1)}, u32[]{:S(2)}, u32[]{:S(2)}) collective-permute-start(s16[4,9,16,128]{3,2,1,0:T(8,128)(2,1)} %get-tuple-element.48), channel_id=1, source_target_pairs={{0,192},{8,200},{16,208},{24,216},{32,224},{40,232},{48,240},{56,2... | collective-permute-start | bytes 442376 | tf_op jit(solution)/shard_map/ppermute | solution.py:203
  52.2 8.3 %collective-permute-start.10 = (s16[4,9,16,128]{3,2,1,0:T(8,128)(2,1)}, s16[4,9,16,128]{3,2,1,0:T(8,128)(2,1)S(1)}, u32[]{:S(2)}, u32[]{:S(2)}) collective-permute-start(s16[4,9,16,128]{3,2,1,0:T(8,128)(2,1)} %get-tuple-element.55), channel_id=1, source_target_pairs={{0,16},{8,24},{16,32},{24,40},{32,48},{40,56},{48,0},{56,8},{64,80... | collective-permute-start | bytes 442376 | tf_op jit(solution)/shard_map/ppermute | solution.py:203
  52.9 15.3 %collective-permute-start.11 = (s16[4,9,16,128]{3,2,1,0:T(8,128)(2,1)}, s16[4,9,16,128]{3,2,1,0:T(8,128)(2,1)S(1)}, u32[]{:S(2)}, u32[]{:S(2)}) collective-permute-start(s16[4,9,16,128]{3,2,1,0:T(8,128)(2,1)} %get-tuple-element.56), channel_id=1, source_target_pairs={{0,32},{8,40},{16,48},{24,56},{32,0},{40,8},{48,16},{56,24},{64,96... | collective-permute-start | bytes 442376 | tf_op jit(solution)/shard_map/ppermute | solution.py:203
  56.4 11.8 %copy-start.4 = (s16[4,9,16,128]{3,2,1,0:T(8,128)(2,1)}, s16[4,9,16,128]{3,2,1,0:T(8,128)(2,1)S(1)}, u32[]{:S(2)}) copy-start(s16[4,9,16,128]{3,2,1,0:T(8,128)(2,1)S(1)} %collective-permute-done.3.refs_1_) | copy-start | bytes 442372
  56.4 11.8 %collective-permute-start.12 = (s16[4,9,16,128]{3,2,1,0:T(8,128)(2,1)}, s16[4,9,16,128]{3,2,1,0:T(8,128)(2,1)S(1)}, u32[]{:S(2)}, u32[]{:S(2)}) collective-permute-start(s16[4,9,16,128]{3,2,1,0:T(8,128)(2,1)} %get-tuple-element.57), channel_id=1, source_target_pairs={{0,48},{8,56},{16,0},{24,8},{32,16},{40,24},{48,32},{56,40},{64,11... | collective-permute-start | bytes 442376 | tf_op jit(solution)/shard_map/ppermute | solution.py:203
  60.4 7.8 %copy-start.6 = (s16[4,9,16,128]{3,2,1,0:T(8,128)(2,1)}, s16[4,9,16,128]{3,2,1,0:T(8,128)(2,1)S(1)}, u32[]{:S(2)}) copy-start(s16[4,9,16,128]{3,2,1,0:T(8,128)(2,1)S(1)} %collective-permute-done.4.refs_2_) | copy-start | bytes 442372
  83.0 62.5 %all-to-all-start.1 = ((bf16[256,2,16,128]{3,2,1,0:T(8,128)(2,1)}), bf16[256,2,16,128]{3,2,1,0:T(8,128)(2,1)S(1)}, u32[]{:S(2)}, u32[]{:S(2)}) async-start(bf16[256,2,16,128]{3,2,1,0:T(8,128)(2,1)} %bitcast.8), calls=%async_computation.1 | async-start | bytes 4194304 | tf_op jit(solution)/shard_map/all_to_all | solution.py:240
  94.7 5.3 %collective-permute-start.19 = (s16[16,9,16,128]{3,2,1,0:T(8,128)(2,1)}, s16[16,9,16,128]{3,2,1,0:T(8,128)(2,1)S(1)}, u32[]{:S(2)}, u32[]{:S(2)}) collective-permute-start(s16[16,9,16,128]{3,2,1,0:T(8,128)(2,1)} %get-tuple-element.67), channel_id=1, source_target_pairs={{0,8},{8,0},{16,24},{24,16},{32,40},{40,32},{48,56},{56,48},{64,72... | collective-permute-start | bytes 1769480 | tf_op jit(solution)/shard_map/ppermute | solution.py:203
  96.8 9.9 %collective-permute-start.13 = (s16[4,9,16,128]{3,2,1,0:T(8,128)(2,1)}, s16[4,9,16,128]{3,2,1,0:T(8,128)(2,1)S(1)}, u32[]{:S(2)}, u32[]{:S(2)}) collective-permute-start(s16[4,9,16,128]{3,2,1,0:T(8,128)(2,1)} %get-tuple-element.60), channel_id=1, source_target_pairs={{0,16},{8,24},{16,32},{24,40},{32,48},{40,56},{48,0},{56,8},{64,80... | collective-permute-start | bytes 442376 | tf_op jit(solution)/shard_map/ppermute | solution.py:203
  96.8 14.7 %collective-permute-start.14 = (s16[4,9,16,128]{3,2,1,0:T(8,128)(2,1)}, s16[4,9,16,128]{3,2,1,0:T(8,128)(2,1)S(1)}, u32[]{:S(2)}, u32[]{:S(2)}) collective-permute-start(s16[4,9,16,128]{3,2,1,0:T(8,128)(2,1)} %get-tuple-element.61), channel_id=1, source_target_pairs={{0,32},{8,40},{16,48},{24,56},{32,0},{40,8},{48,16},{56,24},{64,96... | collective-permute-start | bytes 442376 | tf_op jit(solution)/shard_map/ppermute | solution.py:203
  98.8 12.9 %collective-permute-start.15 = (s16[4,9,16,128]{3,2,1,0:T(8,128)(2,1)}, s16[4,9,16,128]{3,2,1,0:T(8,128)(2,1)S(1)}, u32[]{:S(2)}, u32[]{:S(2)}) collective-permute-start(s16[4,9,16,128]{3,2,1,0:T(8,128)(2,1)} %get-tuple-element.62), channel_id=1, source_target_pairs={{0,48},{8,56},{16,0},{24,8},{32,16},{40,24},{48,32},{56,40},{64,11... | collective-permute-start | bytes 442376 | tf_op jit(solution)/shard_map/ppermute | solution.py:203
  102.8 14.7 %collective-permute-start.20 = (s16[4,9,16,128]{3,2,1,0:T(8,128)(2,1)}, s16[4,9,16,128]{3,2,1,0:T(8,128)(2,1)S(1)}, u32[]{:S(2)}, u32[]{:S(2)}) collective-permute-start(s16[4,9,16,128]{3,2,1,0:T(8,128)(2,1)} %get-tuple-element.69), channel_id=1, source_target_pairs={{0,64},{8,72},{16,80},{24,88},{32,96},{40,104},{48,112},{56,120},{... | collective-permute-start | bytes 442376 | tf_op jit(solution)/shard_map/ppermute | solution.py:203
  103.9 14.7 %collective-permute-start.21 = (s16[4,9,16,128]{3,2,1,0:T(8,128)(2,1)}, s16[4,9,16,128]{3,2,1,0:T(8,128)(2,1)S(1)}, u32[]{:S(2)}, u32[]{:S(2)}) collective-permute-start(s16[4,9,16,128]{3,2,1,0:T(8,128)(2,1)} %get-tuple-element.70), channel_id=1, source_target_pairs={{0,128},{8,136},{16,144},{24,152},{32,160},{40,168},{48,176},{56,1... | collective-permute-start | bytes 442376 | tf_op jit(solution)/shard_map/ppermute | solution.py:203
  106.8 11.9 %collective-permute-start.22 = (s16[4,9,16,128]{3,2,1,0:T(8,128)(2,1)}, s16[4,9,16,128]{3,2,1,0:T(8,128)(2,1)S(1)}, u32[]{:S(2)}, u32[]{:S(2)}) collective-permute-start(s16[4,9,16,128]{3,2,1,0:T(8,128)(2,1)} %get-tuple-element.71), channel_id=1, source_target_pairs={{0,192},{8,200},{16,208},{24,216},{32,224},{40,232},{48,240},{56,2... | collective-permute-start | bytes 442376 | tf_op jit(solution)/shard_map/ppermute | solution.py:203
  114.4 11.2 %collective-permute-start.16 = (s16[4,9,16,128]{3,2,1,0:T(8,128)(2,1)}, s16[4,9,16,128]{3,2,1,0:T(8,128)(2,1)S(1)}, u32[]{:S(2)}, u32[]{:S(2)}) collective-permute-start(s16[4,9,16,128]{3,2,1,0:T(8,128)(2,1)} %get-tuple-element.64), channel_id=1, source_target_pairs={{0,64},{8,72},{16,80},{24,88},{32,96},{40,104},{48,112},{56,120},{... | collective-permute-start | bytes 442376 | tf_op jit(solution)/shard_map/ppermute | solution.py:203
  115.3 14.3 %collective-permute-start.17 = (s16[4,9,16,128]{3,2,1,0:T(8,128)(2,1)}, s16[4,9,16,128]{3,2,1,0:T(8,128)(2,1)S(1)}, u32[]{:S(2)}, u32[]{:S(2)}) collective-permute-start(s16[4,9,16,128]{3,2,1,0:T(8,128)(2,1)} %get-tuple-element.65), channel_id=1, source_target_pairs={{0,128},{8,136},{16,144},{24,152},{32,160},{40,168},{48,176},{56,1... | collective-permute-start | bytes 442376 | tf_op jit(solution)/shard_map/ppermute | solution.py:203
  117.5 12.1 %collective-permute-start.18 = (s16[4,9,16,128]{3,2,1,0:T(8,128)(2,1)}, s16[4,9,16,128]{3,2,1,0:T(8,128)(2,1)S(1)}, u32[]{:S(2)}, u32[]{:S(2)}) collective-permute-start(s16[4,9,16,128]{3,2,1,0:T(8,128)(2,1)} %get-tuple-element.66), channel_id=1, source_target_pairs={{0,192},{8,200},{16,208},{24,216},{32,224},{40,232},{48,240},{56,2... | collective-permute-start | bytes 442376 | tf_op jit(solution)/shard_map/ppermute | solution.py:203
  121.3 8.3 %collective-permute-start.23 = (s16[4,9,16,128]{3,2,1,0:T(8,128)(2,1)}, s16[4,9,16,128]{3,2,1,0:T(8,128)(2,1)S(1)}, u32[]{:S(2)}, u32[]{:S(2)}) collective-permute-start(s16[4,9,16,128]{3,2,1,0:T(8,128)(2,1)} %get-tuple-element.73), channel_id=1, source_target_pairs={{0,16},{8,24},{16,32},{24,40},{32,48},{40,56},{48,0},{56,8},{64,80... | collective-permute-start | bytes 442376 | tf_op jit(solution)/shard_map/ppermute | solution.py:203
  122.5 12.6 %collective-permute-start.24 = (s16[4,9,16,128]{3,2,1,0:T(8,128)(2,1)}, s16[4,9,16,128]{3,2,1,0:T(8,128)(2,1)S(1)}, u32[]{:S(2)}, u32[]{:S(2)}) collective-permute-start(s16[4,9,16,128]{3,2,1,0:T(8,128)(2,1)} %get-tuple-element.74), channel_id=1, source_target_pairs={{0,32},{8,40},{16,48},{24,56},{32,0},{40,8},{48,16},{56,24},{64,96... | collective-permute-start | bytes 442376 | tf_op jit(solution)/shard_map/ppermute | solution.py:203
  125.6 9.4 %copy-start.5 = (s16[4,9,16,128]{3,2,1,0:T(8,128)(2,1)}, s16[4,9,16,128]{3,2,1,0:T(8,128)(2,1)S(1)}, u32[]{:S(2)}) copy-start(s16[4,9,16,128]{3,2,1,0:T(8,128)(2,1)S(1)} %collective-permute-done.16.refs_1_) | copy-start | bytes 442372
  125.6 9.4 %collective-permute-start.25 = (s16[4,9,16,128]{3,2,1,0:T(8,128)(2,1)}, s16[4,9,16,128]{3,2,1,0:T(8,128)(2,1)S(1)}, u32[]{:S(2)}, u32[]{:S(2)}) collective-permute-start(s16[4,9,16,128]{3,2,1,0:T(8,128)(2,1)} %get-tuple-element.75), channel_id=1, source_target_pairs={{0,48},{8,56},{16,0},{24,8},{32,16},{40,24},{48,32},{56,40},{64,11... | collective-permute-start | bytes 442376 | tf_op jit(solution)/shard_map/ppermute | solution.py:203
  (25 other events, 56.6 us)

commit v3 on v2

--- a/solution.py
+++ b/solution.py
@@ -15,24 +15,24 @@
 LIMIT = 32000.0
 STEPS = 8.0
 TR, TC = 16, 128
-VMEM_LIMIT = 60 * 1024 * 1024
+MIB = 1024 * 1024
 
 SMEM = pl.BlockSpec(memory_space=pltpu.SMEM)
 VMEM = pl.BlockSpec(memory_space=pltpu.VMEM)
-AFTER = pl.BlockSpec(memory_space=pl.ANY)
-
-
-def call(kernel, out_shape, in_specs, out_specs, scratch=(), grid=None, moved=0):
-    extra = {} if grid is None else {"grid": grid}
+ANY = pl.BlockSpec(memory_space=pl.ANY)
+DMA = pltpu.SemaphoreType.DMA
+copy = pltpu.make_async_copy
+
+
+def call(kernel, out_shape, in_specs, out_specs, scratch=(), vmem=16, moved=0):
     return pl.pallas_call(
         kernel,
         out_shape=out_shape,
         in_specs=in_specs,
         out_specs=out_specs,
         scratch_shapes=scratch,
-        compiler_params=pltpu.CompilerParams(vmem_limit_bytes=VMEM_LIMIT),
+        compiler_params=pltpu.CompilerParams(vmem_limit_bytes=vmem * MIB),
         cost_estimate=pl.CostEstimate(flops=moved, bytes_accessed=moved, transcendentals=0),
-        **extra,
     )
 
 
@@ -40,20 +40,45 @@
     return jax.ShapeDtypeStruct((*lead, TR, TC), dtype)
 
 
-def pack_kernel(jrs, jcs, levels, x_ref, out_ref):
-    for l in range(levels):
-        for jr in range(jrs):
-            rows = slice(jr * TR, (jr + 1) * TR)
-            for jc in range(jcs):
-                out_ref[jr * jcs + jc, 0, l] = x_ref[0, l, rows, jc * TC : (jc + 1) * TC]
-
-
-def unpack_kernel(jrs, jcs, levels, y_ref, out_ref):
-    for l in range(levels):
-        for jr in range(jrs):
-            rows = slice(jr * TR, (jr + 1) * TR)
-            for jc in range(jcs):
-                out_ref[0, l, rows, jc * TC : (jc + 1) * TC] = y_ref[jr * jcs + jc, 0, l]
+def stream(ins, work, outs):
+    for c in ins:
+        c.start()
+    for k, c in enumerate(ins):
+        c.wait()
+        work(k)
+        outs[k].start()
+    for c in outs:
+        c.wait()
+
+
+def pack_kernel(n, zr, jrs, jcs, levels, x_ref, out_ref, rows_vm, tiles_vm, in_sem, out_sem):
+    def work(z):
+        for l in range(levels):
+            for jr in range(jrs):
+                for jc in range(jcs):
+                    tile = rows_vm[z, l, jr * TR : (jr + 1) * TR, jc * TC : (jc + 1) * TC]
+                    tiles_vm[z, jr * jcs + jc, l] = tile
+
+    stream(
+        [copy(x_ref.at[0, :, pl.ds(z * zr, zr)], rows_vm.at[z], in_sem.at[z]) for z in range(n)],
+        work,
+        [copy(tiles_vm.at[z], out_ref.at[:, z], out_sem.at[z]) for z in range(n)],
+    )
+
+
+def unpack_kernel(n, zr, jrs, jcs, levels, y_ref, out_ref, rows_vm, tiles_vm, in_sem, out_sem):
+    def work(z):
+        for l in range(levels):
+            for jr in range(jrs):
+                for jc in range(jcs):
+                    tile = tiles_vm[z, jr * jcs + jc, l]
+                    rows_vm[z, l, jr * TR : (jr + 1) * TR, jc * TC : (jc + 1) * TC] = tile
+
+    stream(
+        [copy(y_ref.at[:, z], tiles_vm.at[z], in_sem.at[z]) for z in range(n)],
+        work,
+        [copy(rows_vm.at[z], out_ref.at[0, :, pl.ds(z * zr, zr)], out_sem.at[z]) for z in range(n)],
+    )
 
 
 def store_coded(out, n, values):
@@ -98,22 +123,61 @@
     towards(at_ref, emit)
 
 
-def update_kernel(n, jrs, jcs, g_ref, p_ref, m_ref, np_ref, nm_ref):
-    for jr in range(jrs):
-        rows = slice(jr * TR, (jr + 1) * TR)
-        for jc in range(jcs):
-            j = jr * jcs + jc
-            scale = scale_of(g_ref[j, n])
-            for s in range(n):
-                cols = slice((s * jcs + jc) * TC, (s * jcs + jc + 1) * TC)
-                g = decoded(g_ref[j, s], scale)
-                nm = MOMENTUM_COEF * m_ref[0, rows, cols] + g
-                nm_ref[0, rows, cols] = nm
-                np_ref[0, rows, cols] = p_ref[0, rows, cols] - LEARN_RATE * (g + MOMENTUM_COEF * nm)
-
-
-def reduce_kernel(n, islands, levels, per_level, path_ref, owner_ref, q_ref, x_ref, sum_ref, pick_ref, new, cnt):
-    sum_ref[...] = jnp.zeros_like(sum_ref)
+def update_kernel(n, jcs, at_ref, *refs):
+    parts, (p_ref, m_ref, np_ref, nm_ref) = refs[: 2 * SIDE], refs[2 * SIDE : 2 * SIDE + 4]
+    parts_vm, p_vm, m_vm, np_vm, nm_vm, part_sem, in_sem, out_sem = refs[2 * SIDE + 4 :]
+    core, x, y = place(at_ref)
+    deep = SIDE * TR
+    bands = [pl.ds(pl.multiple_of(lax.rem(y + SIDE - a, SIDE) * deep, deep), deep) for a in range(SIDE)]
+    g_in = [copy(parts[k], parts_vm.at[k], part_sem.at[k]) for k in range(2 * SIDE)]
+    p_in = [copy(p_ref.at[0, bands[a]], p_vm.at[a], in_sem.at[0, a]) for a in range(SIDE)]
+    m_in = [copy(m_ref.at[0, bands[a]], m_vm.at[a], in_sem.at[1, a]) for a in range(SIDE)]
+    p_out = [copy(np_vm.at[a], np_ref.at[0, bands[a]], out_sem.at[0, a]) for a in range(SIDE)]
+    m_out = [copy(nm_vm.at[a], nm_ref.at[0, bands[a]], out_sem.at[1, a]) for a in range(SIDE)]
+    for c in g_in:
+        c.start()
+    for a in range(SIDE):
+        p_in[a].start()
+        m_in[a].start()
+    for c in g_in:
+        c.wait()
+    for a in range(SIDE):
+        p_in[a].wait()
+        m_in[a].wait()
+        for e in range(SIDE):
+            rows = pl.ds(pl.multiple_of(lax.rem(x + SIDE - e, SIDE) * TR, TR), TR)
+            for block, jc in ((parts_vm.at[a, e], core), (parts_vm.at[SIDE + e, a], 1 - core)):
+                scale = scale_of(block[n])
+                for s in range(n):
+                    cols = pl.ds(pl.multiple_of((s * jcs + jc) * TC, TC), TC)
+                    g = decoded(block[s], scale)
+                    nm = MOMENTUM_COEF * m_vm[a, rows, cols] + g
+                    nm_vm[a, rows, cols] = nm
+                    np_vm[a, rows, cols] = p_vm[a, rows, cols] - LEARN_RATE * (g + MOMENTUM_COEF * nm)
+        p_out[a].start()
+        m_out[a].start()
+    for c in p_out + m_out:
+        c.wait()
+
+
+def share_of(count):
+    return jnp.full((TR, TC), 1.0, jnp.float32) / jnp.maximum(count, 1).astype(jnp.float32)
+
+
+CHUNK = 4
+
+
+def reduce_kernel(n, islands, levels, per_level, path_ref, owner_ref, q_ref, x_ref, sum_ref, pick_ref, *scratch):
+    q_vm, x_vm, acc, new, pick_vm, cnt, q_sem, in_sem, out_sem, sum_sem = scratch
+    pieces = [pl.ds(k * CHUNK, CHUNK) for k in range(islands // CHUNK)]
+    ins = [copy(x_ref.at[p], x_vm.at[p], in_sem.at[k]) for k, p in enumerate(pieces)]
+    outs = [copy(pick_vm.at[p], pick_ref.at[p], out_sem.at[k]) for k, p in enumerate(pieces)]
+    q_in = copy(q_ref, q_vm, q_sem)
+    sum_out = copy(acc, sum_ref, sum_sem)
+    for c in ins:
+        c.start()
+    q_in.start()
+    acc[...] = jnp.zeros_like(acc)
     for m in range(levels * per_level):
         cnt[m] = 0
 
@@ -122,41 +186,58 @@
             m = l * per_level + path_ref[i, l]
             cnt[m] = cnt[m] + 1
             for s in range(n):
-                sum_ref[m, s] += x_ref[i, s, l].astype(jnp.float32)
+                acc[m, s] += x_vm[i, s, l].astype(jnp.float32)
         return carry
 
-    lax.fori_loop(0, islands, add, 0)
+    for k, c in enumerate(ins):
+        c.wait()
+        lax.fori_loop(k * CHUNK, (k + 1) * CHUNK, add, 0)
+    sum_out.start()
+    q_in.wait()
 
     def finish(m, carry):
         t = owner_ref[m]
-        share = jnp.full((TR, TC), 1.0, jnp.float32) / jnp.maximum(cnt[m], 1).astype(jnp.float32)
-        scale = scale_of(q_ref[t, n])
+        weight = G_COEF * share_of(cnt[m])
+        scale = scale_of(q_vm[t, n])
         for s in range(n):
-            g = sum_ref[m, s] * share
-            sum_ref[m, s] = g
-            new[m, s] = (decoded(q_ref[t, s], scale) - G_COEF * g).astype(jnp.bfloat16)
+            new[m, s] = (decoded(q_vm[t, s], scale) - acc[m, s] * weight).astype(jnp.bfloat16)
         return carry
 
-    lax.fori_loop(0, levels * per_level, finish, 0)
+    lax.fori_loop(0, levels * per_level, finish, 0, unroll=2)
 
     def pick(i, carry):
         for l in range(levels):
             m = l * per_level + path_ref[i, l]
             for s in range(n):
-                pick_ref[i, s, l] = new[m, s]
+                pick_vm[i, s, l] = new[m, s]
         return carry
 
-    lax.fori_loop(0, islands, pick, 0)
-
-
-def mean_kernel(n, modules, at_ref, owner_ref, sum_ref, *refs):
-    outs, module = refs[: SIDE + 1], refs[SIDE + 1]
-    for m in range(modules):
+    for k, c in enumerate(outs):
+        lax.fori_loop(k * CHUNK, (k + 1) * CHUNK, pick, 0, unroll=2)
+        c.start()
+    for c in outs:
+        c.wait()
+    sum_out.wait()
+
+
+def mean_kernel(n, islands, levels, per_level, at_ref, path_ref, owner_ref, sum_ref, *refs):
+    outs, module, cnt = refs[: SIDE + 1], refs[SIDE + 1], refs[SIDE + 2]
+    for m in range(levels * per_level):
         module[owner_ref[m]] = m
+        cnt[m] = 0
+
+    def add(i, carry):
+        for l in range(levels):
+            m = l * per_level + path_ref[i, l]
+            cnt[m] = cnt[m] + 1
+        return carry
+
+    lax.fori_loop(0, islands, add, 0)
 
     def emit(d, slot, y, x, core):
         m = module[(y * SIDE + x) * CORES + core]
-        store_coded(outs[d].at[slot], n, [sum_ref[m, s] for s in range(n)])
+        share = share_of(cnt[m])
+        store_coded(outs[d].at[slot], n, [sum_ref[m, s] * share for s in range(n)])
 
     towards(at_ref, emit)
 
@@ -216,13 +297,7 @@
     other = along(relay(split_other, [other]), 1, 0)
     same = along(relay(functools.partial(turn, 2), same), 1, 0)
     other = along(relay(functools.partial(turn, 1), other), 0, 1)
-    return call(
-        join_all,
-        jax.ShapeDtypeStruct((islands, *block), dtype),
-        [SMEM] + [VMEM] * (2 * SIDE),
-        VMEM,
-        moved=2 * moved,
-    )(at, *same, *other)
+    return [*same, *other]
 
 
 def body(pseudo_grad, path_table, owner_place, outer_param, outer_momentum):
@@ -241,21 +316,19 @@
         return x.reshape(islands, n, levels, TR, TC)
 
     at = lax.axis_index("island").astype(jnp.int32).reshape(1)
-    row_block = pl.BlockSpec((1, levels, zr, narrow), lambda z: (0, 0, z, 0))
-    z_tiles = pl.BlockSpec((islands, 1, levels, TR, TC), lambda z: (0, z, 0, 0, 0))
+    in_rows = pltpu.VMEM((n, levels, zr, narrow), jnp.bfloat16)
+    in_tiles = pltpu.VMEM((n, islands, levels, TR, TC), jnp.bfloat16)
     packed = call(
-        functools.partial(pack_kernel, jrs, jcs, levels),
+        functools.partial(pack_kernel, n, zr, jrs, jcs, levels),
         tiles(islands, n, levels),
-        [row_block],
-        z_tiles,
-        grid=(n,),
+        [ANY],
+        ANY,
+        (in_rows, in_tiles, DMA((n,)), DMA((n,))),
+        vmem=63,
         moved=4 << 20,
     )(pseudo_grad)
     grads = swap(packed)
 
-    steps = 4
-    band = pl.BlockSpec((1, zr // steps, width), lambda g: (0, g, 0))
-    tile_band = pl.BlockSpec((islands // steps, n + 1, TR, TC), lambda g: (g, 0, 0, 0))
     leaving = [tiles(SIDE, n + 1, dtype=jnp.int16)] * SIDE + [tiles(islands // CORES, n + 1, dtype=jnp.int16)]
     *q, other = call(
         functools.partial(q_kernel, n, jcs),
@@ -264,42 +337,66 @@
         [VMEM] * (SIDE + 1),
         moved=6 << 20,
     )(at, outer_param, outer_momentum)
-    q = exchange(at, q, other)
+    q = call(
+        join_all,
+        tiles(islands, n + 1, dtype=jnp.int16),
+        [SMEM] + [VMEM] * (2 * SIDE),
+        VMEM,
+        moved=4 << 20,
+    )(at, *exchange(at, q, other))
 
     sums, picked = call(
         functools.partial(reduce_kernel, n, islands, levels, per_level),
         [tiles(modules, n, dtype=jnp.float32), tiles(islands, n, levels)],
-        [SMEM] * 2 + [VMEM] * 2,
-        [VMEM] * 2,
-        (pltpu.VMEM((modules, n, TR, TC), jnp.bfloat16), pltpu.SMEM((modules,), jnp.int32)),
+        [SMEM] * 2 + [ANY] * 2,
+        [ANY] * 2,
+        (
+            pltpu.VMEM((islands, n + 1, TR, TC), jnp.int16),
+            pltpu.VMEM((islands, n, levels, TR, TC), jnp.bfloat16),
+            pltpu.VMEM((modules, n, TR, TC), jnp.float32),
+            pltpu.VMEM((modules, n, TR, TC), jnp.bfloat16),
+            pltpu.VMEM((islands, n, levels, TR, TC), jnp.bfloat16),
+            pltpu.SMEM((modules,), jnp.int32),
+            DMA,
+            DMA((islands // CHUNK,)),
+            DMA((islands // CHUNK,)),
+            DMA,
+        ),
+        vmem=63,
         moved=8 << 20,
     )(path_table, owner_place, q, grads)
     arrived = swap(picked)
 
     *mean, other = call(
-        functools.partial(mean_kernel, n, modules),
+        functools.partial(mean_kernel, n, islands, levels, per_level),
         leaving,
-        [SMEM] * 2 + [VMEM],
+        [SMEM] * 3 + [VMEM],
         [VMEM] * (SIDE + 1),
-        (pltpu.SMEM((modules,), jnp.int32),),
+        (pltpu.SMEM((modules,), jnp.int32),) * 2,
         moved=3 << 20,
-    )(at, owner_place, sums)
-    mean = exchange(at, mean, other)
-
+    )(at, path_table, owner_place, sums)
+    bands = pltpu.VMEM((SIDE, SIDE * TR, width), jnp.float32)
     new_param, new_momentum = call(
-        functools.partial(update_kernel, n, jrs // steps, jcs),
+        functools.partial(update_kernel, n, jcs),
         [jax.ShapeDtypeStruct(outer_param.shape, jnp.float32)] * 2,
-        [tile_band, band, band],
-        [band, band],
-        grid=(steps,),
+        [SMEM] + [ANY] * (2 * SIDE + 2),
+        [ANY] * 2,
+        (
+            pltpu.VMEM((2 * SIDE, SIDE, n + 1, TR, TC), jnp.int16),
+            *[bands] * 4,
+            DMA((2 * SIDE,)),
+            DMA((2, SIDE)),
+            DMA((2, SIDE)),
+        ),
         moved=10 << 20,
-    )(mean, outer_param, outer_momentum)
+    )(at, *exchange(at, mean, other), outer_param, outer_momentum)
     returned = call(
-        functools.partial(unpack_kernel, jrs, jcs, levels),
+        functools.partial(unpack_kernel, n, zr, jrs, jcs, levels),
         jax.ShapeDtypeStruct(pseudo_grad.shape, jnp.bfloat16),
-        [z_tiles],
-        row_block,
-        grid=(n,),
+        [ANY],
+        ANY,
+        (in_rows, in_tiles, DMA((n,)), DMA((n,))),
+        vmem=63,
         moved=4 << 20,
     )(arrived)
     return new_param, new_momentum, returned

time: 155 us -> 142 us (0.916); the launches traced: 153 us -> 141 us
  Pallas kernels: 45.9 us -> 16.8 us
  waiting for transfers between devices: 34.1 us -> 58.8 us
  local copies, waits for them, and re-layouts: 9.05 us -> 5.05 us
  starting transfers between devices: 62.7 us -> 59.6 us
    all_to_all x2, waiting for transfers between devices: 6.63 us -> 21.9 us  [swap(): x = lax.all_to_all(x, ('island', 'shard'), 0, 0, tiled=True)]
    pallas_call x6 -> x5, Pallas kernels: 24.5 us -> 11 us  [the longest x1 4.33 us: body(): call(functools.partial(update_kernel, n, jcs), [jax.ShapeDtypeStruct(oute...]
    pallas_call x6, Pallas kernels: 11.8 us -> 0.23 us  [relay(): call(kernel, [line] * SIDE, [SMEM] + [VMEM] * len(parts), [VMEM] * SIDE,...]
    ppermute x26, waiting for transfers between devices: 27.5 us -> 36.8 us  [shift(): return lax.ppermute(v, 'island', pairs)]
    unnamed x59 -> x19, local copies, waits for them, and re-layouts: 9.05 us -> 5.05 us
    ppermute x26, starting transfers between devices: 38.2 us -> 34.9 us  [shift(): return lax.ppermute(v, 'island', pairs)]
    pallas_call x1, Pallas kernels: 3.82 us -> 0.68 us  [body(): call(functools.partial(q_kernel, n, jcs), leaving, [SMEM, VMEM, VMEM], [V...]
  transfers between devices with their start and end apart: 28 -> 28, of which waited for: 13 -> 15; matrix products, arithmetic and copies ran while one was open for 0% -> 0% of each run, Pallas kernels for 19% -> 5%
where the time goes in v3:
time: 142 us; the launch traced here: 141 us
  starting transfers between devices  59.6 us (42%)
  waiting for transfers between devices  58.8 us (41%)
  Pallas kernels  16.8 us (12%)
  local copies, waits for them, and re-layouts  5.05 us (4%)
    ppermute x26, waiting for transfers between devices, shift(): return lax.ppermute(v, 'island', pairs)  36.8 us
    ppermute x26, starting transfers between devices, shift(): return lax.ppermute(v, 'island', pairs)  34.9 us
    all_to_all x2, starting transfers between devices, swap(): x = lax.all_to_all(x, ('island', 'shard'), 0, 0, tiled=True)  24.7 us
    all_to_all x2, waiting for transfers between devices, swap(): x = lax.all_to_all(x, ('island', 'shard'), 0, 0, tiled=True)  21.9 us
    unnamed x19, local copies, waits for them, and re-layouts  5.05 us
    pallas_call x1, Pallas kernels, body(): call(functools.partial(reduce_kernel, n, islands, levels, per_level), [ti...  4.91 us
    pallas_call x1, Pallas kernels, body(): call(functools.partial(update_kernel, n, jcs), [jax.ShapeDtypeStruct(oute...  4.33 us
  transfers between devices with their start and end apart: 28, of which 15 were waited for; matrix products, arithmetic and copies ran while one was open for 0% of the time, Pallas kernels for 5%

profile of v3, /device:TPU:1, one launch (start us, length us, event | category | flops | bytes accessed | tf_op | source)
XLA Modules:
  0.0 141.2 jit_solution(12639653598595554365)
XLA Ops:
  0.6 2.4 %shard_map.81 = bf16[32,8,2,16,128]{4,3,2,1,0:T(8,128)(2,1)} custom-call(bf16[1,2,2048,256]{3,2,1,0:T(8,128)(2,1)} %x_ref.1), custom_call_target="tpu_custom_call" | custom-call | flops 4194304 | bytes 4194304 | tf_op jit(solution)/shard_map/pallas_call | solution.py:321
  3.1 16.7 %all-to-all-start = ((bf16[256,2,16,128]{3,2,1,0:T(8,128)(2,1)}), bf16[256,2,16,128]{3,2,1,0:T(8,128)(2,1)}, u32[]{:S(2)}, u32[]{:S(2)}) async-start(bf16[256,2,16,128]{3,2,1,0:T(8,128)(2,1)} %bitcast.5), calls=%async_computation | async-start | bytes 4194304 | tf_op jit(solution)/shard_map/all_to_all | solution.py:315
  19.8 1.6 %copy-done.2 = f32[1,256,2048]{2,1,0:T(8,128)S(1)} copy-done((f32[1,256,2048]{2,1,0:T(8,128)S(1)}, f32[1,256,2048]{2,1,0:T(8,128)}, u32[]{:S(2)}) %copy-start.2) | copy-done | bytes 2097176
  22.1 2.3 %collective-permute-start.6 = (s16[16,9,16,128]{3,2,1,0:T(8,128)(2,1)S(1)}, s16[16,9,16,128]{3,2,1,0:T(8,128)(2,1)S(1)}, u32[]{:S(2)}, u32[]{:S(2)}) collective-permute-start(s16[16,9,16,128]{3,2,1,0:T(8,128)(2,1)S(1)} %get-tuple-element.49), channel_id=1, source_target_pairs={{0,8},{8,0},{16,24},{24,16},{32,40},{40,32},{48,56},{56,48},{64,72... | collective-permute-start | bytes 1769480 | tf_op jit(solution)/shard_map/ppermute | solution.py:284
  24.4 1.9 %collective-permute-start.1 = (s16[4,9,16,128]{3,2,1,0:T(8,128)(2,1)S(1)}, s16[4,9,16,128]{3,2,1,0:T(8,128)(2,1)S(1)}, u32[]{:S(2)}, u32[]{:S(2)}) collective-permute-start(s16[4,9,16,128]{3,2,1,0:T(8,128)(2,1)S(1)} %get-tuple-element.43), channel_id=1, source_target_pairs={{0,32},{8,40},{16,48},{24,56},{32,0},{40,8},{48,16},{56,24},{64,96... | collective-permute-start | bytes 442376 | tf_op jit(solution)/shard_map/ppermute | solution.py:284
  27.5 1.3 collective-permute-start.7
  28.8 2.5 %collective-permute-start.8 = (s16[4,9,16,128]{3,2,1,0:T(8,128)(2,1)S(1)}, s16[4,9,16,128]{3,2,1,0:T(8,128)(2,1)S(1)}, u32[]{:S(2)}, u32[]{:S(2)}) collective-permute-start(s16[4,9,16,128]{3,2,1,0:T(8,128)(2,1)S(1)} %get-tuple-element.52), channel_id=1, source_target_pairs={{0,128},{8,136},{16,144},{24,152},{32,160},{40,168},{48,176},{56,1... | collective-permute-start | bytes 442376 | tf_op jit(solution)/shard_map/ppermute | solution.py:284
  31.3 2.1 %collective-permute-done.refs_1_ = s16[4,9,16,128]{3,2,1,0:T(8,128)(2,1)S(1)} collective-permute-done((s16[4,9,16,128]{3,2,1,0:T(8,128)(2,1)S(1)}, s16[4,9,16,128]{3,2,1,0:T(8,128)(2,1)S(1)}, u32[]{:S(2)}, u32[]{:S(2)}) %collective-permute-start) | collective-permute-done | bytes 147488 | tf_op jit(solution)/shard_map/ppermute | solution.py:284
  34.2 4.7 %collective-permute-done.1.refs_2_ = s16[4,9,16,128]{3,2,1,0:T(8,128)(2,1)S(1)} collective-permute-done((s16[4,9,16,128]{3,2,1,0:T(8,128)(2,1)S(1)}, s16[4,9,16,128]{3,2,1,0:T(8,128)(2,1)S(1)}, u32[]{:S(2)}, u32[]{:S(2)}) %collective-permute-start.1) | collective-permute-done | bytes 147488 | tf_op jit(solution)/shard_map/ppermute | solution.py:284
  40.1 2.6 %collective-permute-start.4 = (s16[4,9,16,128]{3,2,1,0:T(8,128)(2,1)S(1)}, s16[4,9,16,128]{3,2,1,0:T(8,128)(2,1)S(1)}, u32[]{:S(2)}, u32[]{:S(2)}) collective-permute-start(s16[4,9,16,128]{3,2,1,0:T(8,128)(2,1)S(1)} %get-tuple-element.47), channel_id=1, source_target_pairs={{0,128},{8,136},{16,144},{24,152},{32,160},{40,168},{48,176},{56,1... | collective-permute-start | bytes 442376 | tf_op jit(solution)/shard_map/ppermute | solution.py:284
  44.5 3.1 %collective-permute-start.11 = (s16[4,9,16,128]{3,2,1,0:T(8,128)(2,1)S(1)}, s16[4,9,16,128]{3,2,1,0:T(8,128)(2,1)S(1)}, u32[]{:S(2)}, u32[]{:S(2)}) collective-permute-start(s16[4,9,16,128]{3,2,1,0:T(8,128)(2,1)S(1)} %get-tuple-element.56), channel_id=1, source_target_pairs={{0,32},{8,40},{16,48},{24,56},{32,0},{40,8},{48,16},{56,24},{64,96... | collective-permute-start | bytes 442376 | tf_op jit(solution)/shard_map/ppermute | solution.py:284
  48.6 2.4 %collective-permute-start.12 = (s16[4,9,16,128]{3,2,1,0:T(8,128)(2,1)S(1)}, s16[4,9,16,128]{3,2,1,0:T(8,128)(2,1)S(1)}, u32[]{:S(2)}, u32[]{:S(2)}) collective-permute-start(s16[4,9,16,128]{3,2,1,0:T(8,128)(2,1)S(1)} %get-tuple-element.57), channel_id=1, source_target_pairs={{0,48},{8,56},{16,0},{24,8},{32,16},{40,24},{48,32},{56,40},{64,11... | collective-permute-start | bytes 442376 | tf_op jit(solution)/shard_map/ppermute | solution.py:284
  51.7 3.6 %collective-permute-done.4.refs_2_ = s16[4,9,16,128]{3,2,1,0:T(8,128)(2,1)S(1)} collective-permute-done((s16[4,9,16,128]{3,2,1,0:T(8,128)(2,1)S(1)}, s16[4,9,16,128]{3,2,1,0:T(8,128)(2,1)S(1)}, u32[]{:S(2)}, u32[]{:S(2)}) %collective-permute-start.4) | collective-permute-done | bytes 147488 | tf_op jit(solution)/shard_map/ppermute | solution.py:284
  55.3 3.2 %collective-permute-done.11.refs_6_ = s16[4,9,16,128]{3,2,1,0:T(8,128)(2,1)S(1)} collective-permute-done((s16[4,9,16,128]{3,2,1,0:T(8,128)(2,1)S(1)}, s16[4,9,16,128]{3,2,1,0:T(8,128)(2,1)S(1)}, u32[]{:S(2)}, u32[]{:S(2)}) %collective-permute-start.11) | collective-permute-done | bytes 147488 | tf_op jit(solution)/shard_map/ppermute | solution.py:284
  59.7 13.0 %all-to-all-done = bf16[256,2,16,128]{3,2,1,0:T(8,128)(2,1)} async-done(((bf16[256,2,16,128]{3,2,1,0:T(8,128)(2,1)}), bf16[256,2,16,128]{3,2,1,0:T(8,128)(2,1)}, u32[]{:S(2)}, u32[]{:S(2)}) %all-to-all-start) | async-done | bytes 2097184 | tf_op jit(solution)/shard_map/all_to_all | solution.py:315
  72.6 4.9 %shard_map.82 = (f32[32,8,16,128]{3,2,1,0:T(8,128)}, bf16[32,8,2,16,128]{4,3,2,1,0:T(8,128)(2,1)}) custom-call(s32[32,2]{1,0:T(8,128)} %copy.9.path_ref, s32[32]{0:T(128)} %owner_ref.3, s16[32,9,16,128]{3,2,1,0:T(8,128)(2,1)} %copy-done.4, bf16[32,8,2,16,128]{4,3,2,1,0:T(8,128)(2,1)} %bitcast.2.x_ref), custom_call_target="tpu_custom_call" | custom-call | flops 8388608 | bytes 8388608 | tf_op jit(solution)/shard_map/pallas_call | solution.py:348
  77.6 8.0 %all-to-all-start.1 = ((bf16[256,2,16,128]{3,2,1,0:T(8,128)(2,1)}), bf16[256,2,16,128]{3,2,1,0:T(8,128)(2,1)}, u32[]{:S(2)}, u32[]{:S(2)}) async-start(bf16[256,2,16,128]{3,2,1,0:T(8,128)(2,1)} %bitcast.6), calls=%async_computation.1 | async-start | bytes 4194304 | tf_op jit(solution)/shard_map/all_to_all | solution.py:315
  85.7 1.7 %copy-done.5 = f32[32,8,16,128]{3,2,1,0:T(8,128)S(1)} copy-done((f32[32,8,16,128]{3,2,1,0:T(8,128)S(1)}, f32[32,8,16,128]{3,2,1,0:T(8,128)}, u32[]{:S(2)}) %copy-start.5) | copy-done | bytes 2097176
  87.4 1.7 %shard_map.83 = (s16[4,9,16,128]{3,2,1,0:T(8,128)(2,1)S(1)}, s16[4,9,16,128]{3,2,1,0:T(8,128)(2,1)S(1)}, s16[4,9,16,128]{3,2,1,0:T(8,128)(2,1)S(1)}, s16[4,9,16,...) custom-call(s32[1]{0:T(128)} %bitcast.at_ref, s32[32,2]{1,0:T(8,128)S(1)} %copy-done.6, s32[32]{0:T(128)S(1)} %copy-done.7, ...), custom_call_target="tpu_custom_call" | custom-call | flops 3145728 | bytes 3145728 | tf_op jit(solution)/shard_map/pallas_call | solution.py:370
  89.1 2.4 %collective-permute-start.19 = (s16[16,9,16,128]{3,2,1,0:T(8,128)(2,1)S(1)}, s16[16,9,16,128]{3,2,1,0:T(8,128)(2,1)S(1)}, u32[]{:S(2)}, u32[]{:S(2)}) collective-permute-start(s16[16,9,16,128]{3,2,1,0:T(8,128)(2,1)S(1)} %get-tuple-element.67), channel_id=1, source_target_pairs={{0,8},{8,0},{16,24},{24,16},{32,40},{40,32},{48,56},{56,48},{64,72... | collective-permute-start | bytes 1769480 | tf_op jit(solution)/shard_map/ppermute | solution.py:284
  91.5 1.8 %collective-permute-start.14 = (s16[4,9,16,128]{3,2,1,0:T(8,128)(2,1)S(1)}, s16[4,9,16,128]{3,2,1,0:T(8,128)(2,1)S(1)}, u32[]{:S(2)}, u32[]{:S(2)}) collective-permute-start(s16[4,9,16,128]{3,2,1,0:T(8,128)(2,1)S(1)} %get-tuple-element.61), channel_id=1, source_target_pairs={{0,32},{8,40},{16,48},{24,56},{32,0},{40,8},{48,16},{56,24},{64,96... | collective-permute-start | bytes 442376 | tf_op jit(solution)/shard_map/ppermute | solution.py:284
  94.6 1.3 collective-permute-start.20
  95.9 2.5 %collective-permute-start.21 = (s16[4,9,16,128]{3,2,1,0:T(8,128)(2,1)S(1)}, s16[4,9,16,128]{3,2,1,0:T(8,128)(2,1)S(1)}, u32[]{:S(2)}, u32[]{:S(2)}) collective-permute-start(s16[4,9,16,128]{3,2,1,0:T(8,128)(2,1)S(1)} %get-tuple-element.70), channel_id=1, source_target_pairs={{0,128},{8,136},{16,144},{24,152},{32,160},{40,168},{48,176},{56,1... | collective-permute-start | bytes 442376 | tf_op jit(solution)/shard_map/ppermute | solution.py:284
  98.4 7.5 %collective-permute-done.13.refs_1_ = s16[4,9,16,128]{3,2,1,0:T(8,128)(2,1)S(1)} collective-permute-done((s16[4,9,16,128]{3,2,1,0:T(8,128)(2,1)S(1)}, s16[4,9,16,128]{3,2,1,0:T(8,128)(2,1)S(1)}, u32[]{:S(2)}, u32[]{:S(2)}) %collective-permute-start.13) | collective-permute-done | bytes 147488 | tf_op jit(solution)/shard_map/ppermute | solution.py:284
  107.5 1.5 %collective-permute-start.17 = (s16[4,9,16,128]{3,2,1,0:T(8,128)(2,1)S(1)}, s16[4,9,16,128]{3,2,1,0:T(8,128)(2,1)S(1)}, u32[]{:S(2)}, u32[]{:S(2)}) collective-permute-start(s16[4,9,16,128]{3,2,1,0:T(8,128)(2,1)S(1)} %get-tuple-element.65), channel_id=1, source_target_pairs={{0,128},{8,136},{16,144},{24,152},{32,160},{40,168},{48,176},{56,1... | collective-permute-start | bytes 442376 | tf_op jit(solution)/shard_map/ppermute | solution.py:284
  110.1 3.2 %collective-permute-done.22.refs_3_ = s16[4,9,16,128]{3,2,1,0:T(8,128)(2,1)S(1)} collective-permute-done((s16[4,9,16,128]{3,2,1,0:T(8,128)(2,1)S(1)}, s16[4,9,16,128]{3,2,1,0:T(8,128)(2,1)S(1)}, u32[]{:S(2)}, u32[]{:S(2)}) %collective-permute-start.22) | collective-permute-done | bytes 147488 | tf_op jit(solution)/shard_map/ppermute | solution.py:284
  114.3 2.1 %collective-permute-done.16.refs_1_ = s16[4,9,16,128]{3,2,1,0:T(8,128)(2,1)S(1)} collective-permute-done((s16[4,9,16,128]{3,2,1,0:T(8,128)(2,1)S(1)}, s16[4,9,16,128]{3,2,1,0:T(8,128)(2,1)S(1)}, u32[]{:S(2)}, u32[]{:S(2)}) %collective-permute-start.16) | collective-permute-done | bytes 147488 | tf_op jit(solution)/shard_map/ppermute | solution.py:284
  116.9 5.5 %collective-permute-done.17.refs_2_ = s16[4,9,16,128]{3,2,1,0:T(8,128)(2,1)S(1)} collective-permute-done((s16[4,9,16,128]{3,2,1,0:T(8,128)(2,1)S(1)}, s16[4,9,16,128]{3,2,1,0:T(8,128)(2,1)S(1)}, u32[]{:S(2)}, u32[]{:S(2)}) %collective-permute-start.17) | collective-permute-done | bytes 147488 | tf_op jit(solution)/shard_map/ppermute | solution.py:284
  122.4 1.8 %collective-permute-done.18.refs_3_ = s16[4,9,16,128]{3,2,1,0:T(8,128)(2,1)S(1)} collective-permute-done((s16[4,9,16,128]{3,2,1,0:T(8,128)(2,1)S(1)}, s16[4,9,16,128]{3,2,1,0:T(8,128)(2,1)S(1)}, u32[]{:S(2)}, u32[]{:S(2)}) %collective-permute-start.18) | collective-permute-done | bytes 147488 | tf_op jit(solution)/shard_map/ppermute | solution.py:284
  125.3 4.3 %shard_map.87 = (f32[1,256,2048]{2,1,0:T(8,128)}, f32[1,256,2048]{2,1,0:T(8,128)}) custom-call(s32[1]{0:T(128)} %bitcast.at_ref, s16[4,9,16,128]{3,2,1,0:T(8,128)(2,1)S(1)} %get-tuple-element.63.refs_0_, s16[4,9,16,128]{3,2,1,0:T(8,128)(2,1)S(1)} %collective-permute-done.16.refs_1_, s16[4,9,16,128]{3,2,1,0:T(8,128)(2,1)S(1)} %collective-permute-done.17.refs_2_, ...), custom_call_target="tpu_custom_call" | custom-call | flops 10485760 | bytes 10485760 | tf_op jit(solution)/shard_map/pallas_call | solution.py:379
  129.7 9.0 %all-to-all-done.1 = bf16[256,2,16,128]{3,2,1,0:T(8,128)(2,1)} async-done(((bf16[256,2,16,128]{3,2,1,0:T(8,128)(2,1)}), bf16[256,2,16,128]{3,2,1,0:T(8,128)(2,1)}, u32[]{:S(2)}, u32[]{:S(2)}) %all-to-all-start.1) | async-done | bytes 2097184 | tf_op jit(solution)/shard_map/all_to_all | solution.py:315
  138.6 2.4 %shard_map.88 = bf16[1,2,2048,256]{3,2,1,0:T(8,128)(2,1)} custom-call(bf16[32,8,2,16,128]{4,3,2,1,0:T(8,128)(2,1)} %bitcast.4.y_ref), custom_call_target="tpu_custom_call" | custom-call | flops 4194304 | bytes 4194304 | tf_op jit(solution)/shard_map/pallas_call | solution.py:393
  (56 shorter events, 15.2 us)
Async XLA Ops:
  3.1 16.7 %copy-start = (f32[1,256,2048]{2,1,0:T(8,128)S(1)}, f32[1,256,2048]{2,1,0:T(8,128)}, u32[]{:S(2)}) copy-start(f32[1,256,2048]{2,1,0:T(8,128)} %refs_8_.1) | copy-start | bytes 6291460
  3.1 69.5 %all-to-all-start = ((bf16[256,2,16,128]{3,2,1,0:T(8,128)(2,1)}), bf16[256,2,16,128]{3,2,1,0:T(8,128)(2,1)}, u32[]{:S(2)}, u32[]{:S(2)}) async-start(bf16[256,2,16,128]{3,2,1,0:T(8,128)(2,1)} %bitcast.5), calls=%async_computation | async-start | bytes 4194304 | tf_op jit(solution)/shard_map/all_to_all | solution.py:315
  21.4 29.7 %copy-start.8 = (s32[32,2]{0,1:T(2,128)S(1)}, s32[32,2]{0,1:T(2,128)}, u32[]{:S(2)}) copy-start(s32[32,2]{0,1:T(2,128)} %param.6) | copy-start | bytes 772
  22.1 5.4 %collective-permute-start.6 = (s16[16,9,16,128]{3,2,1,0:T(8,128)(2,1)S(1)}, s16[16,9,16,128]{3,2,1,0:T(8,128)(2,1)S(1)}, u32[]{:S(2)}, u32[]{:S(2)}) collective-permute-start(s16[16,9,16,128]{3,2,1,0:T(8,128)(2,1)S(1)} %get-tuple-element.49), channel_id=1, source_target_pairs={{0,8},{8,0},{16,24},{24,16},{32,40},{40,32},{48,56},{56,48},{64,72... | collective-permute-start | bytes 1769480 | tf_op jit(solution)/shard_map/ppermute | solution.py:284
  24.4 9.0 %collective-permute-start = (s16[4,9,16,128]{3,2,1,0:T(8,128)(2,1)S(1)}, s16[4,9,16,128]{3,2,1,0:T(8,128)(2,1)S(1)}, u32[]{:S(2)}, u32[]{:S(2)}) collective-permute-start(s16[4,9,16,128]{3,2,1,0:T(8,128)(2,1)S(1)} %get-tuple-element.42), channel_id=1, source_target_pairs={{0,16},{8,24},{16,32},{24,40},{32,48},{40,56},{48,0},{56,8},{64,80... | collective-permute-start | bytes 442376 | tf_op jit(solution)/shard_map/ppermute | solution.py:284
  24.4 14.5 %collective-permute-start.1 = (s16[4,9,16,128]{3,2,1,0:T(8,128)(2,1)S(1)}, s16[4,9,16,128]{3,2,1,0:T(8,128)(2,1)S(1)}, u32[]{:S(2)}, u32[]{:S(2)}) collective-permute-start(s16[4,9,16,128]{3,2,1,0:T(8,128)(2,1)S(1)} %get-tuple-element.43), channel_id=1, source_target_pairs={{0,32},{8,40},{16,48},{24,56},{32,0},{40,8},{48,16},{56,24},{64,96... | collective-permute-start | bytes 442376 | tf_op jit(solution)/shard_map/ppermute | solution.py:284
  26.3 12.7 %collective-permute-start.2 = (s16[4,9,16,128]{3,2,1,0:T(8,128)(2,1)S(1)}, s16[4,9,16,128]{3,2,1,0:T(8,128)(2,1)S(1)}, u32[]{:S(2)}, u32[]{:S(2)}) collective-permute-start(s16[4,9,16,128]{3,2,1,0:T(8,128)(2,1)S(1)} %get-tuple-element.44), channel_id=1, source_target_pairs={{0,48},{8,56},{16,0},{24,8},{32,16},{40,24},{48,32},{56,40},{64,11... | collective-permute-start | bytes 442376 | tf_op jit(solution)/shard_map/ppermute | solution.py:284
  27.5 15.2 %collective-permute-start.7 = (s16[4,9,16,128]{3,2,1,0:T(8,128)(2,1)S(1)}, s16[4,9,16,128]{3,2,1,0:T(8,128)(2,1)S(1)}, u32[]{:S(2)}, u32[]{:S(2)}) collective-permute-start(s16[4,9,16,128]{3,2,1,0:T(8,128)(2,1)S(1)} %get-tuple-element.51), channel_id=1, source_target_pairs={{0,64},{8,72},{16,80},{24,88},{32,96},{40,104},{48,112},{56,120},{... | collective-permute-start | bytes 442376 | tf_op jit(solution)/shard_map/ppermute | solution.py:284
  28.8 15.1 %collective-permute-start.8 = (s16[4,9,16,128]{3,2,1,0:T(8,128)(2,1)S(1)}, s16[4,9,16,128]{3,2,1,0:T(8,128)(2,1)S(1)}, u32[]{:S(2)}, u32[]{:S(2)}) collective-permute-start(s16[4,9,16,128]{3,2,1,0:T(8,128)(2,1)S(1)} %get-tuple-element.52), channel_id=1, source_target_pairs={{0,128},{8,136},{16,144},{24,152},{32,160},{40,168},{48,176},{56,1... | collective-permute-start | bytes 442376 | tf_op jit(solution)/shard_map/ppermute | solution.py:284
  33.4 10.5 %collective-permute-start.9 = (s16[4,9,16,128]{3,2,1,0:T(8,128)(2,1)S(1)}, s16[4,9,16,128]{3,2,1,0:T(8,128)(2,1)S(1)}, u32[]{:S(2)}, u32[]{:S(2)}) collective-permute-start(s16[4,9,16,128]{3,2,1,0:T(8,128)(2,1)S(1)} %get-tuple-element.53), channel_id=1, source_target_pairs={{0,192},{8,200},{16,208},{24,216},{32,224},{40,232},{48,240},{56,2... | collective-permute-start | bytes 442376 | tf_op jit(solution)/shard_map/ppermute | solution.py:284
  39.0 9.6 %collective-permute-start.3 = (s16[4,9,16,128]{3,2,1,0:T(8,128)(2,1)S(1)}, s16[4,9,16,128]{3,2,1,0:T(8,128)(2,1)S(1)}, u32[]{:S(2)}, u32[]{:S(2)}) collective-permute-start(s16[4,9,16,128]{3,2,1,0:T(8,128)(2,1)S(1)} %get-tuple-element.46), channel_id=1, source_target_pairs={{0,64},{8,72},{16,80},{24,88},{32,96},{40,104},{48,112},{56,120},{... | collective-permute-start | bytes 442376 | tf_op jit(solution)/shard_map/ppermute | solution.py:284
  40.1 15.2 %collective-permute-start.4 = (s16[4,9,16,128]{3,2,1,0:T(8,128)(2,1)S(1)}, s16[4,9,16,128]{3,2,1,0:T(8,128)(2,1)S(1)}, u32[]{:S(2)}, u32[]{:S(2)}) collective-permute-start(s16[4,9,16,128]{3,2,1,0:T(8,128)(2,1)S(1)} %get-tuple-element.47), channel_id=1, source_target_pairs={{0,128},{8,136},{16,144},{24,152},{32,160},{40,168},{48,176},{56,1... | collective-permute-start | bytes 442376 | tf_op jit(solution)/shard_map/ppermute | solution.py:284
  42.8 12.6 %collective-permute-start.5 = (s16[4,9,16,128]{3,2,1,0:T(8,128)(2,1)S(1)}, s16[4,9,16,128]{3,2,1,0:T(8,128)(2,1)S(1)}, u32[]{:S(2)}, u32[]{:S(2)}) collective-permute-start(s16[4,9,16,128]{3,2,1,0:T(8,128)(2,1)S(1)} %get-tuple-element.48), channel_id=1, source_target_pairs={{0,192},{8,200},{16,208},{24,216},{32,224},{40,232},{48,240},{56,2... | collective-permute-start | bytes 442376 | tf_op jit(solution)/shard_map/ppermute | solution.py:284
  43.9 11.4 %collective-permute-start.10 = (s16[4,9,16,128]{3,2,1,0:T(8,128)(2,1)S(1)}, s16[4,9,16,128]{3,2,1,0:T(8,128)(2,1)S(1)}, u32[]{:S(2)}, u32[]{:S(2)}) collective-permute-start(s16[4,9,16,128]{3,2,1,0:T(8,128)(2,1)S(1)} %get-tuple-element.55), channel_id=1, source_target_pairs={{0,16},{8,24},{16,32},{24,40},{32,48},{40,56},{48,0},{56,8},{64,80... | collective-permute-start | bytes 442376 | tf_op jit(solution)/shard_map/ppermute | solution.py:284
  44.5 14.1 %collective-permute-start.11 = (s16[4,9,16,128]{3,2,1,0:T(8,128)(2,1)S(1)}, s16[4,9,16,128]{3,2,1,0:T(8,128)(2,1)S(1)}, u32[]{:S(2)}, u32[]{:S(2)}) collective-permute-start(s16[4,9,16,128]{3,2,1,0:T(8,128)(2,1)S(1)} %get-tuple-element.56), channel_id=1, source_target_pairs={{0,32},{8,40},{16,48},{24,56},{32,0},{40,8},{48,16},{56,24},{64,96... | collective-permute-start | bytes 442376 | tf_op jit(solution)/shard_map/ppermute | solution.py:284
  48.6 9.9 %collective-permute-start.12 = (s16[4,9,16,128]{3,2,1,0:T(8,128)(2,1)S(1)}, s16[4,9,16,128]{3,2,1,0:T(8,128)(2,1)S(1)}, u32[]{:S(2)}, u32[]{:S(2)}) collective-permute-start(s16[4,9,16,128]{3,2,1,0:T(8,128)(2,1)S(1)} %get-tuple-element.57), channel_id=1, source_target_pairs={{0,48},{8,56},{16,0},{24,8},{32,16},{40,24},{48,32},{56,40},{64,11... | collective-permute-start | bytes 442376 | tf_op jit(solution)/shard_map/ppermute | solution.py:284
  77.6 47.8 %copy-start.3 = (f32[1,256,2048]{2,1,0:T(8,128)S(1)}, f32[1,256,2048]{2,1,0:T(8,128)}, u32[]{:S(2)}) copy-start(f32[1,256,2048]{2,1,0:T(8,128)} %refs_9_.1) | copy-start | bytes 6291460
  77.6 61.0 %all-to-all-start.1 = ((bf16[256,2,16,128]{3,2,1,0:T(8,128)(2,1)}), bf16[256,2,16,128]{3,2,1,0:T(8,128)(2,1)}, u32[]{:S(2)}, u32[]{:S(2)}) async-start(bf16[256,2,16,128]{3,2,1,0:T(8,128)(2,1)} %bitcast.6), calls=%async_computation.1 | async-start | bytes 4194304 | tf_op jit(solution)/shard_map/all_to_all | solution.py:315
  85.6 39.7 %copy-start.1 = (f32[1,256,2048]{2,1,0:T(8,128)S(1)}, f32[1,256,2048]{2,1,0:T(8,128)}, u32[]{:S(2)}) copy-start(f32[1,256,2048]{2,1,0:T(8,128)} %refs_8_.1) | copy-start | bytes 6291460
  89.1 5.4 %collective-permute-start.19 = (s16[16,9,16,128]{3,2,1,0:T(8,128)(2,1)S(1)}, s16[16,9,16,128]{3,2,1,0:T(8,128)(2,1)S(1)}, u32[]{:S(2)}, u32[]{:S(2)}) collective-permute-start(s16[16,9,16,128]{3,2,1,0:T(8,128)(2,1)S(1)} %get-tuple-element.67), channel_id=1, source_target_pairs={{0,8},{8,0},{16,24},{24,16},{32,40},{40,32},{48,56},{56,48},{64,72... | collective-permute-start | bytes 1769480 | tf_op jit(solution)/shard_map/ppermute | solution.py:284
  91.5 14.4 %collective-permute-start.13 = (s16[4,9,16,128]{3,2,1,0:T(8,128)(2,1)S(1)}, s16[4,9,16,128]{3,2,1,0:T(8,128)(2,1)S(1)}, u32[]{:S(2)}, u32[]{:S(2)}) collective-permute-start(s16[4,9,16,128]{3,2,1,0:T(8,128)(2,1)S(1)} %get-tuple-element.60), channel_id=1, source_target_pairs={{0,16},{8,24},{16,32},{24,40},{32,48},{40,56},{48,0},{56,8},{64,80... | collective-permute-start | bytes 442376 | tf_op jit(solution)/shard_map/ppermute | solution.py:284
  91.5 14.4 %collective-permute-start.14 = (s16[4,9,16,128]{3,2,1,0:T(8,128)(2,1)S(1)}, s16[4,9,16,128]{3,2,1,0:T(8,128)(2,1)S(1)}, u32[]{:S(2)}, u32[]{:S(2)}) collective-permute-start(s16[4,9,16,128]{3,2,1,0:T(8,128)(2,1)S(1)} %get-tuple-element.61), channel_id=1, source_target_pairs={{0,32},{8,40},{16,48},{24,56},{32,0},{40,8},{48,16},{56,24},{64,96... | collective-permute-start | bytes 442376 | tf_op jit(solution)/shard_map/ppermute | solution.py:284
  93.4 13.4 %collective-permute-start.15 = (s16[4,9,16,128]{3,2,1,0:T(8,128)(2,1)S(1)}, s16[4,9,16,128]{3,2,1,0:T(8,128)(2,1)S(1)}, u32[]{:S(2)}, u32[]{:S(2)}) collective-permute-start(s16[4,9,16,128]{3,2,1,0:T(8,128)(2,1)S(1)} %get-tuple-element.62), channel_id=1, source_target_pairs={{0,48},{8,56},{16,0},{24,8},{32,16},{40,24},{48,32},{56,40},{64,11... | collective-permute-start | bytes 442376 | tf_op jit(solution)/shard_map/ppermute | solution.py:284
  94.6 14.4 %collective-permute-start.20 = (s16[4,9,16,128]{3,2,1,0:T(8,128)(2,1)S(1)}, s16[4,9,16,128]{3,2,1,0:T(8,128)(2,1)S(1)}, u32[]{:S(2)}, u32[]{:S(2)}) collective-permute-start(s16[4,9,16,128]{3,2,1,0:T(8,128)(2,1)S(1)} %get-tuple-element.69), channel_id=1, source_target_pairs={{0,64},{8,72},{16,80},{24,88},{32,96},{40,104},{48,112},{56,120},{... | collective-permute-start | bytes 442376 | tf_op jit(solution)/shard_map/ppermute | solution.py:284
  95.9 14.2 %collective-permute-start.21 = (s16[4,9,16,128]{3,2,1,0:T(8,128)(2,1)S(1)}, s16[4,9,16,128]{3,2,1,0:T(8,128)(2,1)S(1)}, u32[]{:S(2)}, u32[]{:S(2)}) collective-permute-start(s16[4,9,16,128]{3,2,1,0:T(8,128)(2,1)S(1)} %get-tuple-element.70), channel_id=1, source_target_pairs={{0,128},{8,136},{16,144},{24,152},{32,160},{40,168},{48,176},{56,1... | collective-permute-start | bytes 442376 | tf_op jit(solution)/shard_map/ppermute | solution.py:284
  105.9 7.3 %collective-permute-start.22 = (s16[4,9,16,128]{3,2,1,0:T(8,128)(2,1)S(1)}, s16[4,9,16,128]{3,2,1,0:T(8,128)(2,1)S(1)}, u32[]{:S(2)}, u32[]{:S(2)}) collective-permute-start(s16[4,9,16,128]{3,2,1,0:T(8,128)(2,1)S(1)} %get-tuple-element.71), channel_id=1, source_target_pairs={{0,192},{8,200},{16,208},{24,216},{32,224},{40,232},{48,240},{56,2... | collective-permute-start | bytes 442376 | tf_op jit(solution)/shard_map/ppermute | solution.py:284
  106.8 9.6 %collective-permute-start.16 = (s16[4,9,16,128]{3,2,1,0:T(8,128)(2,1)S(1)}, s16[4,9,16,128]{3,2,1,0:T(8,128)(2,1)S(1)}, u32[]{:S(2)}, u32[]{:S(2)}) collective-permute-start(s16[4,9,16,128]{3,2,1,0:T(8,128)(2,1)S(1)} %get-tuple-element.64), channel_id=1, source_target_pairs={{0,64},{8,72},{16,80},{24,88},{32,96},{40,104},{48,112},{56,120},{... | collective-permute-start | bytes 442376 | tf_op jit(solution)/shard_map/ppermute | solution.py:284
  107.5 14.9 %collective-permute-start.17 = (s16[4,9,16,128]{3,2,1,0:T(8,128)(2,1)S(1)}, s16[4,9,16,128]{3,2,1,0:T(8,128)(2,1)S(1)}, u32[]{:S(2)}, u32[]{:S(2)}) collective-permute-start(s16[4,9,16,128]{3,2,1,0:T(8,128)(2,1)S(1)} %get-tuple-element.65), channel_id=1, source_target_pairs={{0,128},{8,136},{16,144},{24,152},{32,160},{40,168},{48,176},{56,1... | collective-permute-start | bytes 442376 | tf_op jit(solution)/shard_map/ppermute | solution.py:284
  109.0 15.2 %collective-permute-start.18 = (s16[4,9,16,128]{3,2,1,0:T(8,128)(2,1)S(1)}, s16[4,9,16,128]{3,2,1,0:T(8,128)(2,1)S(1)}, u32[]{:S(2)}, u32[]{:S(2)}) collective-permute-start(s16[4,9,16,128]{3,2,1,0:T(8,128)(2,1)S(1)} %get-tuple-element.66), channel_id=1, source_target_pairs={{0,192},{8,200},{16,208},{24,216},{32,224},{40,232},{48,240},{56,2... | collective-permute-start | bytes 442376 | tf_op jit(solution)/shard_map/ppermute | solution.py:284
  113.3 10.9 %collective-permute-start.23 = (s16[4,9,16,128]{3,2,1,0:T(8,128)(2,1)S(1)}, s16[4,9,16,128]{3,2,1,0:T(8,128)(2,1)S(1)}, u32[]{:S(2)}, u32[]{:S(2)}) collective-permute-start(s16[4,9,16,128]{3,2,1,0:T(8,128)(2,1)S(1)} %get-tuple-element.73), channel_id=1, source_target_pairs={{0,16},{8,24},{16,32},{24,40},{32,48},{40,56},{48,0},{56,8},{64,80... | collective-permute-start | bytes 442376 | tf_op jit(solution)/shard_map/ppermute | solution.py:284
  113.4 11.9 %collective-permute-start.24 = (s16[4,9,16,128]{3,2,1,0:T(8,128)(2,1)S(1)}, s16[4,9,16,128]{3,2,1,0:T(8,128)(2,1)S(1)}, u32[]{:S(2)}, u32[]{:S(2)}) collective-permute-start(s16[4,9,16,128]{3,2,1,0:T(8,128)(2,1)S(1)} %get-tuple-element.74), channel_id=1, source_target_pairs={{0,32},{8,40},{16,48},{24,56},{32,0},{40,8},{48,16},{56,24},{64,96... | collective-permute-start | bytes 442376 | tf_op jit(solution)/shard_map/ppermute | solution.py:284
  116.4 8.9 %collective-permute-start.25 = (s16[4,9,16,128]{3,2,1,0:T(8,128)(2,1)S(1)}, s16[4,9,16,128]{3,2,1,0:T(8,128)(2,1)S(1)}, u32[]{:S(2)}, u32[]{:S(2)}) collective-permute-start(s16[4,9,16,128]{3,2,1,0:T(8,128)(2,1)S(1)} %get-tuple-element.75), channel_id=1, source_target_pairs={{0,48},{8,56},{16,0},{24,8},{32,16},{40,24},{48,32},{56,40},{64,11... | collective-permute-start | bytes 442376 | tf_op jit(solution)/shard_map/ppermute | solution.py:284
  (5 other events, 20.5 us)

commit v4 on v3

--- a/solution.py
+++ b/solution.py
@@ -40,45 +40,19 @@
     return jax.ShapeDtypeStruct((*lead, TR, TC), dtype)
 
 
-def stream(ins, work, outs):
-    for c in ins:
+def repack_kernel(n, jcs, levels, unpack, src_ref, dst_ref, sem):
+    rows, packed = (dst_ref, src_ref) if unpack else (src_ref, dst_ref)
+    moves = []
+    for z in range(n):
+        for l in range(levels):
+            for jc in range(jcs):
+                pair = (rows.at[l, z, :, :, pl.ds(jc * TC, TC)], packed.at[:, jc, z, l])
+                src, dst = pair[::-1] if unpack else pair
+                moves.append(copy(src, dst, sem.at[z, l, jc]))
+    for c in moves:
         c.start()
-    for k, c in enumerate(ins):
-        c.wait()
-        work(k)
-        outs[k].start()
-    for c in outs:
-        c.wait()
-
-
-def pack_kernel(n, zr, jrs, jcs, levels, x_ref, out_ref, rows_vm, tiles_vm, in_sem, out_sem):
-    def work(z):
-        for l in range(levels):
-            for jr in range(jrs):
-                for jc in range(jcs):
-                    tile = rows_vm[z, l, jr * TR : (jr + 1) * TR, jc * TC : (jc + 1) * TC]
-                    tiles_vm[z, jr * jcs + jc, l] = tile
-
-    stream(
-        [copy(x_ref.at[0, :, pl.ds(z * zr, zr)], rows_vm.at[z], in_sem.at[z]) for z in range(n)],
-        work,
-        [copy(tiles_vm.at[z], out_ref.at[:, z], out_sem.at[z]) for z in range(n)],
-    )
-
-
-def unpack_kernel(n, zr, jrs, jcs, levels, y_ref, out_ref, rows_vm, tiles_vm, in_sem, out_sem):
-    def work(z):
-        for l in range(levels):
-            for jr in range(jrs):
-                for jc in range(jcs):
-                    tile = tiles_vm[z, jr * jcs + jc, l]
-                    rows_vm[z, l, jr * TR : (jr + 1) * TR, jc * TC : (jc + 1) * TC] = tile
-
-    stream(
-        [copy(y_ref.at[:, z], tiles_vm.at[z], in_sem.at[z]) for z in range(n)],
-        work,
-        [copy(rows_vm.at[z], out_ref.at[0, :, pl.ds(z * zr, zr)], out_sem.at[z]) for z in range(n)],
-    )
+    for c in moves:
+        c.wait()
 
 
 def store_coded(out, n, values):
@@ -316,17 +290,21 @@
         return x.reshape(islands, n, levels, TR, TC)
 
     at = lax.axis_index("island").astype(jnp.int32).reshape(1)
-    in_rows = pltpu.VMEM((n, levels, zr, narrow), jnp.bfloat16)
-    in_tiles = pltpu.VMEM((n, islands, levels, TR, TC), jnp.bfloat16)
-    packed = call(
-        functools.partial(pack_kernel, n, zr, jrs, jcs, levels),
-        tiles(islands, n, levels),
-        [ANY],
-        ANY,
-        (in_rows, in_tiles, DMA((n,)), DMA((n,))),
-        vmem=63,
-        moved=4 << 20,
-    )(pseudo_grad)
+    in_rows = jax.ShapeDtypeStruct((levels, n, jrs, TR, narrow), jnp.bfloat16)
+    in_tiles = tiles(jrs, jcs, n, levels)
+
+    def repack(x, unpack):
+        return call(
+            functools.partial(repack_kernel, n, jcs, levels, unpack),
+            in_rows if unpack else in_tiles,
+            [ANY],
+            ANY,
+            (DMA((n, levels, jcs)),),
+            vmem=63,
+            moved=4 << 20,
+        )(x.reshape((in_tiles if unpack else in_rows).shape))
+
+    packed = repack(pseudo_grad, False).reshape(islands, n, levels, TR, TC)
     grads = swap(packed)
 
     leaving = [tiles(SIDE, n + 1, dtype=jnp.int16)] * SIDE + [tiles(islands // CORES, n + 1, dtype=jnp.int16)]
@@ -390,15 +368,7 @@
         ),
         moved=10 << 20,
     )(at, *exchange(at, mean, other), outer_param, outer_momentum)
-    returned = call(
-        functools.partial(unpack_kernel, n, zr, jrs, jcs, levels),
-        jax.ShapeDtypeStruct(pseudo_grad.shape, jnp.bfloat16),
-        [ANY],
-        ANY,
-        (in_rows, in_tiles, DMA((n,)), DMA((n,))),
-        vmem=63,
-        moved=4 << 20,
-    )(arrived)
+    returned = repack(arrived, True).reshape(pseudo_grad.shape)
     return new_param, new_momentum, returned
 
 

time: 142 us -> 267 us (1.88)
  Pallas kernels: 16.8 us -> 142 us
    pallas_call x2, Pallas kernels: 4.88 us -> 130 us  [repack(): call(functools.partial(repack_kernel, n, jcs, levels, unpack), in_rows if...]
  transfers between devices with their start and end apart: 28 -> 28, of which waited for: 15 -> 15; matrix products, arithmetic and copies ran while one was open for 0% -> 0% of each run, Pallas kernels for 5% -> 3%
where the time goes in v4:
time: 267 us; the launch traced here: 266 us
  Pallas kernels  142 us (53%)
  starting transfers between devices  59.8 us (22%)
  waiting for transfers between devices  58.8 us (22%)
  local copies, waits for them, and re-layouts  5.05 us (2%)
    pallas_call x2, Pallas kernels, repack(): call(functools.partial(repack_kernel, n, jcs, levels, unpack), in_rows if...  130 us
    ppermute x26, waiting for transfers between devices, shift(): return lax.ppermute(v, 'island', pairs)  36.8 us
    ppermute x26, starting transfers between devices, shift(): return lax.ppermute(v, 'island', pairs)  34.9 us
    all_to_all x2, starting transfers between devices, swap(): x = lax.all_to_all(x, ('island', 'shard'), 0, 0, tiled=True)  24.9 us
    all_to_all x2, waiting for transfers between devices, swap(): x = lax.all_to_all(x, ('island', 'shard'), 0, 0, tiled=True)  21.9 us
  transfers between devices with their start and end apart: 28, of which 15 were waited for; matrix products, arithmetic and copies ran while one was open for 0% of the time, Pallas kernels for 3%

profile of v4, /device:TPU:1, one launch (start us, length us, event | category | flops | bytes accessed | tf_op | source)
XLA Modules:
  0.0 266.4 jit_solution(14446959157645551307)
XLA Ops:
  0.6 64.9 %shard_map.81 = bf16[16,2,8,2,16,128]{5,4,3,2,1,0:T(8,128)(2,1)} custom-call(bf16[2,8,16,16,256]{4,3,2,1,0:T(8,128)(2,1)} %bitcast.8), custom_call_target="tpu_custom_call" | custom-call | flops 4194304 | bytes 4194304 | tf_op jit(solution)/shard_map/pallas_call | solution.py:297
  65.6 16.7 %all-to-all-start = ((bf16[256,2,16,128]{3,2,1,0:T(8,128)(2,1)}), bf16[256,2,16,128]{3,2,1,0:T(8,128)(2,1)}, u32[]{:S(2)}, u32[]{:S(2)}) async-start(bf16[256,2,16,128]{3,2,1,0:T(8,128)(2,1)} %bitcast.7), calls=%async_computation | async-start | bytes 4194304 | tf_op jit(solution)/shard_map/all_to_all | solution.py:289
  82.3 1.6 copy-done.2
  84.5 2.3 collective-permute-start.6
  86.8 1.9 collective-permute-start.1
  90.0 1.3 collective-permute-start.7
  91.3 2.5 collective-permute-start.8
  93.7 2.1 collective-permute-done.refs_1_
  96.7 4.7 %collective-permute-done.1.refs_2_ = s16[4,9,16,128]{3,2,1,0:T(8,128)(2,1)S(1)} collective-permute-done((s16[4,9,16,128]{3,2,1,0:T(8,128)(2,1)S(1)}, s16[4,9,16,128]{3,2,1,0:T(8,128)(2,1)S(1)}, u32[]{:S(2)}, u32[]{:S(2)}) %collective-permute-start.1) | collective-permute-done | bytes 147488 | tf_op jit(solution)/shard_map/ppermute | solution.py:258
  102.6 2.6 collective-permute-start.4
  107.0 3.1 %collective-permute-start.11 = (s16[4,9,16,128]{3,2,1,0:T(8,128)(2,1)S(1)}, s16[4,9,16,128]{3,2,1,0:T(8,128)(2,1)S(1)}, u32[]{:S(2)}, u32[]{:S(2)}) collective-permute-start(s16[4,9,16,128]{3,2,1,0:T(8,128)(2,1)S(1)} %get-tuple-element.56), channel_id=1, source_target_pairs={{0,32},{8,40},{16,48},{24,56},{32,0},{40,8},{48,16},{56,24},{64,96... | collective-permute-start | bytes 442376 | tf_op jit(solution)/shard_map/ppermute | solution.py:258
  111.1 2.4 collective-permute-start.12
  114.2 3.6 %collective-permute-done.4.refs_2_ = s16[4,9,16,128]{3,2,1,0:T(8,128)(2,1)S(1)} collective-permute-done((s16[4,9,16,128]{3,2,1,0:T(8,128)(2,1)S(1)}, s16[4,9,16,128]{3,2,1,0:T(8,128)(2,1)S(1)}, u32[]{:S(2)}, u32[]{:S(2)}) %collective-permute-start.4) | collective-permute-done | bytes 147488 | tf_op jit(solution)/shard_map/ppermute | solution.py:258
  117.8 3.2 %collective-permute-done.11.refs_6_ = s16[4,9,16,128]{3,2,1,0:T(8,128)(2,1)S(1)} collective-permute-done((s16[4,9,16,128]{3,2,1,0:T(8,128)(2,1)S(1)}, s16[4,9,16,128]{3,2,1,0:T(8,128)(2,1)S(1)}, u32[]{:S(2)}, u32[]{:S(2)}) %collective-permute-start.11) | collective-permute-done | bytes 147488 | tf_op jit(solution)/shard_map/ppermute | solution.py:258
  122.1 13.0 %all-to-all-done = bf16[256,2,16,128]{3,2,1,0:T(8,128)(2,1)} async-done(((bf16[256,2,16,128]{3,2,1,0:T(8,128)(2,1)}), bf16[256,2,16,128]{3,2,1,0:T(8,128)(2,1)}, u32[]{:S(2)}, u32[]{:S(2)}) %all-to-all-start) | async-done | bytes 2097184 | tf_op jit(solution)/shard_map/all_to_all | solution.py:289
  135.1 4.9 %shard_map.82 = (f32[32,8,16,128]{3,2,1,0:T(8,128)}, bf16[32,8,2,16,128]{4,3,2,1,0:T(8,128)(2,1)}) custom-call(s32[32,2]{1,0:T(8,128)} %copy.9.path_ref, s32[32]{0:T(128)} %owner_ref.3, s16[32,9,16,128]{3,2,1,0:T(8,128)(2,1)} %copy-done.4, bf16[32,8,2,16,128]{4,3,2,1,0:T(8,128)(2,1)} %bitcast.3.x_ref), custom_call_target="tpu_custom_call" | custom-call | flops 8388608 | bytes 8388608 | tf_op jit(solution)/shard_map/pallas_call | solution.py:326
  140.1 8.2 %all-to-all-start.1 = ((bf16[256,2,16,128]{3,2,1,0:T(8,128)(2,1)}), bf16[256,2,16,128]{3,2,1,0:T(8,128)(2,1)}, u32[]{:S(2)}, u32[]{:S(2)}) async-start(bf16[256,2,16,128]{3,2,1,0:T(8,128)(2,1)} %bitcast.9), calls=%async_computation.1 | async-start | bytes 4194304 | tf_op jit(solution)/shard_map/all_to_all | solution.py:289
  148.3 1.7 copy-done.5
  150.1 1.7 shard_map.83
  151.7 2.4 collective-permute-start.19
  154.2 1.8 collective-permute-start.14
  157.2 1.3 collective-permute-start.20
  158.6 2.5 collective-permute-start.21
  161.1 7.5 %collective-permute-done.13.refs_1_ = s16[4,9,16,128]{3,2,1,0:T(8,128)(2,1)S(1)} collective-permute-done((s16[4,9,16,128]{3,2,1,0:T(8,128)(2,1)S(1)}, s16[4,9,16,128]{3,2,1,0:T(8,128)(2,1)S(1)}, u32[]{:S(2)}, u32[]{:S(2)}) %collective-permute-start.13) | collective-permute-done | bytes 147488 | tf_op jit(solution)/shard_map/ppermute | solution.py:258
  170.2 1.5 collective-permute-start.17
  172.8 3.2 %collective-permute-done.22.refs_3_ = s16[4,9,16,128]{3,2,1,0:T(8,128)(2,1)S(1)} collective-permute-done((s16[4,9,16,128]{3,2,1,0:T(8,128)(2,1)S(1)}, s16[4,9,16,128]{3,2,1,0:T(8,128)(2,1)S(1)}, u32[]{:S(2)}, u32[]{:S(2)}) %collective-permute-start.22) | collective-permute-done | bytes 147488 | tf_op jit(solution)/shard_map/ppermute | solution.py:258
  177.0 2.1 collective-permute-done.16.refs_1_
  179.5 5.5 %collective-permute-done.17.refs_2_ = s16[4,9,16,128]{3,2,1,0:T(8,128)(2,1)S(1)} collective-permute-done((s16[4,9,16,128]{3,2,1,0:T(8,128)(2,1)S(1)}, s16[4,9,16,128]{3,2,1,0:T(8,128)(2,1)S(1)}, u32[]{:S(2)}, u32[]{:S(2)}) %collective-permute-start.17) | collective-permute-done | bytes 147488 | tf_op jit(solution)/shard_map/ppermute | solution.py:258
  185.0 1.8 collective-permute-done.18.refs_3_
  188.0 4.3 %shard_map.87 = (f32[1,256,2048]{2,1,0:T(8,128)}, f32[1,256,2048]{2,1,0:T(8,128)}) custom-call(s32[1]{0:T(128)} %bitcast.at_ref, s16[4,9,16,128]{3,2,1,0:T(8,128)(2,1)S(1)} %get-tuple-element.63.refs_0_, s16[4,9,16,128]{3,2,1,0:T(8,128)(2,1)S(1)} %collective-permute-done.16.refs_1_, s16[4,9,16,128]{3,2,1,0:T(8,128)(2,1)S(1)} %collective-permute-done.17.refs_2_, ...), custom_call_target="tpu_custom_call" | custom-call | flops 10485760 | bytes 10485760 | tf_op jit(solution)/shard_map/pallas_call | solution.py:357
  192.3 9.0 %all-to-all-done.1 = bf16[256,2,16,128]{3,2,1,0:T(8,128)(2,1)} async-done(((bf16[256,2,16,128]{3,2,1,0:T(8,128)(2,1)}), bf16[256,2,16,128]{3,2,1,0:T(8,128)(2,1)}, u32[]{:S(2)}, u32[]{:S(2)}) %all-to-all-start.1) | async-done | bytes 2097184 | tf_op jit(solution)/shard_map/all_to_all | solution.py:289
  201.3 64.9 %shard_map.88 = bf16[2,8,16,16,256]{4,3,2,1,0:T(8,128)(2,1)} custom-call(bf16[16,2,8,2,16,128]{5,4,3,2,1,0:T(8,128)(2,1)} %bitcast.5.src_ref), custom_call_target="tpu_custom_call" | custom-call | flops 4194304 | bytes 4194304 | tf_op jit(solution)/shard_map/pallas_call | solution.py:297
  (56 shorter events, 15.2 us)
Async XLA Ops:
  65.6 16.7 %copy-start = (f32[1,256,2048]{2,1,0:T(8,128)S(1)}, f32[1,256,2048]{2,1,0:T(8,128)}, u32[]{:S(2)}) copy-start(f32[1,256,2048]{2,1,0:T(8,128)} %refs_8_.1) | copy-start | bytes 6291460
  65.6 69.5 %all-to-all-start = ((bf16[256,2,16,128]{3,2,1,0:T(8,128)(2,1)}), bf16[256,2,16,128]{3,2,1,0:T(8,128)(2,1)}, u32[]{:S(2)}, u32[]{:S(2)}) async-start(bf16[256,2,16,128]{3,2,1,0:T(8,128)(2,1)} %bitcast.7), calls=%async_computation | async-start | bytes 4194304 | tf_op jit(solution)/shard_map/all_to_all | solution.py:289
  83.8 29.7 %copy-start.8 = (s32[32,2]{0,1:T(2,128)S(1)}, s32[32,2]{0,1:T(2,128)}, u32[]{:S(2)}) copy-start(s32[32,2]{0,1:T(2,128)} %param.6) | copy-start | bytes 772
  84.5 5.4 %collective-permute-start.6 = (s16[16,9,16,128]{3,2,1,0:T(8,128)(2,1)S(1)}, s16[16,9,16,128]{3,2,1,0:T(8,128)(2,1)S(1)}, u32[]{:S(2)}, u32[]{:S(2)}) collective-permute-start(s16[16,9,16,128]{3,2,1,0:T(8,128)(2,1)S(1)} %get-tuple-element.49), channel_id=1, source_target_pairs={{0,8},{8,0},{16,24},{24,16},{32,40},{40,32},{48,56},{56,48},{64,72... | collective-permute-start | bytes 1769480 | tf_op jit(solution)/shard_map/ppermute | solution.py:258
  86.8 9.0 %collective-permute-start = (s16[4,9,16,128]{3,2,1,0:T(8,128)(2,1)S(1)}, s16[4,9,16,128]{3,2,1,0:T(8,128)(2,1)S(1)}, u32[]{:S(2)}, u32[]{:S(2)}) collective-permute-start(s16[4,9,16,128]{3,2,1,0:T(8,128)(2,1)S(1)} %get-tuple-element.42), channel_id=1, source_target_pairs={{0,16},{8,24},{16,32},{24,40},{32,48},{40,56},{48,0},{56,8},{64,80... | collective-permute-start | bytes 442376 | tf_op jit(solution)/shard_map/ppermute | solution.py:258
  86.8 14.5 %collective-permute-start.1 = (s16[4,9,16,128]{3,2,1,0:T(8,128)(2,1)S(1)}, s16[4,9,16,128]{3,2,1,0:T(8,128)(2,1)S(1)}, u32[]{:S(2)}, u32[]{:S(2)}) collective-permute-start(s16[4,9,16,128]{3,2,1,0:T(8,128)(2,1)S(1)} %get-tuple-element.43), channel_id=1, source_target_pairs={{0,32},{8,40},{16,48},{24,56},{32,0},{40,8},{48,16},{56,24},{64,96... | collective-permute-start | bytes 442376 | tf_op jit(solution)/shard_map/ppermute | solution.py:258
  88.8 12.7 %collective-permute-start.2 = (s16[4,9,16,128]{3,2,1,0:T(8,128)(2,1)S(1)}, s16[4,9,16,128]{3,2,1,0:T(8,128)(2,1)S(1)}, u32[]{:S(2)}, u32[]{:S(2)}) collective-permute-start(s16[4,9,16,128]{3,2,1,0:T(8,128)(2,1)S(1)} %get-tuple-element.44), channel_id=1, source_target_pairs={{0,48},{8,56},{16,0},{24,8},{32,16},{40,24},{48,32},{56,40},{64,11... | collective-permute-start | bytes 442376 | tf_op jit(solution)/shard_map/ppermute | solution.py:258
  90.0 15.2 %collective-permute-start.7 = (s16[4,9,16,128]{3,2,1,0:T(8,128)(2,1)S(1)}, s16[4,9,16,128]{3,2,1,0:T(8,128)(2,1)S(1)}, u32[]{:S(2)}, u32[]{:S(2)}) collective-permute-start(s16[4,9,16,128]{3,2,1,0:T(8,128)(2,1)S(1)} %get-tuple-element.51), channel_id=1, source_target_pairs={{0,64},{8,72},{16,80},{24,88},{32,96},{40,104},{48,112},{56,120},{... | collective-permute-start | bytes 442376 | tf_op jit(solution)/shard_map/ppermute | solution.py:258
  91.3 15.1 %collective-permute-start.8 = (s16[4,9,16,128]{3,2,1,0:T(8,128)(2,1)S(1)}, s16[4,9,16,128]{3,2,1,0:T(8,128)(2,1)S(1)}, u32[]{:S(2)}, u32[]{:S(2)}) collective-permute-start(s16[4,9,16,128]{3,2,1,0:T(8,128)(2,1)S(1)} %get-tuple-element.52), channel_id=1, source_target_pairs={{0,128},{8,136},{16,144},{24,152},{32,160},{40,168},{48,176},{56,1... | collective-permute-start | bytes 442376 | tf_op jit(solution)/shard_map/ppermute | solution.py:258
  95.8 10.5 %collective-permute-start.9 = (s16[4,9,16,128]{3,2,1,0:T(8,128)(2,1)S(1)}, s16[4,9,16,128]{3,2,1,0:T(8,128)(2,1)S(1)}, u32[]{:S(2)}, u32[]{:S(2)}) collective-permute-start(s16[4,9,16,128]{3,2,1,0:T(8,128)(2,1)S(1)} %get-tuple-element.53), channel_id=1, source_target_pairs={{0,192},{8,200},{16,208},{24,216},{32,224},{40,232},{48,240},{56,2... | collective-permute-start | bytes 442376 | tf_op jit(solution)/shard_map/ppermute | solution.py:258
  101.5 9.6 %collective-permute-start.3 = (s16[4,9,16,128]{3,2,1,0:T(8,128)(2,1)S(1)}, s16[4,9,16,128]{3,2,1,0:T(8,128)(2,1)S(1)}, u32[]{:S(2)}, u32[]{:S(2)}) collective-permute-start(s16[4,9,16,128]{3,2,1,0:T(8,128)(2,1)S(1)} %get-tuple-element.46), channel_id=1, source_target_pairs={{0,64},{8,72},{16,80},{24,88},{32,96},{40,104},{48,112},{56,120},{... | collective-permute-start | bytes 442376 | tf_op jit(solution)/shard_map/ppermute | solution.py:258
  102.6 15.2 %collective-permute-start.4 = (s16[4,9,16,128]{3,2,1,0:T(8,128)(2,1)S(1)}, s16[4,9,16,128]{3,2,1,0:T(8,128)(2,1)S(1)}, u32[]{:S(2)}, u32[]{:S(2)}) collective-permute-start(s16[4,9,16,128]{3,2,1,0:T(8,128)(2,1)S(1)} %get-tuple-element.47), channel_id=1, source_target_pairs={{0,128},{8,136},{16,144},{24,152},{32,160},{40,168},{48,176},{56,1... | collective-permute-start | bytes 442376 | tf_op jit(solution)/shard_map/ppermute | solution.py:258
  105.2 12.6 %collective-permute-start.5 = (s16[4,9,16,128]{3,2,1,0:T(8,128)(2,1)S(1)}, s16[4,9,16,128]{3,2,1,0:T(8,128)(2,1)S(1)}, u32[]{:S(2)}, u32[]{:S(2)}) collective-permute-start(s16[4,9,16,128]{3,2,1,0:T(8,128)(2,1)S(1)} %get-tuple-element.48), channel_id=1, source_target_pairs={{0,192},{8,200},{16,208},{24,216},{32,224},{40,232},{48,240},{56,2... | collective-permute-start | bytes 442376 | tf_op jit(solution)/shard_map/ppermute | solution.py:258
  106.4 11.4 %collective-permute-start.10 = (s16[4,9,16,128]{3,2,1,0:T(8,128)(2,1)S(1)}, s16[4,9,16,128]{3,2,1,0:T(8,128)(2,1)S(1)}, u32[]{:S(2)}, u32[]{:S(2)}) collective-permute-start(s16[4,9,16,128]{3,2,1,0:T(8,128)(2,1)S(1)} %get-tuple-element.55), channel_id=1, source_target_pairs={{0,16},{8,24},{16,32},{24,40},{32,48},{40,56},{48,0},{56,8},{64,80... | collective-permute-start | bytes 442376 | tf_op jit(solution)/shard_map/ppermute | solution.py:258
  107.0 14.1 %collective-permute-start.11 = (s16[4,9,16,128]{3,2,1,0:T(8,128)(2,1)S(1)}, s16[4,9,16,128]{3,2,1,0:T(8,128)(2,1)S(1)}, u32[]{:S(2)}, u32[]{:S(2)}) collective-permute-start(s16[4,9,16,128]{3,2,1,0:T(8,128)(2,1)S(1)} %get-tuple-element.56), channel_id=1, source_target_pairs={{0,32},{8,40},{16,48},{24,56},{32,0},{40,8},{48,16},{56,24},{64,96... | collective-permute-start | bytes 442376 | tf_op jit(solution)/shard_map/ppermute | solution.py:258
  111.1 9.9 %collective-permute-start.12 = (s16[4,9,16,128]{3,2,1,0:T(8,128)(2,1)S(1)}, s16[4,9,16,128]{3,2,1,0:T(8,128)(2,1)S(1)}, u32[]{:S(2)}, u32[]{:S(2)}) collective-permute-start(s16[4,9,16,128]{3,2,1,0:T(8,128)(2,1)S(1)} %get-tuple-element.57), channel_id=1, source_target_pairs={{0,48},{8,56},{16,0},{24,8},{32,16},{40,24},{48,32},{56,40},{64,11... | collective-permute-start | bytes 442376 | tf_op jit(solution)/shard_map/ppermute | solution.py:258
  140.0 47.9 %copy-start.3 = (f32[1,256,2048]{2,1,0:T(8,128)S(1)}, f32[1,256,2048]{2,1,0:T(8,128)}, u32[]{:S(2)}) copy-start(f32[1,256,2048]{2,1,0:T(8,128)} %refs_9_.1) | copy-start | bytes 6291460
  140.1 61.2 %all-to-all-start.1 = ((bf16[256,2,16,128]{3,2,1,0:T(8,128)(2,1)}), bf16[256,2,16,128]{3,2,1,0:T(8,128)(2,1)}, u32[]{:S(2)}, u32[]{:S(2)}) async-start(bf16[256,2,16,128]{3,2,1,0:T(8,128)(2,1)} %bitcast.9), calls=%async_computation.1 | async-start | bytes 4194304 | tf_op jit(solution)/shard_map/all_to_all | solution.py:289
  148.3 39.7 %copy-start.1 = (f32[1,256,2048]{2,1,0:T(8,128)S(1)}, f32[1,256,2048]{2,1,0:T(8,128)}, u32[]{:S(2)}) copy-start(f32[1,256,2048]{2,1,0:T(8,128)} %refs_8_.1) | copy-start | bytes 6291460
  151.7 5.4 %collective-permute-start.19 = (s16[16,9,16,128]{3,2,1,0:T(8,128)(2,1)S(1)}, s16[16,9,16,128]{3,2,1,0:T(8,128)(2,1)S(1)}, u32[]{:S(2)}, u32[]{:S(2)}) collective-permute-start(s16[16,9,16,128]{3,2,1,0:T(8,128)(2,1)S(1)} %get-tuple-element.67), channel_id=1, source_target_pairs={{0,8},{8,0},{16,24},{24,16},{32,40},{40,32},{48,56},{56,48},{64,72... | collective-permute-start | bytes 1769480 | tf_op jit(solution)/shard_map/ppermute | solution.py:258
  154.2 14.4 %collective-permute-start.13 = (s16[4,9,16,128]{3,2,1,0:T(8,128)(2,1)S(1)}, s16[4,9,16,128]{3,2,1,0:T(8,128)(2,1)S(1)}, u32[]{:S(2)}, u32[]{:S(2)}) collective-permute-start(s16[4,9,16,128]{3,2,1,0:T(8,128)(2,1)S(1)} %get-tuple-element.60), channel_id=1, source_target_pairs={{0,16},{8,24},{16,32},{24,40},{32,48},{40,56},{48,0},{56,8},{64,80... | collective-permute-start | bytes 442376 | tf_op jit(solution)/shard_map/ppermute | solution.py:258
  154.2 14.4 %collective-permute-start.14 = (s16[4,9,16,128]{3,2,1,0:T(8,128)(2,1)S(1)}, s16[4,9,16,128]{3,2,1,0:T(8,128)(2,1)S(1)}, u32[]{:S(2)}, u32[]{:S(2)}) collective-permute-start(s16[4,9,16,128]{3,2,1,0:T(8,128)(2,1)S(1)} %get-tuple-element.61), channel_id=1, source_target_pairs={{0,32},{8,40},{16,48},{24,56},{32,0},{40,8},{48,16},{56,24},{64,96... | collective-permute-start | bytes 442376 | tf_op jit(solution)/shard_map/ppermute | solution.py:258
  156.0 13.4 %collective-permute-start.15 = (s16[4,9,16,128]{3,2,1,0:T(8,128)(2,1)S(1)}, s16[4,9,16,128]{3,2,1,0:T(8,128)(2,1)S(1)}, u32[]{:S(2)}, u32[]{:S(2)}) collective-permute-start(s16[4,9,16,128]{3,2,1,0:T(8,128)(2,1)S(1)} %get-tuple-element.62), channel_id=1, source_target_pairs={{0,48},{8,56},{16,0},{24,8},{32,16},{40,24},{48,32},{56,40},{64,11... | collective-permute-start | bytes 442376 | tf_op jit(solution)/shard_map/ppermute | solution.py:258
  157.2 14.4 %collective-permute-start.20 = (s16[4,9,16,128]{3,2,1,0:T(8,128)(2,1)S(1)}, s16[4,9,16,128]{3,2,1,0:T(8,128)(2,1)S(1)}, u32[]{:S(2)}, u32[]{:S(2)}) collective-permute-start(s16[4,9,16,128]{3,2,1,0:T(8,128)(2,1)S(1)} %get-tuple-element.69), channel_id=1, source_target_pairs={{0,64},{8,72},{16,80},{24,88},{32,96},{40,104},{48,112},{56,120},{... | collective-permute-start | bytes 442376 | tf_op jit(solution)/shard_map/ppermute | solution.py:258
  158.6 14.2 %collective-permute-start.21 = (s16[4,9,16,128]{3,2,1,0:T(8,128)(2,1)S(1)}, s16[4,9,16,128]{3,2,1,0:T(8,128)(2,1)S(1)}, u32[]{:S(2)}, u32[]{:S(2)}) collective-permute-start(s16[4,9,16,128]{3,2,1,0:T(8,128)(2,1)S(1)} %get-tuple-element.70), channel_id=1, source_target_pairs={{0,128},{8,136},{16,144},{24,152},{32,160},{40,168},{48,176},{56,1... | collective-permute-start | bytes 442376 | tf_op jit(solution)/shard_map/ppermute | solution.py:258
  168.6 7.3 %collective-permute-start.22 = (s16[4,9,16,128]{3,2,1,0:T(8,128)(2,1)S(1)}, s16[4,9,16,128]{3,2,1,0:T(8,128)(2,1)S(1)}, u32[]{:S(2)}, u32[]{:S(2)}) collective-permute-start(s16[4,9,16,128]{3,2,1,0:T(8,128)(2,1)S(1)} %get-tuple-element.71), channel_id=1, source_target_pairs={{0,192},{8,200},{16,208},{24,216},{32,224},{40,232},{48,240},{56,2... | collective-permute-start | bytes 442376 | tf_op jit(solution)/shard_map/ppermute | solution.py:258
  169.5 9.6 %collective-permute-start.16 = (s16[4,9,16,128]{3,2,1,0:T(8,128)(2,1)S(1)}, s16[4,9,16,128]{3,2,1,0:T(8,128)(2,1)S(1)}, u32[]{:S(2)}, u32[]{:S(2)}) collective-permute-start(s16[4,9,16,128]{3,2,1,0:T(8,128)(2,1)S(1)} %get-tuple-element.64), channel_id=1, source_target_pairs={{0,64},{8,72},{16,80},{24,88},{32,96},{40,104},{48,112},{56,120},{... | collective-permute-start | bytes 442376 | tf_op jit(solution)/shard_map/ppermute | solution.py:258
  170.2 14.9 %collective-permute-start.17 = (s16[4,9,16,128]{3,2,1,0:T(8,128)(2,1)S(1)}, s16[4,9,16,128]{3,2,1,0:T(8,128)(2,1)S(1)}, u32[]{:S(2)}, u32[]{:S(2)}) collective-permute-start(s16[4,9,16,128]{3,2,1,0:T(8,128)(2,1)S(1)} %get-tuple-element.65), channel_id=1, source_target_pairs={{0,128},{8,136},{16,144},{24,152},{32,160},{40,168},{48,176},{56,1... | collective-permute-start | bytes 442376 | tf_op jit(solution)/shard_map/ppermute | solution.py:258
  171.6 15.2 %collective-permute-start.18 = (s16[4,9,16,128]{3,2,1,0:T(8,128)(2,1)S(1)}, s16[4,9,16,128]{3,2,1,0:T(8,128)(2,1)S(1)}, u32[]{:S(2)}, u32[]{:S(2)}) collective-permute-start(s16[4,9,16,128]{3,2,1,0:T(8,128)(2,1)S(1)} %get-tuple-element.66), channel_id=1, source_target_pairs={{0,192},{8,200},{16,208},{24,216},{32,224},{40,232},{48,240},{56,2... | collective-permute-start | bytes 442376 | tf_op jit(solution)/shard_map/ppermute | solution.py:258
  176.0 10.9 %collective-permute-start.23 = (s16[4,9,16,128]{3,2,1,0:T(8,128)(2,1)S(1)}, s16[4,9,16,128]{3,2,1,0:T(8,128)(2,1)S(1)}, u32[]{:S(2)}, u32[]{:S(2)}) collective-permute-start(s16[4,9,16,128]{3,2,1,0:T(8,128)(2,1)S(1)} %get-tuple-element.73), channel_id=1, source_target_pairs={{0,16},{8,24},{16,32},{24,40},{32,48},{40,56},{48,0},{56,8},{64,80... | collective-permute-start | bytes 442376 | tf_op jit(solution)/shard_map/ppermute | solution.py:258
  176.1 11.9 %collective-permute-start.24 = (s16[4,9,16,128]{3,2,1,0:T(8,128)(2,1)S(1)}, s16[4,9,16,128]{3,2,1,0:T(8,128)(2,1)S(1)}, u32[]{:S(2)}, u32[]{:S(2)}) collective-permute-start(s16[4,9,16,128]{3,2,1,0:T(8,128)(2,1)S(1)} %get-tuple-element.74), channel_id=1, source_target_pairs={{0,32},{8,40},{16,48},{24,56},{32,0},{40,8},{48,16},{56,24},{64,96... | collective-permute-start | bytes 442376 | tf_op jit(solution)/shard_map/ppermute | solution.py:258
  179.1 8.9 %collective-permute-start.25 = (s16[4,9,16,128]{3,2,1,0:T(8,128)(2,1)S(1)}, s16[4,9,16,128]{3,2,1,0:T(8,128)(2,1)S(1)}, u32[]{:S(2)}, u32[]{:S(2)}) collective-permute-start(s16[4,9,16,128]{3,2,1,0:T(8,128)(2,1)S(1)} %get-tuple-element.75), channel_id=1, source_target_pairs={{0,48},{8,56},{16,0},{24,8},{32,16},{40,24},{48,32},{56,40},{64,11... | collective-permute-start | bytes 442376 | tf_op jit(solution)/shard_map/ppermute | solution.py:258
  (5 other events, 20.9 us)
